TPU v7x, 32 devices: a whole 2x2x4 slice. The times are simulated.
32 devices in a mesh: replica: 2 (over x), fsdp: 16 (over z, y, core).
Axes of the slice: x: 2, y: 2, z: 4, core: 2. Of those that a mesh axis runs over, the one named last changes fastest.
Arguments:
- tokens: bfloat16 [8192, 2048], P(('replica', 'fsdp')), may hold values from -88 to 88
- doc_ids: int32 [32, 256], P(('replica', 'fsdp')), may hold values from 0 to 31, never falling along the last dimension, each value on 1 to 128 neighbouring positions
- norm_gain: bfloat16 [2048], P('fsdp'), may hold values from 0.5 to 1.5
- in_weight: bfloat16 [2048, 8192], P('fsdp'), may hold values from -0.125 to 0.125
- conv_taps: bfloat16 [4096, 4], P('fsdp'), may hold values from -3 to 3
- conv_offset: bfloat16 [4096], P('fsdp'), may hold values from -0.5 to 0.5
- select_weight: bfloat16 [4096, 160], P('fsdp'), may hold values from -0.09375 to 0.09375
- step_weight: bfloat16 [4096, 128], P('fsdp'), may hold values from -0.5 to 0.5
- step_bias: bfloat16 [4096], P('fsdp'), may hold values from -7 to -2
- decay_log: bfloat16 [4096, 16], P('fsdp'), may hold values from -3 to 2
- skip_gain: bfloat16 [4096], P('fsdp'), may hold values from 0.5 to 1.5
- out_weight: bfloat16 [4096, 2048], P('fsdp'), may hold values from -0.375 to 0.375
- cotangent: bfloat16 [8192, 2048], P(('replica', 'fsdp')), may hold values from -6 to 6
Outputs:
- layer_out: bfloat16 [8192, 2048], P(('replica', 'fsdp'))
- tokens_grad: bfloat16 [8192, 2048], P(('replica', 'fsdp'))
- grad_norm_gain: float32 [2048], P('fsdp')
- grad_in_weight: float32 [2048, 8192], P('fsdp')
- grad_conv_taps: float32 [4096, 4], P('fsdp')
- grad_conv_offset: float32 [4096], P('fsdp')
- grad_select_weight: float32 [4096, 160], P('fsdp')
- grad_step_weight: float32 [4096, 128], P('fsdp')
- grad_step_bias: float32 [4096], P('fsdp')
- grad_decay_log: float32 [4096, 16], P('fsdp')
- grad_skip_gain: float32 [4096], P('fsdp')
- grad_out_weight: float32 [4096, 2048], P('fsdp')
Inputs may be any that keep to these rules, and one draw needn't show every extreme that they name: `doc_ids`: within each row of 256 tokens the ids never fall; tokens with one id in a row form one document.
All inputs are finite; a program needn't handle non-finite values.
Results may differ from a plain program's by a relative error of at most 0.014.
Values may be sent and summed in bfloat16 or wider, within the bound.
A program may use at most 384 MiB of HBM per device.

v0:
```python
from functools import partial
import math

import jax
import jax.numpy as jnp
from jax import lax
from jax.sharding import PartitionSpec as P

epsilon = 1e-05


def causal_conv(values, weights, offsets, doc_ids):
    length = values.shape[1]
    kernel_len = weights.shape[1]
    padded = jnp.pad(values, ((0, 0), (kernel_len - 1, 0), (0, 0)))
    padded_ids = jnp.pad(doc_ids, ((0, 0), (kernel_len - 1, 0)), constant_values=-1)
    result = offsets + jnp.zeros_like(values)
    for back_step in range(kernel_len):
        first_row = kernel_len - 1 - back_step
        shifted = padded[:, first_row : first_row + length]
        same_doc = (padded_ids[:, first_row : first_row + length] == doc_ids).astype(values.dtype)
        result = result + shifted * same_doc[:, :, None] * weights[:, kernel_len - 1 - back_step]
    return result


def scan_block(hidden_state, pieces, decay_rates):
    inputs, steps_in, in_gate, out_gate, keep_mask = pieces
    outputs = []
    for position in range(inputs.shape[0]):
        decay_now = (
            jnp.exp(steps_in[position][:, None, :] * decay_rates[None])
            * keep_mask[position][:, None, None]
        )
        hidden_state = (
            decay_now * hidden_state
            + (steps_in[position] * inputs[position])[:, None, :] * in_gate[position][:, :, None]
        )
        outputs.append(jnp.sum(hidden_state * out_gate[position][:, :, None], axis=1))
    return (hidden_state, jnp.stack(outputs))


def time_major(member, blocks, block_len):
    return member.swapaxes(0, 1).reshape((blocks, block_len, member.shape[0]) + member.shape[2:])


def selective_scan(inputs, steps_in, in_gate, out_gate, keep_mask, decay_rates):
    length = inputs.shape[1]
    block_len = math.gcd(length, 16)
    blocks = length // block_len
    pieces = tuple(
        (
            time_major(member, blocks, block_len)
            for member in (inputs, steps_in, in_gate, out_gate, keep_mask)
        )
    )
    initial = jnp.zeros((inputs.shape[0], decay_rates.shape[0], inputs.shape[2]), inputs.dtype)
    runner = jax.checkpoint(partial(scan_block, decay_rates=decay_rates))
    final_state, outputs = lax.scan(runner, initial, pieces)
    return outputs.reshape((length,) + outputs.shape[2:]).swapaxes(0, 1)


def contract_rows(left, right):
    return lax.dot_general(
        left, right, (((0,), (0,)), ((), ())), preferred_element_type=jnp.float32
    )


def contract_cols(left, right):
    return lax.dot_general(
        left, right, (((1,), (1,)), ((), ())), preferred_element_type=jnp.float32
    )


def shards(
    tokens,
    doc_ids,
    norm_gain,
    in_weight,
    conv_taps,
    conv_offset,
    select_weight,
    step_weight,
    step_bias,
    decay_log,
    skip_gain,
    out_weight,
    cotangent,
):
    gathered = (
        lax.all_gather(norm_gain, "fsdp", axis=0, tiled=True),
        lax.all_gather(in_weight, "fsdp", axis=0, tiled=True),
        lax.all_gather(conv_taps, "fsdp", axis=0, tiled=True),
        lax.all_gather(conv_offset, "fsdp", axis=0, tiled=True),
        lax.all_gather(select_weight, "fsdp", axis=0, tiled=True),
        lax.all_gather(step_weight, "fsdp", axis=0, tiled=True),
        lax.all_gather(step_bias, "fsdp", axis=0, tiled=True),
        lax.all_gather(decay_log, "fsdp", axis=0, tiled=True),
        lax.all_gather(skip_gain, "fsdp", axis=0, tiled=True),
        lax.all_gather(out_weight, "fsdp", axis=0, tiled=True),
    )
    (
        all_gain,
        all_in,
        all_taps,
        all_offset,
        all_select,
        all_step,
        all_bias,
        all_decay,
        all_skip,
        all_out,
    ) = gathered
    inner_width = all_step.shape[0]
    rank_width = all_step.shape[1]
    state_size = all_decay.shape[1]
    residual = tokens.astype(jnp.float32)

    def norm_piece(values, scale_gain):
        mean_square = jnp.mean(values * values, axis=-1, keepdims=True)
        return values * lax.rsqrt(mean_square + epsilon) * scale_gain

    normed, norm_pull = jax.vjp(norm_piece, residual, all_gain.astype(jnp.float32))
    normed_low = normed.astype(jnp.bfloat16)
    projected = jnp.dot(normed_low, all_in, preferred_element_type=jnp.float32)
    conv_in = projected[:, :inner_width]
    gate_in = projected[:, inner_width:]

    def conv_piece(values, kernel, offsets):
        return jax.nn.silu(causal_conv(values[None], kernel, offsets, doc_ids)[0])

    selected, conv_pull = jax.vjp(
        conv_piece, conv_in, all_taps.astype(jnp.float32), all_offset.astype(jnp.float32)
    )
    selected_low = selected.astype(jnp.bfloat16)
    selection = jnp.dot(selected_low, all_select, preferred_element_type=jnp.float32)
    rank_low = selection[:, :rank_width].astype(jnp.bfloat16)
    pre_step = contract_cols(rank_low, all_step)

    def step_piece(values, offsets):
        return jax.nn.softplus(values + offsets)

    steps_in, step_pull = jax.vjp(step_piece, pre_step, all_bias.astype(jnp.float32))
    same_prev = (doc_ids[:, 1:] == doc_ids[:, :-1]).astype(jnp.int32)
    keep_mask = jnp.concatenate([jnp.zeros_like(doc_ids[:, :1]), same_prev], axis=1).astype(
        jnp.float32
    )

    def mix_piece(values, step_values, in_gate, out_gate, rates_log, skip_scale, gate_values):
        scanned = (
            selective_scan(
                values[None],
                step_values[None],
                in_gate[None],
                out_gate[None],
                keep_mask,
                -jnp.exp(rates_log).T,
            )[0]
            + skip_scale * values
        )
        return scanned * jax.nn.silu(gate_values)

    gated, mix_pull = jax.vjp(
        mix_piece,
        selected_low.astype(jnp.float32),
        steps_in,
        selection[:, rank_width : rank_width + state_size],
        selection[:, rank_width + state_size :],
        all_decay.astype(jnp.float32),
        all_skip.astype(jnp.float32),
        gate_in,
    )
    gated_low = gated.astype(jnp.bfloat16)
    layer_out = (residual + jnp.dot(gated_low, all_out, preferred_element_type=jnp.float32)).astype(
        jnp.bfloat16
    )
    all_out, all_step, all_select, all_in = (
        lax.all_gather(out_weight, "fsdp", axis=0, tiled=True),
        lax.all_gather(step_weight, "fsdp", axis=0, tiled=True),
        lax.all_gather(select_weight, "fsdp", axis=0, tiled=True),
        lax.all_gather(in_weight, "fsdp", axis=0, tiled=True),
    )
    grad_out = contract_rows(gated_low, cotangent)
    back_gated = contract_cols(cotangent, all_out).astype(jnp.bfloat16).astype(jnp.float32)
    back_values, back_steps, back_in_gate, back_out_gate, grad_decay, grad_skip, back_gate_in = (
        mix_pull(back_gated)
    )
    back_pre, grad_bias = step_pull(back_steps)
    back_pre_low = back_pre.astype(jnp.bfloat16)
    grad_step = contract_rows(back_pre_low, rank_low)
    back_rank = jnp.dot(back_pre_low, all_step, preferred_element_type=jnp.float32)
    back_selection = jnp.concatenate([back_rank, back_in_gate, back_out_gate], axis=1).astype(
        jnp.bfloat16
    )
    grad_select = contract_rows(selected_low, back_selection)
    back_selected = contract_cols(back_selection, all_select) + back_values
    back_conv_in, grad_taps, grad_offset = conv_pull(back_selected)
    back_projected = jnp.concatenate([back_conv_in, back_gate_in], axis=1).astype(jnp.bfloat16)
    grad_in = contract_rows(normed_low, back_projected)
    back_normed = contract_cols(back_projected, all_in)
    back_residual, grad_gain = norm_pull(back_normed)
    tokens_grad = (cotangent.astype(jnp.float32) + back_residual).astype(jnp.bfloat16)
    (
        share_gain,
        share_in,
        share_taps,
        share_offset,
        share_select,
        share_step,
        share_bias,
        share_decay,
        share_skip,
        share_out,
    ) = (
        lax.psum_scatter(grad_gain, "fsdp", scatter_dimension=0, tiled=True),
        lax.psum_scatter(grad_in, "fsdp", scatter_dimension=0, tiled=True),
        lax.psum_scatter(grad_taps, "fsdp", scatter_dimension=0, tiled=True),
        lax.psum_scatter(grad_offset, "fsdp", scatter_dimension=0, tiled=True),
        lax.psum_scatter(grad_select, "fsdp", scatter_dimension=0, tiled=True),
        lax.psum_scatter(grad_step, "fsdp", scatter_dimension=0, tiled=True),
        lax.psum_scatter(grad_bias, "fsdp", scatter_dimension=0, tiled=True),
        lax.psum_scatter(grad_decay, "fsdp", scatter_dimension=0, tiled=True),
        lax.psum_scatter(grad_skip, "fsdp", scatter_dimension=0, tiled=True),
        lax.psum_scatter(grad_out, "fsdp", scatter_dimension=0, tiled=True),
    )
    (
        share_gain,
        share_in,
        share_taps,
        share_offset,
        share_select,
        share_step,
        share_bias,
        share_decay,
        share_skip,
        share_out,
    ) = lax.psum(
        (
            share_gain,
            share_in,
            share_taps,
            share_offset,
            share_select,
            share_step,
            share_bias,
            share_decay,
            share_skip,
            share_out,
        ),
        "replica",
    )
    return (
        layer_out,
        tokens_grad,
        share_gain,
        share_in,
        share_taps,
        share_offset,
        share_select,
        share_step,
        share_bias,
        share_decay,
        share_skip,
        share_out,
    )


def solution(mesh):
    return jax.shard_map(
        shards,
        mesh=mesh,
        in_specs=(
            P(("replica", "fsdp"), None),
            P(("replica", "fsdp"), None),
            P("fsdp"),
            P("fsdp", None),
            P("fsdp", None),
            P("fsdp"),
            P("fsdp", None),
            P("fsdp", None),
            P("fsdp"),
            P("fsdp", None),
            P("fsdp"),
            P("fsdp", None),
            P(("replica", "fsdp"), None),
        ),
        out_specs=(
            P(("replica", "fsdp"), None),
            P(("replica", "fsdp"), None),
            P("fsdp"),
            P("fsdp", None),
            P("fsdp", None),
            P("fsdp"),
            P("fsdp", None),
            P("fsdp", None),
            P("fsdp"),
            P("fsdp", None),
            P("fsdp"),
            P("fsdp", None),
        ),
        check_vma=False,
    )
```

profile of v0, /device:TPU:11, one launch (start us, length us, event | category | flops | bytes accessed | tf_op | source)
XLA Modules:
  0.0 3528.7 jit_solution(14046620343621993803)
XLA Ops:
  11.9 19.4 all-gather.1
  33.5 17.5 all_gather.37
  51.1 19.0 all-gather
  70.2 17.5 all-gather.2
  87.7 19.8 all_gather.41
  108.3 71.9 %all-gather.9.cloned.1.call-done = bf16[2048,8192]{1,0:T(8,128)(2,1)} async-done(((bf16[128,8192]{1,0:T(8,128)(2,1)}), bf16[2048,8192]{1,0:T(8,128)(2,1)}) %all-gather.9.cloned.1.call-update) | async-done | bytes 33554448 | tf_op jit(solution)/shard_map/all_gather | solution.py:91
  180.2 17.1 fusion.87
  202.0 106.5 %all-gather.15.cloned.1.call-done = bf16[4096,2048]{1,0:T(8,128)(2,1)} async-done(((bf16[256,2048]{1,0:T(8,128)(2,1)}), bf16[4096,2048]{1,0:T(8,128)(2,1)}) %all-gather.15.cloned.1.call-update) | async-done | bytes 16777232 | tf_op jit(solution)/shard_map/all_gather | solution.py:99
  308.5 21.1 fusion.51
  329.6 18.6 all-gather.11.cloned.1.call-done
  351.0 35.7 %all-gather.13.cloned.1.call-done = bf16[4096,128]{1,0:T(8,128)(2,1)} async-done(((bf16[256,128]{1,0:T(8,128)(2,1)}), bf16[4096,128]{1,0:T(8,128)(2,1)}) %all-gather.13.cloned.1.call-update) | async-done | bytes 1048592 | tf_op jit(solution)/shard_map/all_gather | solution.py:95
  416.1 640.0 %while.41 = (s32[]{:T(128)}, f32[1,16,4096]{2,1,0:T(8,128)S(1)}, f32[16,16,1,4096]{3,1,2,0:T(8,128)}, f32[16,1,16,4096]{3,2,1,0:T(8,128)}, f32[16,16,1,4096]{3,2...) while((s32[]{:T(128)}, f32[1,16,4096]{2,1,0:T(8,128)S(1)}, ...), condition=%wide.region_18.19_spmd.clone, body=%wide.region_1.18_spmd.clone.sunk | while | flops 11141138 | bytes 9285513 | solution.py:58
  590.7 12.3 multiply_reduce_fusion.74
  1061.0 1054.5 %while.42 = (s32[]{:T(128)}, f32[16,4096]{1,0:T(8,128)S(1)}, f32[1,16,4096]{2,1,0:T(8,128)S(1)}, f32[16,16,1,4096]{3,1,2,0:T(8,128)}, f32[16,16,1,4096]{3,1,2,0:...) while((s32[]{:T(128)}, f32[16,4096]{1,0:T(8,128)S(1)}, ...), condition=%wide.region_84.85_spmd.clone, body=%wide.region_19.84_spmd.clone.sunk | while | flops 44899332 | bytes 29712532 | solution.py:58
  2124.2 17.6 all-gather.3
  2178.4 13.1 fusion.124
  2201.5 25.6 fusion.71
  2232.4 17.8 reduce-scatter.11.cloned.1.call-done
  2250.2 336.8 %reduce-scatter.17.cloned.1.call-done = f32[256,2048]{1,0:T(8,128)} async-done(((f32[4096,2048]{1,0:T(8,128)}), f32[256,2048]{1,0:T(8,128)}) %reduce-scatter.17.cloned.1.call-update) | async-done | bytes 2097168 | tf_op jit(solution)/shard_map/reduce_scatter | solution.py:223
  2587.1 640.2 %reduce-scatter.9.cloned.1.call-done = f32[128,8192]{1,0:T(8,128)} async-done(((f32[2048,8192]{1,0:T(8,128)}), f32[128,8192]{1,0:T(8,128)}) %reduce-scatter.9.cloned.1.call-update) | async-done | bytes 4194320 | tf_op jit(solution)/shard_map/reduce_scatter | solution.py:215
  3229.2 16.2 fusion.77
  3245.4 50.3 %all-reduce.94 = (f32[2048]{0:T(1024)S(1)}, f32[4096]{0:T(1024)S(1)}, f32[4096]{0:T(1024)S(1)}, f32[4096]{0:T(1024)S(1)}) all-reduce(f32[2048]{0:T(1024)S(1)} %get-tuple-element.670, f32[4096]{0:T(1024)S(1)} %copy-done.24, f32[4096]{0:T(1024)S(1)} %copy-done.33, ...), channel_id=2, replica_groups=mesh['replica'=2,'fsdp'=16] {'fsdp'}, use_global_device_ids=true, to_apply=%region_87.88.clone | all-reduce | flops 14336 | bytes 114688
  3309.9 40.8 %reduce-scatter.15.cloned.1.call-done = f32[256,16]{0,1:T(8,128)} async-done(((f32[4096,16]{0,1:T(8,128)}), f32[256,16]{0,1:T(8,128)}) %reduce-scatter.15.cloned.1.call-update) | async-done | bytes 16400 | tf_op jit(solution)/shard_map/reduce_scatter | solution.py:221
  3357.2 157.1 %all-reduce.99.cloned.1.call-done = (f32[128,8192]{1,0:T(8,128)}, f32[256,160]{0,1:T(8,128)}, f32[256,128]{1,0:T(8,128)}, f32[256,2048]{1,0:T(8,128)}) async-done(((f32[128,8192]{1,0:T(8,128)}, f32[256,160]{0,1:T(8,128)}, f32[256,128]{1,0:T(8,128)}, f32[256,2048]{1,0:T(8,128)}), (f32[128,8192]{1,0:T(8,128)}, f32[256,160]{0,1:T(8,128)}, f32[256,128]{1,0:T(8,128)}, ...) | async-done | bytes 6586384 | tf_op jit(solution)/shard_map/psum | solution.py:236
  (2108 shorter events, 1806.6 us)
Async XLA Ops:
  7.2 173.0 %copy-start.6 = (bf16[256,2048]{1,0:T(8,128)(2,1)S(1)}, bf16[256,2048]{1,0:T(8,128)(2,1)}, u32[]{:S(2)}) copy-start(bf16[256,2048]{1,0:T(8,128)(2,1)} %param.17) | copy-start | bytes 3145732
  7.2 80.4 %copy-start.39 = (bf16[256,16]{0,1:T(8,128)(2,1)S(1)}, bf16[256,16]{0,1:T(8,128)(2,1)}, u32[]{:S(2)}) copy-start(bf16[256,16]{0,1:T(8,128)(2,1)} %param.26) | copy-start | bytes 24580
  7.2 173.0 %all-gather.9.cloned.1.call-start = ((), (), s32[]{:S(2)}) async-start(), calls=%async_computation.6 | async-start | bytes 35651584 | tf_op jit(solution)/shard_map/all_gather | solution.py:91
  8.0 300.5 %all-gather.15.cloned.1.call-start = ((), (), s32[]{:S(2)}) async-start(), calls=%async_computation.9 | async-start | bytes 17825792 | tf_op jit(solution)/shard_map/all_gather | solution.py:99
  8.7 339.5 %all-gather.11.cloned.1.call-start = ((), (), s32[]{:S(2)}) async-start(), calls=%async_computation.7 | async-start | bytes 1392640 | tf_op jit(solution)/shard_map/all_gather | solution.py:94
  9.4 377.3 %all-gather.13.cloned.1.call-start = ((), (), s32[]{:S(2)}) async-start(), calls=%async_computation.8 | async-start | bytes 1114112 | tf_op jit(solution)/shard_map/all_gather | solution.py:95
  10.0 2222.3 %reduce-scatter.13.cloned.1.call-start = ((), (), s32[]{:S(2)}) async-start(), calls=%async_computation.12 | async-start | bytes 2228224 | tf_op jit(solution)/shard_map/reduce_scatter | solution.py:219
  11.0 297.5 %copy-start.40 = (f32[1,256]{1,0:T(1,128)}, f32[1,256]{1,0:T(1,128)S(1)}, u32[]{:S(2)}) copy-start(f32[1,256]{1,0:T(1,128)S(1)} %get-tuple-element.1024) | copy-start | bytes 3076
  11.0 297.5 %copy-start.43 = (f32[1,256]{1,0:T(1,128)}, f32[1,256]{1,0:T(1,128)S(1)}, u32[]{:S(2)}) copy-start(f32[1,256]{1,0:T(1,128)S(1)} %get-tuple-element.1025) | copy-start | bytes 3076
  11.0 297.4 %copy-start.46 = (f32[1,256]{1,0:T(1,128)}, f32[1,256]{1,0:T(1,128)S(1)}, u32[]{:S(2)}) copy-start(f32[1,256]{1,0:T(1,128)S(1)} %get-tuple-element.1026) | copy-start | bytes 3076
  31.3 166.0 %copy-start.15 = (f32[16,1,128]{2,1,0:T(1,128)}, f32[16,1,128]{2,1,0:T(1,128)S(1)}, u32[]{:S(2)}) copy-start(f32[16,1,128]{2,1,0:T(1,128)S(1)} %convert_element_type.120) | copy-start | bytes 24580
  33.5 163.8 %copy-start.22 = (f32[256]{0:T(256)}, f32[256]{0:T(256)S(1)}, u32[]{:S(2)}) copy-start(f32[256]{0:T(256)S(1)} %fusion.95) | copy-start | bytes 3076
  51.1 257.4 %copy-start.25 = (f32[4096,1]{0,1:T(1,128)}, f32[4096,1]{0,1:T(1,128)S(1)}, u32[]{:S(2)}) copy-start(f32[4096,1]{0,1:T(1,128)S(1)} %get-tuple-element.1020) | copy-start | bytes 49156
  51.1 257.4 %copy-start.27 = (f32[4096,1]{0,1:T(1,128)}, f32[4096,1]{0,1:T(1,128)S(1)}, u32[]{:S(2)}) copy-start(f32[4096,1]{0,1:T(1,128)S(1)} %get-tuple-element.1021) | copy-start | bytes 49156
  51.1 257.4 %copy-start.29 = (f32[4096,1]{0,1:T(1,128)}, f32[4096,1]{0,1:T(1,128)S(1)}, u32[]{:S(2)}) copy-start(f32[4096,1]{0,1:T(1,128)S(1)} %get-tuple-element.1022) | copy-start | bytes 49156
  51.1 257.4 %copy-start.31 = (f32[4096,1]{0,1:T(1,128)}, f32[4096,1]{0,1:T(1,128)S(1)}, u32[]{:S(2)}) copy-start(f32[4096,1]{0,1:T(1,128)S(1)} %get-tuple-element.1023) | copy-start | bytes 49156
  107.4 89.9 %copy-start.12 = (bf16[4096,16]{0,1:T(8,128)(2,1)}, bf16[4096,16]{0,1:T(8,128)(2,1)S(1)}, u32[]{:S(2)}) copy-start(bf16[4096,16]{0,1:T(8,128)(2,1)S(1)} %all_gather.41) | copy-start | bytes 393220
  2124.2 126.0 %reduce-scatter.11.cloned.1.call-start = ((), (), s32[]{:S(2)}) async-start(), calls=%async_computation.11 | async-start | bytes 2785280 | tf_op jit(solution)/shard_map/reduce_scatter | solution.py:218
  2153.5 433.6 %reduce-scatter.17.cloned.1.call-start = ((), (), s32[]{:S(2)}) async-start(), calls=%async_computation.14 | async-start | bytes 35651584 | tf_op jit(solution)/shard_map/reduce_scatter | solution.py:223
  2191.5 1035.7 %reduce-scatter.9.cloned.1.call-start = ((), (), s32[]{:S(2)}) async-start(), calls=%async_computation.10 | async-start | bytes 71303168 | tf_op jit(solution)/shard_map/reduce_scatter | solution.py:215
  2227.1 1081.8 %reduce-scatter.19.cloned.1.call-start = ((), (), s32[]{:S(2)}) async-start(), calls=%async_computation.15 | async-start | bytes 2228224
  2231.4 995.8 %copy-start.53 = (u32[32]{0:T(128)S(1)}, u32[32]{0:T(128)}, u32[]{:S(2)}) copy-start(u32[32]{0:T(128)} %constant.296) | copy-start | bytes 388
  2231.5 1119.3 %reduce-scatter.15.cloned.1.call-start = ((), (), s32[]{:S(2)}) async-start(), calls=%async_computation.13 | async-start | bytes 278528 | tf_op jit(solution)/shard_map/reduce_scatter | solution.py:221
  2232.3 1282.0 %all-reduce.99.cloned.1.call-start = ((), (), s32[]{:S(2)}) async-start(), calls=%async_computation.16 | async-start | bytes 13172736 | tf_op jit(solution)/shard_map/psum | solution.py:236
  (56 other events, 830.8 us)
Sparse Core Ops, SparseCore 0:
  9.7 170.4 all-gather.8
  182.3 126.0 all-gather.14
  310.6 37.5 all-gather.10
  350.2 36.5 all-gather.12
  2124.3 58.9 reduce-scatter.12
  2187.3 62.8 reduce-scatter.10
  2255.1 331.9 reduce-scatter.16
  2591.9 635.2 reduce-scatter.8
  3232.0 60.9 reduce-scatter.18
  3296.4 54.2 reduce-scatter.14
  3353.4 160.8 all-reduce.98
where the time goes:
time: 3560 us; the launch traced here: 3530 us
  waiting for transfers between devices  1430 us (40%)
  other arithmetic  1370 us (38%)
  local copies, waits for them, and re-layouts  404 us (11%)
  blocking collectives  168 us (5%)
  matrix products  129 us (4%)
    reduce_scatter x1, waiting for transfers between devices, shards(): lax.psum_scatter(grad_in, 'fsdp', scatter_dimension=0, tiled=True)  640 us
    reduce_sum x96, other arithmetic, scan_block(): steps_in[position][:, None, :] * decay_rates[None]  526 us
    reduce_sum x80, other arithmetic, scan_block(): jnp.sum(hidden_state * out_gate[position][:, :, None], axis=1)  370 us
    reduce_scatter x1, waiting for transfers between devices, shards(): lax.psum_scatter(grad_out, 'fsdp', scatter_dimension=0, tiled=True)  337 us
    add_any x16, other arithmetic, selective_scan(): final_state, outputs = lax.scan(runner, initial, pieces)  193 us
    while x800, local copies, waits for them, and re-layouts  187 us
    psum x1, waiting for transfers between devices, shards(): lax.psum((share_gain, share_in, share_taps, share_offset, share_select, s...  157 us
    reduce_sum x32, other arithmetic, scan_block(): hidden_state * out_gate[position][:, :, None]  122 us
  transfers between devices with their start and end apart: 11, of which 9 were waited for; matrix products, arithmetic and copies ran while one was open for 5% of the time, Pallas kernels for 0%

commit v1 on v0

v1 whole, which is shorter than its diff:
```python
import functools

import jax
import jax.numpy as jnp
from jax import lax
from jax.experimental import pallas as pl
from jax.experimental.pallas import tpu as pltpu
from jax.sharding import Mesh
from jax.sharding import PartitionSpec as P

F32 = jnp.float32
BF16 = jnp.bfloat16
epsilon = 1e-05
PLANE = ("x", "y", "c")
BIG = 1e30
STEPS = 32
INNER = 4
LOG2E = 1.4426950408889634


def dot(a, b, dims):
    return lax.dot_general(a, b, (dims, ((), ())), preferred_element_type=F32)


def dot_nn(a, b):
    return dot(a, b, ((1,), (0,)))


def dot_tn(a, b):
    return dot(a, b, ((0,), (0,)))


def dot_nt(a, b):
    return dot(a, b, ((1,), (1,)))


def fwd_kernel(states, dt_ref, dtm_ref, x_ref, bc_ref, rate_ref, y_ref, hist_ref, last_ref, h_ref):
    @pl.when(pl.program_id(0) == 0)
    def _():
        h_ref[...] = jnp.zeros_like(h_ref)

    width = dt_ref.shape[2]
    groups = width // 128

    def body(tb, carry):
        t0 = tb * INNER
        bc = [bc_ref[t0 + i] for i in range(INNER)]
        for g in range(groups):
            lanes = pl.ds(g * 128, 128)
            dtm = [dtm_ref[t0 + i, :, lanes] for i in range(INNER)]
            u = [dt_ref[t0 + i, :, lanes] * x_ref[t0 + i, :, lanes] for i in range(INNER)]
            y = [None] * INNER
            for n in range(states):
                h = h_ref[n, :, lanes]
                rate = rate_ref[n, :, lanes]
                for i in range(INNER):
                    hist_ref[t0 + i, n, :, lanes] = h
                    a = jnp.exp2(dtm[i] * rate)
                    h = a * h + u[i] * bc[i][:, n : n + 1]
                    term = h * bc[i][:, states + n : states + n + 1]
                    y[i] = term if y[i] is None else y[i] + term
                h_ref[n, :, lanes] = h
            for i in range(INNER):
                y_ref[t0 + i, :, lanes] = y[i]
        return carry

    lax.fori_loop(0, dt_ref.shape[0] // INNER, body, 0)
    last_ref[...] = h_ref[...]


def scan_forward(dt, dtm, x, bc, rate):
    length, seqs, width = dt.shape
    states = rate.shape[0]
    block = lambda *tail: pl.BlockSpec((STEPS,) + tail, lambda i: (i,) + (0,) * len(tail))
    whole = lambda *dims: pl.BlockSpec(dims, lambda i: (0,) * len(dims))
    return pl.pallas_call(
        functools.partial(fwd_kernel, states),
        grid=(length // STEPS,),
        in_specs=[
            block(seqs, width),
            block(seqs, width),
            block(seqs, width),
            block(seqs, 2 * states),
            whole(states, seqs, width),
        ],
        out_specs=[block(seqs, width), block(states, seqs, width), whole(states, seqs, width)],
        out_shape=[
            jax.ShapeDtypeStruct(dt.shape, F32),
            jax.ShapeDtypeStruct((length, states, seqs, width), F32),
            jax.ShapeDtypeStruct((states, seqs, width), F32),
        ],
        scratch_shapes=[pltpu.VMEM((states, seqs, width), F32)],
        compiler_params=pltpu.CompilerParams(vmem_limit_bytes=56 << 20),
    )(dt, dtm, x, bc, rate)


def bwd_kernel(
    states,
    dt_ref,
    dtm_ref,
    x_ref,
    ds_ref,
    bc_ref,
    rate_ref,
    hist_ref,
    last_ref,
    ones_ref,
    s1_ref,
    s2_ref,
    gates_ref,
    da_ref,
    ag_ref,
    h_ref,
    pb_ref,
    pc_ref,
):
    @pl.when(pl.program_id(0) == 0)
    def _():
        ag_ref[...] = jnp.zeros_like(ag_ref)
        da_ref[...] = jnp.zeros_like(da_ref)
        h_ref[...] = last_ref[...]

    steps, seqs, width = dt_ref.shape
    groups = width // 128
    blocks = steps // INNER

    def body(back, carry):
        t0 = (blocks - 1 - back) * INNER
        rows = pl.multiple_of(t0 * seqs, INNER * seqs)
        bc = [bc_ref[t0 + i] for i in range(INNER)]
        for g in range(groups):
            lanes = pl.ds(g * 128, 128)
            dt = [dt_ref[t0 + i, :, lanes] for i in range(INNER)]
            dtm = [dtm_ref[t0 + i, :, lanes] for i in range(INNER)]
            ds = [ds_ref[t0 + i, :, lanes] for i in range(INNER)]
            u = [dt[i] * x_ref[t0 + i, :, lanes] for i in range(INNER)]
            s1 = [None] * INNER
            s2 = [None] * INNER
            for n in range(states):
                ag = ag_ref[n, :, lanes]
                h = h_ref[n, :, lanes]
                rate = rate_ref[n, :, lanes]
                da = da_ref[n, :, lanes]
                pb = [None] * INNER
                pc = [None] * INNER
                for i in reversed(range(INNER)):
                    prev = hist_ref[t0 + i, n, :, lanes]
                    a = jnp.exp2(dtm[i] * rate)
                    adj = ds[i] * bc[i][:, states + n : states + n + 1] + ag
                    pc[i] = ds[i] * h
                    pb[i] = adj * u[i]
                    ag = a * adj
                    w = ag * prev
                    rw = rate * w
                    gb = adj * bc[i][:, n : n + 1]
                    s1[i] = rw if s1[i] is None else s1[i] + rw
                    s2[i] = gb if s2[i] is None else s2[i] + gb
                    da = da + dt[i] * w
                    h = prev
                ag_ref[n, :, lanes] = ag
                h_ref[n, :, lanes] = h
                da_ref[n, :, lanes] = da
                cols = pl.ds((g * states + n) * 128, 128)
                pb_ref[pl.ds(rows, INNER * seqs), cols] = jnp.concatenate(pb, axis=0).astype(BF16)
                pc_ref[pl.ds(rows, INNER * seqs), cols] = jnp.concatenate(pc, axis=0).astype(BF16)
            for i in range(INNER):
                s1_ref[t0 + i, :, lanes] = s1[i]
                s2_ref[t0 + i, :, lanes] = s2[i]
        return carry

    lax.fori_loop(0, blocks, body, 0)
    span = states * 128
    total = jnp.zeros((steps * seqs, 128), F32)
    for g in range(groups):
        total = total + dot_nn(pb_ref[:, pl.ds(g * span, span)], ones_ref[0])
        total = total + dot_nn(pc_ref[:, pl.ds(g * span, span)], ones_ref[1])
    gates_ref[...] = total


def scan_backward(dt, dtm, x, ds, bc, rate, hist, last):
    length, seqs, width = dt.shape
    states = rate.shape[0]
    chunks = length // STEPS
    block = lambda *tail: pl.BlockSpec((STEPS,) + tail, lambda i: (chunks - 1 - i,) + (0,) * len(tail))
    whole = lambda *dims: pl.BlockSpec(dims, lambda i: (0,) * len(dims))
    span = states * 128
    entry = jnp.arange(span)[:, None] // 128
    column = jnp.arange(128)[None, :]
    ones = jnp.stack([entry == column, entry + states == column]).astype(BF16)
    return pl.pallas_call(
        functools.partial(bwd_kernel, states),
        grid=(chunks,),
        in_specs=[
            block(seqs, width),
            block(seqs, width),
            block(seqs, width),
            block(seqs, width),
            block(seqs, 2 * states),
            whole(states, seqs, width),
            block(states, seqs, width),
            whole(states, seqs, width),
            whole(2, span, 128),
        ],
        out_specs=[
            block(seqs, width),
            block(seqs, width),
            pl.BlockSpec((STEPS * seqs, 128), lambda i: (chunks - 1 - i, 0)),
            whole(states, seqs, width),
        ],
        out_shape=[
            jax.ShapeDtypeStruct(dt.shape, F32),
            jax.ShapeDtypeStruct(dt.shape, F32),
            jax.ShapeDtypeStruct((length * seqs, 128), F32),
            jax.ShapeDtypeStruct((states, seqs, width), F32),
        ],
        scratch_shapes=[
            pltpu.VMEM((states, seqs, width), F32),
            pltpu.VMEM((states, seqs, width), F32),
            pltpu.VMEM((STEPS * seqs, width // 128 * span), BF16),
            pltpu.VMEM((STEPS * seqs, width // 128 * span), BF16),
        ],
        compiler_params=pltpu.CompilerParams(vmem_limit_bytes=60 << 20),
    )(dt, dtm, x, ds, bc, rate, hist, last, ones)


MESH = pl.DeviceIdType.MESH
RING = 4


def place():
    return {a: lax.axis_index(a) for a in ("x", "z", "y", "c")}


def ring_chip(p):
    y = p // 2
    return (p + y) % 2, y


def ring_at(x, y):
    return 2 * y + (x + y) % 2


def share_at(f):
    return {"z": f // 4, "y": f // 2 % 2, "c": f % 2}


def remote(src, dst, send, recv, device):
    return pltpu.make_async_remote_copy(
        src_ref=src, dst_ref=dst, send_sem=send, recv_sem=recv, device_id=device, device_id_type=MESH
    )


def greet(devices):
    barrier = pltpu.get_barrier_semaphore()
    for device in devices:
        pl.semaphore_signal(barrier, inc=1, device_id=device, device_id_type=MESH)
    pl.semaphore_wait(barrier, len(devices))


def plane_others(me):
    out = []
    for dx in range(2):
        for dy in range(2):
            for dc in range(2):
                if dx + dy + dc:
                    out.append(
                        {"x": (me["x"] + dx) % 2, "y": (me["y"] + dy) % 2, "c": (me["c"] + dc) % 2}
                    )
    return out


def share_others(me, shares):
    f = me["z"] * 4 + me["y"] * 2 + me["c"]
    return [share_at((f + k) % shares) for k in range(1, shares)]


def z_only(me, shares):
    f = me["c"] + 2 * me["y"]
    out = []
    for dz in range(1, shares // 4):
        for k in range(4):
            out.append(
                {
                    "z": (me["z"] + dz) % (shares // 4),
                    "y": (f + k) % 4 // 2,
                    "c": (f + k) % 2,
                }
            )
    return out


def start_kernel(
    z_size,
    tokens_ref,
    gain_ref,
    ids_ref,
    conv_ref,
    gate_ref,
    small_ref,
    normed_all,
    conv_all,
    gate_all,
    small_all,
    ids_all,
    gain_all,
    normed_ref,
    gain_got,
    local_sem,
    gain_send,
    gain_recv,
    ids_send,
    ids_recv,
    conv_send,
    conv_recv,
    gate_send,
    gate_recv,
    ring_send,
    ring_recv,
    sib_send,
    sib_recv,
    up_send,
    up_recv,
    down_send,
    down_recv,
):
    me = place()
    x, y, z, c = me["x"], me["y"], me["z"], me["c"]
    shares = z_size * 4
    share = z * 4 + y * 2 + c
    corner = y * 2 + c
    seq = x * 4 + y * 2 + c
    greet(plane_others(me) + z_only(me, shares))

    swaps = []
    for k in range(1, 4):
        to = (corner + k) % 4
        device = {"y": to // 2, "c": to % 2}
        swaps.append(
            remote(conv_ref.at[to], conv_all.at[z, corner], conv_send.at[k - 1], conv_recv.at[k - 1], device)
        )
    for copy in swaps:
        copy.start()
    gains = [
        remote(gain_ref, gain_got.at[share], gain_send.at[k], gain_recv.at[k], device)
        for k, device in enumerate(share_others(me, shares))
    ]
    for copy in gains:
        copy.start()
    own = [
        pltpu.make_async_copy(conv_ref.at[corner], conv_all.at[z, corner], local_sem.at[0]),
        pltpu.make_async_copy(small_ref, small_all.at[z], local_sem.at[1]),
        pltpu.make_async_copy(gate_ref.at[corner], gate_all.at[corner], local_sem.at[2]),
    ]
    for copy in own:
        copy.start()
    others = plane_others(me)
    ids_copies = [
        remote(ids_ref, ids_all.at[seq], ids_send.at[k], ids_recv.at[k], device)
        for k, device in enumerate(others)
    ]
    for copy in ids_copies:
        copy.start()
    ids_all[seq] = ids_ref[...]
    gain_got[share] = gain_ref[...]

    values = tokens_ref[...].astype(F32)
    rstd = lax.rsqrt(jnp.mean(values * values, axis=-1, keepdims=True) + epsilon)
    for copy in gains:
        copy.wait()
    piece = gain_ref.shape[1]
    for f in range(shares):
        cols = pl.ds(f * piece, piece)
        part = tokens_ref[:, cols].astype(F32) * rstd * gain_got[f, 0:1, :]
        normed_ref[:, cols] = part.astype(BF16)
    gain_all[...] = gain_got[...]

    at = ring_at(x, y)
    step = 1 + 2 * c
    nx, ny = ring_chip((at + step) % RING)
    following = {"x": nx, "y": ny}
    sibling = {"c": 1 - c}

    def slot(k):
        ox, oy = ring_chip((at + (RING - step) * k) % RING)
        return ox * 4 + oy * 2 + c

    def ring(k):
        src = normed_ref if k == 0 else normed_all.at[slot(k)]
        return remote(src, normed_all.at[slot(k)], ring_send.at[k], ring_recv.at[k], following)

    def sib(k):
        src = normed_ref if k == 0 else normed_all.at[slot(k)]
        return remote(src, normed_all.at[slot(k)], sib_send.at[k], sib_recv.at[k], sibling)

    keep = pltpu.make_async_copy(normed_ref, normed_all.at[seq], local_sem.at[3])
    keep.start()
    ring(0).start()
    sib(0).start()

    for copy in swaps:
        copy.wait()
    for copy in own:
        copy.wait()

    def upward(k, j):
        ref = (conv_all, small_all)[j].at[z - k]
        return remote(ref, ref, up_send.at[k, j], up_recv.at[k, j], {"z": z + 1})

    def downward(k, j):
        ref = (conv_all, small_all)[j].at[z + k]
        return remote(ref, ref, down_send.at[k, j], down_recv.at[k, j], {"z": z - 1})

    def send_up(k):
        @pl.when((z < z_size - 1) & (z >= k))
        def _():
            upward(k, 0).start()
            upward(k, 1).start()

    def send_down(k):
        @pl.when((z > 0) & (z + k < z_size))
        def _():
            downward(k, 0).start()
            downward(k, 1).start()

    send_up(0)
    send_down(0)
    gates = []
    for k in range(1, 4):
        to = (corner + k) % 4
        device = {"y": to // 2, "c": to % 2}
        gates.append(
            remote(gate_ref.at[to], gate_all.at[corner], gate_send.at[k - 1], gate_recv.at[k - 1], device)
        )
    for copy in gates:
        copy.start()
    for k in range(max(z_size - 1, RING - 1)):
        if k < z_size - 1:
            @pl.when(z > k)
            def _():
                upward(k, 0).wait_recv()
                upward(k, 1).wait_recv()

            send_up(k + 1)

            @pl.when(z + k < z_size - 1)
            def _():
                downward(k, 0).wait_recv()
                downward(k, 1).wait_recv()

            send_down(k + 1)
        if k < RING - 1:
            ring(k).wait_recv()
            if k + 1 < RING - 1:
                ring(k + 1).start()
            sib(k + 1).start()

    for k in range(z_size - 1):
        @pl.when((z < z_size - 1) & (z >= k))
        def _():
            upward(k, 0).wait_send()
            upward(k, 1).wait_send()

        @pl.when((z > 0) & (z + k < z_size))
        def _():
            downward(k, 0).wait_send()
            downward(k, 1).wait_send()

    for k in range(RING - 1):
        ring(k).wait_send()
    for k in range(RING):
        sib(k).wait()
    for copy in gates + ids_copies + [keep]:
        copy.wait()


def start_gathers(z_size, tokens, gain, ids, conv, gate, small):
    length, width = tokens.shape
    shares = z_size * 4
    any_space = pl.BlockSpec(memory_space=pl.ANY)
    vmem = pl.BlockSpec(memory_space=pltpu.VMEM)
    dma = pltpu.SemaphoreType.DMA
    hops = max(z_size - 1, 1)
    return pl.pallas_call(
        functools.partial(start_kernel, z_size),
        in_specs=[vmem, vmem, vmem, any_space, any_space, any_space],
        out_specs=[any_space, any_space, any_space, any_space, vmem, vmem],
        out_shape=[
            jax.ShapeDtypeStruct((8,) + tokens.shape, BF16),
            jax.ShapeDtypeStruct((z_size,) + conv.shape, BF16),
            jax.ShapeDtypeStruct(gate.shape, BF16),
            jax.ShapeDtypeStruct((z_size,) + small.shape, BF16),
            jax.ShapeDtypeStruct((8,) + ids.shape, ids.dtype),
            jax.ShapeDtypeStruct((shares,) + gain.shape, F32),
        ],
        scratch_shapes=[
            pltpu.VMEM(tokens.shape, BF16),
            pltpu.VMEM((shares,) + gain.shape, F32),
            dma((4,)),
            dma((shares - 1,)),
            dma((shares - 1,)),
            dma((7,)),
            dma((7,)),
            dma((3,)),
            dma((3,)),
            dma((3,)),
            dma((3,)),
            dma((RING - 1,)),
            dma((RING - 1,)),
            dma((RING,)),
            dma((RING,)),
            dma((hops, 2)),
            dma((hops, 2)),
            dma((hops, 2)),
            dma((hops, 2)),
        ],
        compiler_params=pltpu.CompilerParams(
            collective_id=0, has_side_effects=True, vmem_limit_bytes=40 << 20
        ),
    )(tokens, gain, ids, conv, gate, small)


def total_kernel(part_ref, out_ref, first, from_sib, stage, got, sib_s, sib_r, rs_s, rs_r, ag_s, ag_r, fw_s, fw_r):
    me = place()
    x, y, c = me["x"], me["y"], me["c"]
    greet(plane_others(me))
    sibling = {"c": 1 - c}
    first[...] = part_ref[:, 1 - c].astype(BF16)
    swap = remote(first, from_sib, sib_s, sib_r, sibling)
    swap.start()
    swap.wait()
    mine = x * 2 + y
    chips = [((x + d // 2) % 2, (y + d % 2) % 2) for d in (1, 2, 3)]
    sends = []
    for k in (2, 1, 0):
        ox, oy = chips[k]
        j = ox * 2 + oy
        stage[k] = (part_ref[j, c] + from_sib[j].astype(F32)).astype(BF16)
        copy = remote(stage.at[k], got.at[k], rs_s.at[k], rs_r.at[k], {"x": ox, "y": oy})
        copy.start()
        sends.append(copy)
    total = part_ref[mine, c] + from_sib[mine].astype(F32)
    for copy in sends:
        copy.wait()
    for k in range(3):
        total = total + got[k].astype(F32)
    out_ref[mine, c] = total.astype(BF16)
    spreads = []
    for k in (2, 1, 0):
        ox, oy = chips[k]
        here = out_ref.at[mine, c]
        copy = remote(here, here, ag_s.at[k], ag_r.at[k], {"x": ox, "y": oy})
        copy.start()
        spreads.append((k, copy))
    forwards = []
    here = out_ref.at[mine, c]
    forwards.append(remote(here, here, fw_s.at[3], fw_r.at[3], sibling))
    forwards[0].start()
    for k, copy in reversed(spreads):
        copy.wait_recv()
        ox, oy = chips[k]
        block = out_ref.at[ox * 2 + oy, c]
        forwards.append(remote(block, block, fw_s.at[k], fw_r.at[k], sibling))
        forwards[-1].start()
    for _, copy in spreads:
        copy.wait_send()
    for copy in forwards:
        copy.wait()


def plane_total(part, collective_id):
    rows, cols = part.shape
    block = (rows // 8, cols)
    vmem = pl.BlockSpec(memory_space=pltpu.VMEM)
    dma = pltpu.SemaphoreType.DMA
    out = pl.pallas_call(
        total_kernel,
        in_specs=[vmem],
        out_specs=vmem,
        out_shape=jax.ShapeDtypeStruct((4, 2) + block, BF16),
        scratch_shapes=[
            pltpu.VMEM((4,) + block, BF16),
            pltpu.VMEM((4,) + block, BF16),
            pltpu.VMEM((3,) + block, BF16),
            pltpu.VMEM((3,) + block, BF16),
            dma(()),
            dma(()),
            dma((3,)),
            dma((3,)),
            dma((3,)),
            dma((3,)),
            dma((4,)),
            dma((4,)),
        ],
        compiler_params=pltpu.CompilerParams(
            collective_id=collective_id, has_side_effects=True, vmem_limit_bytes=40 << 20
        ),
    )(part.reshape((4, 2) + block))
    return out.reshape(rows, cols)


def add_rows(dst, srcs, rows):
    count = dst.shape[0] // rows

    def body(i, carry):
        at = pl.ds(pl.multiple_of(i * rows, rows), rows)
        total = srcs[0][at].astype(F32)
        for src in srcs[1:]:
            total = total + src[at].astype(F32)
        dst[at] = total.astype(dst.dtype)
        return carry

    lax.fori_loop(0, count, body, 0)


def finish_kernel(
    z_size,
    back_ref,
    small_ref,
    gate_ref,
    conv_ref,
    tokens_ref,
    cot_ref,
    gain_ref,
    tgrad_ref,
    in_ref,
    small_out,
    gain_out,
    own_back,
    sib_back,
    ring_stage,
    ring_got,
    own_small,
    own_gate,
    own_conv,
    up_small,
    up_gate,
    up_conv,
    down_small,
    down_gate,
    down_conv,
    up_stage_small,
    up_stage_gate,
    up_stage_conv,
    down_stage_small,
    down_stage_gate,
    down_stage_conv,
    fin_gate,
    fin_conv,
    both_gate,
    both_conv,
    gain_parts,
    gain_got,
    gain_half,
    gain_pair,
    local_sem,
    back_sem,
    sib_send,
    sib_recv,
    ring_send,
    ring_recv,
    up_send,
    up_recv,
    down_send,
    down_recv,
    swap_send,
    swap_recv,
    x_send,
    x_recv,
    gain_send,
    gain_recv,
):
    me = place()
    x, y, z, c = me["x"], me["y"], me["z"], me["c"]
    shares = z_size * 4
    share = z * 4 + y * 2 + c
    corner = y * 2 + c
    sibling = {"c": 1 - c}
    over_x = {"x": 1 - x}
    greet(plane_others(me) + z_only(me, shares))

    at = ring_at(x, y)
    step = 1 + 2 * c
    sib_step = 3 - 2 * c
    nx, ny = ring_chip((at + step) % RING)
    following = {"x": nx, "y": ny}

    def chip_index(p):
        cx, cy = ring_chip(p % RING)
        return cx * 2 + cy

    owns = (own_small, own_gate, own_conv)
    locals_ = [
        pltpu.make_async_copy(src, dst, local_sem.at[i])
        for i, (src, dst) in enumerate(zip((small_ref, gate_ref, conv_ref), owns))
    ]
    for copy in locals_:
        copy.start()
    backs = []
    sibs = []
    for k in range(RING):
        backs.append(
            pltpu.make_async_copy(
                back_ref.at[chip_index(at + step * (RING - 1 - k)), c], own_back.at[k], back_sem.at[k]
            )
        )
        sibs.append(
            remote(
                back_ref.at[chip_index(at + sib_step * (RING - 1 - k)), 1 - c],
                sib_back.at[k],
                sib_send.at[k],
                sib_recv.at[k],
                sibling,
            )
        )
    for k in range(RING):
        backs[k].start()
        sibs[k].start()

    ups = (up_small, up_gate, up_conv)
    downs = (down_small, down_gate, down_conv)
    up_stages = (up_stage_small, up_stage_gate, up_stage_conv)
    down_stages = (down_stage_small, down_stage_gate, down_stage_conv)
    blocks = (16, 64, 64)

    def up_copy(k, h):
        return remote(
            up_stages[h].at[k], ups[h].at[k], up_send.at[k, h], up_recv.at[k, h], {"z": z + 1}
        )

    def down_copy(k, h):
        return remote(
            down_stages[h].at[k], downs[h].at[k], down_send.at[k, h], down_recv.at[k, h], {"z": z - 1}
        )

    def line(k, h):
        high = z_size - 1 - k

        @pl.when((z < high) & (z > 0))
        def _():
            up_copy(k, h).wait_recv()
            add_rows(up_stages[h].at[k], [owns[h].at[high], ups[h].at[k]], blocks[h])
            up_copy(k, h).start()

        @pl.when((z < high) & (z == 0))
        def _():
            add_rows(up_stages[h].at[k], [owns[h].at[high]], blocks[h])
            up_copy(k, h).start()

        @pl.when((z > k) & (z < z_size - 1))
        def _():
            down_copy(k, h).wait_recv()
            add_rows(down_stages[h].at[k], [owns[h].at[k], downs[h].at[k]], blocks[h])
            down_copy(k, h).start()

        @pl.when((z > k) & (z == z_size - 1))
        def _():
            add_rows(down_stages[h].at[k], [owns[h].at[k]], blocks[h])
            down_copy(k, h).start()

    def settle(h, dst):
        low = z
        high = z_size - 1 - z

        @pl.when(z == 0)
        def _():
            down_copy(low, h).wait_recv()
            add_rows(dst, [owns[h].at[z], downs[h].at[low]], blocks[h])

        @pl.when(z == z_size - 1)
        def _():
            up_copy(high, h).wait_recv()
            add_rows(dst, [owns[h].at[z], ups[h].at[high]], blocks[h])

        @pl.when((z > 0) & (z < z_size - 1))
        def _():
            down_copy(low, h).wait_recv()
            up_copy(high, h).wait_recv()
            add_rows(dst, [owns[h].at[z], downs[h].at[low], ups[h].at[high]], blocks[h])

    def ring(k):
        return remote(ring_stage.at[k], ring_got.at[k], ring_send.at[k], ring_recv.at[k], following)

    def ring_step(k):
        backs[k].wait()
        sibs[k].wait_recv()
        srcs = [own_back.at[k], sib_back.at[k]]
        if k:
            ring(k - 1).wait_recv()
            srcs.append(ring_got.at[k - 1])
        add_rows(ring_stage.at[k], srcs, 16)
        ring(k).start()

    def ring_end():
        last = RING - 1
        backs[last].wait()
        sibs[last].wait_recv()
        ring(last - 1).wait_recv()
        rows = 16
        width = tokens_ref.shape[1]

        def body(i, total):
            r = pl.ds(pl.multiple_of(i * rows, rows), rows)
            back = (
                own_back[last, r].astype(F32)
                + sib_back[last, r].astype(F32)
                + ring_got[last - 1, r].astype(F32)
            )
            values = tokens_ref[r].astype(F32)
            rstd = lax.rsqrt(jnp.mean(values * values, axis=-1, keepdims=True) + epsilon)
            scaled = back * gain_ref[...]
            inner = jnp.mean(scaled * values, axis=-1, keepdims=True)
            grad = cot_ref[r].astype(F32) + rstd * scaled - values * (rstd * rstd * rstd * inner)
            tgrad_ref[r] = grad.astype(BF16)
            terms = back * values * rstd
            return total + terms[:8] + terms[8:]

        total = lax.fori_loop(
            0, tokens_ref.shape[0] // rows, body, jnp.zeros((8, width), F32)
        )
        total = jnp.broadcast_to(jnp.sum(total, axis=0, keepdims=True), (8, width))
        piece = gain_parts.shape[2]
        for f in range(shares):
            gain_parts[f] = total[:, f * piece : (f + 1) * piece]
        gain_got[share] = gain_parts[share]

    gains = []
    for k in range(1, shares):
        f = (share + k) % shares
        gains.append(
            remote(
                gain_parts.at[f], gain_got.at[share], gain_send.at[k - 1], gain_recv.at[k - 1], share_at(f)
            )
        )

    for copy in locals_:
        copy.wait()
    hops = z_size - 1
    for h in range(3):
        line(0, h)
    ring_step(0)
    line(1, 0)
    line(1, 1)
    ring_step(1)
    line(1, 2)
    ring_step(2)
    line(2, 0)
    line(2, 1)
    ring_end()
    for copy in gains:
        copy.start()
    line(2, 2)
    for k in range(3, hops):
        for h in range(3):
            line(k, h)

    settle(0, small_out.at[x])
    small_x = remote(small_out.at[x], small_out.at[x], x_send.at[0], x_recv.at[0], over_x)
    small_x.start()
    fins = (None, fin_gate, fin_conv)
    boths = (None, both_gate, both_conv)
    rows_in = in_ref.shape[0]
    swaps = {}
    for h in (1, 2):
        settle(h, fins[h])
        swaps[h] = []
        for k in range(1, 4):
            to = (corner + k) % 4
            copy = remote(
                fins[h].at[pl.ds(pl.multiple_of(to * rows_in, rows_in), rows_in)],
                boths[h].at[x, corner],
                swap_send.at[h - 1, k - 1],
                swap_recv.at[h - 1, k - 1],
                {"y": to // 2, "c": to % 2},
            )
            copy.start()
            swaps[h].append(copy)
        boths[h][x, corner] = fins[h][pl.ds(pl.multiple_of(corner * rows_in, rows_in), rows_in)]
        if h == 1:
            for copy in gains:
                copy.wait()
            gain_half[...] = jnp.sum(gain_got[...], axis=0)
            gain_x = remote(gain_half, gain_pair, x_send.at[3], x_recv.at[3], over_x)
            gain_x.start()
            for copy in swaps[1]:
                copy.wait()
            gate_x = remote(both_gate.at[x], both_gate.at[x], x_send.at[1], x_recv.at[1], over_x)
            gate_x.start()
    for copy in swaps[2]:
        copy.wait()
    conv_x = remote(both_conv.at[x], both_conv.at[x], x_send.at[2], x_recv.at[2], over_x)
    conv_x.start()

    half = small_ref.shape[1]
    branch = 8 * half * z_size

    def lay(h):
        first = branch if h == 1 else 0
        for zz in range(z_size):
            for j in range(4):
                for xx in range(2):
                    col = first + (zz * 4 + j) * 2 * half + xx * half
                    in_ref[:, col : col + half] = boths[h][xx, j, :, zz * half : (zz + 1) * half].astype(F32)

    gate_x.wait()
    lay(1)
    gain_x.wait()
    gain_out[...] = gain_half[...] + gain_pair[...]
    small_x.wait()
    conv_x.wait()
    lay(2)

    for k in range(hops):
        high = z_size - 1 - k
        for h in range(3):

            @pl.when(z < high)
            def _():
                up_copy(k, h).wait_send()

            @pl.when(z > k)
            def _():
                down_copy(k, h).wait_send()

    for k in range(RING - 1):
        ring(k).wait_send()
    for copy in sibs:
        copy.wait_send()


def last_sums(z_size, back, small, gate, conv, tokens, cot, gain, in_width):
    length, width = tokens.shape
    shares = z_size * 4
    hops = z_size - 1
    rows_in = gate.shape[1] // 4
    any_space = pl.BlockSpec(memory_space=pl.ANY)
    vmem = pl.BlockSpec(memory_space=pltpu.VMEM)
    dma = pltpu.SemaphoreType.DMA
    block = (length, width)
    slabs = [small.shape[1:], gate.shape[1:], conv.shape[1:]]
    bufs = lambda n: [pltpu.VMEM((n,) + s, BF16) for s in slabs]
    both = pltpu.VMEM((2, 4, rows_in, gate.shape[2]), BF16)
    piece = (8, width // shares)
    return pl.pallas_call(
        functools.partial(finish_kernel, z_size),
        in_specs=[any_space] * 4 + [vmem] * 3,
        out_specs=[vmem] * 4,
        out_shape=[
            jax.ShapeDtypeStruct(tokens.shape, BF16),
            jax.ShapeDtypeStruct((rows_in, in_width), F32),
            jax.ShapeDtypeStruct((2,) + slabs[0], BF16),
            jax.ShapeDtypeStruct(piece, F32),
        ],
        scratch_shapes=[
            pltpu.VMEM((RING,) + block, BF16),
            pltpu.VMEM((RING,) + block, BF16),
            pltpu.VMEM((RING - 1,) + block, BF16),
            pltpu.VMEM((RING - 1,) + block, BF16),
        ]
        + bufs(z_size)
        + bufs(hops)
        + bufs(hops)
        + bufs(hops)
        + bufs(hops)
        + [
            pltpu.VMEM(slabs[1], BF16),
            pltpu.VMEM(slabs[2], BF16),
            both,
            both,
            pltpu.VMEM((shares,) + piece, F32),
            pltpu.VMEM((shares,) + piece, F32),
            pltpu.VMEM(piece, F32),
            pltpu.VMEM(piece, F32),
            dma((3,)),
            dma((RING,)),
            dma((RING,)),
            dma((RING,)),
            dma((RING - 1,)),
            dma((RING - 1,)),
            dma((hops, 3)),
            dma((hops, 3)),
            dma((hops, 3)),
            dma((hops, 3)),
            dma((2, 3)),
            dma((2, 3)),
            dma((4,)),
            dma((4,)),
            dma((shares - 1,)),
            dma((shares - 1,)),
        ],
        compiler_params=pltpu.CompilerParams(
            collective_id=3, has_side_effects=True, vmem_limit_bytes=60 << 20
        ),
    )(back, small, gate, conv, tokens, cot, gain)


def silu_and_slope(v):
    s = jax.nn.sigmoid(v)
    return v * s, s * (1.0 + v * (1.0 - s))


def shift_down(v, j):
    return jnp.pad(v, ((j, 0),) + ((0, 0),) * (v.ndim - 1))[: v.shape[0]]


def shift_up(v, j):
    return jnp.pad(v, ((0, j),) + ((0, 0),) * (v.ndim - 1))[j:]


def shards(
    tokens,
    doc_ids,
    norm_gain,
    in_weight,
    conv_taps,
    conv_offset,
    select_weight,
    step_weight,
    step_bias,
    decay_log,
    skip_gain,
    out_weight,
    cotangent,
):
    z_size = lax.axis_size("z")
    rh_size = lax.axis_size("rh")
    seqs = 8
    length = doc_ids.shape[1]
    width = tokens.shape[1]
    in_rows = in_weight.shape[0]
    rows = out_weight.shape[0]
    half = rows // 2
    chans = half * z_size
    taps = conv_taps.shape[1]
    rank = step_weight.shape[1]
    states = decay_log.shape[1]
    x_at = lax.axis_index("x")

    def own_half(w):
        return lax.dynamic_slice_in_dim(w, x_at * half, half, 0)

    cuts = [taps, 1, 1, 1, states, rank + 2 * states, rank]
    ends = [sum(cuts[: i + 1]) for i in range(len(cuts))]
    room = -ends[-1] % 128

    def parts(v):
        return [v[:, e - n : e] for e, n in zip(ends, cuts)]

    small = jnp.concatenate(
        [
            own_half(conv_taps),
            own_half(conv_offset)[:, None],
            own_half(step_bias)[:, None],
            own_half(skip_gain)[:, None],
            own_half(decay_log),
            own_half(select_weight),
            own_half(step_weight),
            jnp.zeros((half, room), BF16),
        ],
        axis=1,
    )
    picked = lax.dynamic_index_in_dim(
        in_weight.reshape(in_rows, 2, z_size, 4, 2, half), x_at, 4, keepdims=False
    )
    packed = picked.transpose(1, 3, 0, 2, 4).reshape(2, 4, in_rows, chans)
    gain_tile = jnp.broadcast_to(norm_gain.astype(F32)[None, :], (8, norm_gain.shape[0]))
    ids_tile = jnp.broadcast_to(doc_ids, (8, length))
    all_normed, w_conv, gate_slab, small_all, ids, gains = start_gathers(
        z_size, tokens, gain_tile, ids_tile, packed[0], packed[1], small
    )
    all_normed = all_normed.reshape(-1, width)
    w_conv = w_conv.reshape(-1, chans)
    w_gate = lax.all_gather(gate_slab, "z", axis=0, tiled=True).reshape(-1, chans)
    w_taps, w_offset, w_bias, w_skip, w_decay, w_select, w_step = parts(
        small_all.reshape(chans, -1)
    )
    w_out = lax.all_gather(own_half(out_weight), "z", axis=0, tiled=True)
    gain = gains[:, 0, :].reshape(1, width)
    ids = ids[:, 0, :].T
    all_cot = lax.all_gather(cotangent, PLANE, axis=0, tiled=True)
    residual = tokens.astype(F32)

    def time_major(v):
        return v.reshape(seqs, length, -1).swapaxes(0, 1)

    def seq_major(v):
        return v.reshape(length, seqs, -1).swapaxes(0, 1).reshape(seqs * length, -1)

    conv_in = time_major(dot_nn(all_normed, w_conv))
    gate_in = time_major(dot_nn(all_normed, w_gate))
    same = [
        (shift_down(ids + 1, j) == ids + 1).astype(F32)[:, :, None] for j in range(taps)
    ]
    tap = [w_taps[:, taps - 1 - j].astype(F32) for j in range(taps)]
    conv_out = w_offset[:, 0].astype(F32) + sum(
        shift_down(conv_in, j) * same[j] * tap[j] for j in range(taps)
    )
    selected_f, conv_slope = silu_and_slope(conv_out)
    selected = selected_f.astype(BF16)
    x = selected.astype(F32)
    flat = lambda v: v.reshape(length * seqs, -1)
    spare = -(rank + 2 * states) % 128
    wide_select = jnp.pad(w_select, ((0, 0), (0, spare)))
    selection = plane_total(dot_nn(flat(selected), wide_select), 1)
    rank_in = selection[:, :rank]
    bc = selection[:, rank : rank + 2 * states].astype(F32).reshape(length, seqs, 2 * states)
    pre = dot_nt(rank_in, w_step).reshape(length, seqs, chans) + w_bias[:, 0].astype(F32)
    dt = jax.nn.softplus(pre)
    dtm = dt + (1.0 - same[1]) * BIG
    rates = -jnp.exp(w_decay.astype(F32)).T
    rate2 = jnp.broadcast_to((rates * LOG2E)[:, None, :], (states, seqs, chans))
    y, hist, last = scan_forward(dt, dtm, x, bc, rate2)
    skip = w_skip[:, 0].astype(F32)
    scanned = y + skip * x
    gate, gate_slope = silu_and_slope(gate_in)
    gated = seq_major((scanned * gate).astype(BF16))
    out_part = dot_nn(gated, w_out).astype(BF16)
    layer_sum = lax.psum_scatter(out_part, PLANE, scatter_dimension=0, tiled=True)
    layer_out = (residual + layer_sum.astype(F32)).astype(BF16)

    grad_out = dot_tn(gated, all_cot).astype(BF16)
    back_gated = time_major(dot_nt(all_cot, w_out).astype(BF16)).astype(F32)
    back_scan = back_gated * gate
    back_gate_in = back_gated * scanned * gate_slope
    s1, s2, back_bc, da = scan_backward(dt, dtm, x, back_scan, bc, rate2, hist, last)
    back_steps = s1 * (1.0 / LOG2E) + x * s2
    back_x = dt * s2 + skip * back_scan
    grad_decay = da.sum(1).T * rates.T
    grad_skip = (back_scan * x).sum((0, 1))
    back_pre = back_steps * jax.nn.sigmoid(pre)
    grad_bias = back_pre.sum((0, 1))
    back_pre = flat(back_pre.astype(BF16))
    grad_step = dot_tn(back_pre, rank_in)
    back_rank = dot_nn(back_pre, w_step)
    back_selection = plane_total(
        jnp.concatenate([back_rank, back_bc[:, : rank + 2 * states + spare - rank]], axis=1), 2
    )[:, : rank + 2 * states]
    grad_select = dot_tn(flat(selected), back_selection)
    back_selected = dot_nt(back_selection, w_select).reshape(length, seqs, chans) + back_x
    back_conv = back_selected * conv_slope
    grad_offset = back_conv.sum((0, 1))
    grad_taps = jnp.stack(
        [
            (back_conv * shift_down(conv_in, j) * same[j]).sum((0, 1))
            for j in reversed(range(taps))
        ],
        axis=1,
    )
    back_conv_in = sum(
        shift_up(back_conv * same[j], j) * tap[j] for j in range(taps)
    )
    back_conv_in = seq_major(back_conv_in.astype(BF16))
    back_gate_in = seq_major(back_gate_in.astype(BF16))
    back_part = (dot_nt(back_conv_in, w_conv) + dot_nt(back_gate_in, w_gate)).astype(BF16)
    grad_conv = dot_tn(all_normed, back_conv_in).astype(BF16)
    grad_gate = dot_tn(all_normed, back_gate_in).astype(BF16)
    small_grad = jnp.concatenate(
        [
            grad_taps,
            grad_offset[:, None],
            grad_bias[:, None],
            grad_skip[:, None],
            grad_decay,
            grad_select,
            grad_step,
            jnp.zeros((chans, room), F32),
        ],
        axis=1,
    ).astype(BF16)
    tokens_grad, g_in, small_own, g_gain = last_sums(
        z_size,
        back_part.reshape(4, 2, length, width),
        small_grad.reshape(z_size, half, -1),
        grad_gate.reshape(z_size, -1, chans),
        grad_conv.reshape(z_size, -1, chans),
        tokens,
        cotangent,
        gain,
        in_weight.shape[1],
    )
    g_gain = g_gain[0]
    own_out = lax.psum_scatter(grad_out, "z", scatter_dimension=0, tiled=True)
    if rh_size > 1:
        small_own, g_in, own_out, g_gain = lax.psum(
            (small_own.astype(F32), g_in, own_out, g_gain), "rh"
        )
    g_out = lax.all_gather(own_out, "x", axis=0, tiled=True).astype(F32)
    g_taps, g_offset, g_bias, g_skip, g_decay, g_select, g_step = [
        v.astype(F32) for v in parts(small_own.reshape(rows, -1))
    ]
    return (
        layer_out,
        tokens_grad,
        g_gain,
        g_in,
        g_taps,
        g_offset[:, 0],
        g_select,
        g_step,
        g_bias[:, 0],
        g_decay,
        g_skip[:, 0],
        g_out,
    )


def solution(mesh):
    replicas = mesh.shape["replica"]
    shares = mesh.shape["fsdp"]
    grid = Mesh(
        mesh.devices.reshape(replicas // 2, 2, shares // 4, 2, 2), ("rh", "x", "z", "y", "c")
    )
    tok = ("rh", "x", "z", "y", "c")
    own = ("z", "y", "c")
    return jax.shard_map(
        shards,
        mesh=grid,
        in_specs=(
            P(tok, None),
            P(tok, None),
            P(own),
            P(own, None),
            P(own, None),
            P(own),
            P(own, None),
            P(own, None),
            P(own),
            P(own, None),
            P(own),
            P(own, None),
            P(tok, None),
        ),
        out_specs=(
            P(tok, None),
            P(tok, None),
            P(own),
            P(own, None),
            P(own, None),
            P(own),
            P(own, None),
            P(own, None),
            P(own),
            P(own, None),
            P(own),
            P(own, None),
        ),
        check_vma=False,
    )
```

time: 3560 us -> 730 us (0.21)
  waiting for transfers between devices: 1430 us -> 67.3 us
  other arithmetic: 1370 us -> 42.4 us
  Pallas kernels: 0 us -> 392 us
  local copies, waits for them, and re-layouts: 404 us -> 51.3 us
  blocking collectives: 168 us -> 0 us
    reduce_sum x276 -> x2, other arithmetic: 1100 us -> 2.63 us  [the longest x1 2.56 us: shards(): grad_bias = back_pre.sum((0, 1))]
    reduce_scatter x5 -> x2, waiting for transfers between devices: 1040 us -> 41.4 us  [the longest x1 41.4 us: shards(): own_out = lax.psum_scatter(grad_out, 'z', scatter_dimension=0, tiled=True)]
    pallas_call x0 -> x6, Pallas kernels: none -> 392 us  [the longest x1 154 us: last_sums(): pl.pallas_call(functools.partial(finish_kernel, z_size), in_specs=[any_sp...]
    all_gather x4, waiting for transfers between devices: 233 us -> 25.1 us  [the longest x1 25.1 us: shards(): lax.all_gather(gate_slab, 'z', axis=0, tiled=True).reshape(-1, chans)]
    add_any x50 -> x0, other arithmetic: 202 us -> none  [the longest x16 193 us: selective_scan(): final_state, outputs = lax.scan(runner, initial, pieces)]
    while x800 -> x0, local copies, waits for them, and re-layouts: 187 us -> none
    psum x1 -> x0, waiting for transfers between devices: 157 us -> none  [shards(): lax.psum((share_gain, share_in, share_taps, share_offset, share_select, s...]
    all_gather x6 -> x0, blocking collectives: 111 us -> none  [the longest x1 19.8 us: shards(): lax.all_gather(decay_log, 'fsdp', axis=0, tiled=True)]
  transfers between devices with their start and end apart: 11 -> 6, of which waited for: 9 -> 2; matrix products, arithmetic and copies ran while one was open for 5% -> 24% of each run, Pallas kernels for 0% -> 38%
where the time goes in v1:
time: 730 us; the launch traced here: 722 us
  Pallas kernels  392 us (54%)
  matrix products  154 us (21%)
  waiting for transfers between devices  67.3 us (9%)
  local copies, waits for them, and re-layouts  51.3 us (7%)
  other arithmetic  42.4 us (6%)
  between operations  15.3 us (2%)
    pallas_call x1, Pallas kernels, last_sums(): pl.pallas_call(functools.partial(finish_kernel, z_size), in_specs=[any_sp...  154 us
    dot_general x15, matrix products, dot(): return lax.dot_general(a, b, (dims, ((), ())), preferred_element_type=F32)  154 us
    pallas_call x1, Pallas kernels, start_gathers(): pl.pallas_call(functools.partial(start_kernel, z_size), in_specs=[vmem, v...  92.5 us
    pallas_call x1, Pallas kernels, scan_backward(): pl.pallas_call(functools.partial(bwd_kernel, states), grid=(chunks,), in_...  68.5 us
    pallas_call x2, Pallas kernels, plane_total(): pl.pallas_call(total_kernel, in_specs=[vmem], out_specs=vmem, out_shape=j...  45.7 us
    reduce_scatter x1, waiting for transfers between devices, shards(): own_out = lax.psum_scatter(grad_out, 'z', scatter_dimension=0, tiled=True)  41.4 us
    pallas_call x1, Pallas kernels, scan_forward(): pl.pallas_call(functools.partial(fwd_kernel, states), grid=(length // STE...  30.9 us
    all_gather x1, waiting for transfers between devices, shards(): lax.all_gather(gate_slab, 'z', axis=0, tiled=True).reshape(-1, chans)  25.1 us
  transfers between devices with their start and end apart: 6, of which 2 were waited for; matrix products, arithmetic and copies ran while one was open for 24% of the time, Pallas kernels for 38%

profile of v1, /device:TPU:11, one launch (start us, length us, event | category | flops | bytes accessed | tf_op | source)
XLA Modules:
  0.0 722.3 jit_solution(18341782398114037694)
XLA Ops:
  18.5 92.5 %shard_map.220 = (bf16[8,256,2048]{2,1,0:T(8,128)(2,1)S(1)}, bf16[4,4,128,512]{3,2,1,0:T(8,128)(2,1)S(1)}, bf16[4,128,512]{2,1,0:T(8,128)(2,1)}, bf16[4,128,384]...) custom-call(bf16[256,2048]{1,0:T(8,128)(2,1)S(1)} %copy-done.2, ...), custom_call_target="tpu_custom_call" | custom-call | tf_op jit(solution)/shard_map/pallas_call | solution.py:483
  120.6 15.3 %fusion.19 = f32[256,8,512]{2,1,0:T(8,128)} fusion(bf16[2048,512,1]{1,0,2:T(8,128)(2,1)S(1)} %bitcast.191, bf16[8,256,2048]{2,1,0:T(8,128)(2,1)} %copy-done.4), kind=kOutput, calls=%fused_computation.51 | convolution fusion | flops 4294967296 | bytes 14680064 | tf_op jit(solution)/shard_map/dot_general | solution.py:22
  135.9 10.6 %convert_bitcast_fusion = f32[2048,512]{0,1:T(8,128)} fusion(bf16[512,2048]{1,0:T(8,128)(2,1)} %all-gather.7.cloned.1.call-done, bf16[2048,2048]{1,0:T(8,128)(2,1)} %all-gather.9.cloned.1.call-done), kind=kOutput, calls=%fused_computation.37 | convolution fusion | flops 4297064448 | bytes 14680064 | tf_op jit(solution)/shard_map/dot_general | solution.py:22
  146.4 5.4 copy.150
  151.9 25.1 %all-gather.5.cloned.1.call-done = bf16[16,128,512]{2,1,0:T(8,128)(2,1)} async-done(((bf16[4,128,512]{2,1,0:T(8,128)(2,1)}), bf16[16,128,512]{2,1,0:T(8,128)(2,1)}) %all-gather.5.cloned.1.call-update) | async-done | bytes 2097168 | tf_op jit(solution)/shard_map/all_gather | solution.py:1072
  177.0 24.1 %multiply_reduce_fusion = (bf16[512]{0:T(512)(128)(2,1)S(1)}, f32[256,8,512]{2,1,0:T(8,128)}, bf16[256,8,512]{2,1,0:T(8,128)(2,1)S(1)}, f32[256,8,512]{2,1,0:T(8,128)}, f32[8,256,512]{2,0,1:T(8,128)}) fusion(f32[8,256,512]{2,1,0:T(8,128)} %bitcast.194, f32[512]{0:T(512)S(1)} %get-tuple-element.101, f32[256,8]{1,0:T(8,128)S(1)} %copy.144, ...), kind=kOutput, calls=%fused_computation.38 | convolution fusion | flops 4320132608 | bytes 33590272 | tf_op jit(solution)/shard_map/dot_general | solution.py:22
  204.3 20.8 %shard_map.221 = bf16[4,2,256,256]{3,2,1,0:T(8,128)(2,1)S(1)} custom-call(f32[4,2,256,256]{3,2,1,0:T(8,128)S(1)} %fusion.36.part_ref), custom_call_target="tpu_custom_call" | custom-call | tf_op jit(solution)/shard_map/pallas_call | solution.py:575
  226.2 6.0 broadcast_add_fusion
  232.9 30.9 %shard_map.222 = (f32[256,8,512]{2,1,0:T(8,128)}, f32[256,16,8,512]{3,2,1,0:T(8,128)}, f32[16,8,512]{2,1,0:T(8,128)}) custom-call(f32[256,8,512]{2,1,0:T(8,128)} %get-tuple-element.116.dt_ref, f32[256,8,512]{2,1,0:T(8,128)} %get-tuple-element.115.dtm_ref, f32[256,8,512]{2,1,0:T(8,128)} %convert_element_type.205.x_ref, f32[256,8,32]{2,1,0:T(8,128)} %fusion.31.bc_ref, ...), custom_call_target="tpu_custom_call" | custom-call | tf_op jit(solution)/shard_map/pallas_call | solution.py:76
  263.8 68.5 %shard_map.223 = (f32[256,8,512]{2,1,0:T(8,128)}, f32[256,8,512]{2,1,0:T(8,128)}, f32[2048,128]{1,0:T(8,128)}, f32[16,8,512]{2,1,0:T(8,128)}) custom-call(f32[256,8,512]{2,1,0:T(8,128)} %get-tuple-element.116.dt_ref, f32[256,8,512]{2,1,0:T(8,128)} %get-tuple-element.115.dtm_ref, f32[256,8,512]{2,1,0:T(8,128)} %convert_element_type.205.x_ref, ...), custom_call_target="tpu_custom_call" | custom-call | tf_op jit(solution)/shard_map/pallas_call | solution.py:190
  332.3 14.5 %fusion.26 = (bf16[8,256,512]{2,0,1:T(8,128)(2,1)}, bf16[8,256,512]{2,0,1:T(8,128)(2,1)S(1)}, bf16[512,2048]{0,1:T(8,128)(2,1)}, f32[256,8,512]{2,1,0:T(8,128)}) fusion(f32[8,256,512]{2,0,1:T(8,128)} %get-tuple-element.130, f32[256,8,512]{2,1,0:T(8,128)} %get-tuple-element.33, bf16[256,8,512]{2,1,0:T(8,128)(2,1)} %copy-done.7, f32[512]{0:T(512)S(1)} %get-tuple-element.99, ...), kind=kLoop, calls=%fused_computation.63 | loop fusion | flops 26214400 | bytes 37752832 | tf_op jit(solution)/shard_map/transpose | solution.py:1086
  348.8 9.1 %convolution_convert_fusion.1 = bf16[512,2048]{1,0:T(8,128)(2,1)} fusion(bf16[2048,512]{1,0:T(8,128)(2,1)S(1)} %bitcast.203, bf16[2048,2048]{1,0:T(8,128)(2,1)} %all-gather.9.cloned.1.call-done), kind=kOutput, calls=%fused_computation.49 | convolution fusion | flops 4296015872 | bytes 12582912 | tf_op jit(solution)/shard_map/dot_general | solution.py:22
  358.0 41.4 %reduce-scatter.5.cloned.1.call-done = bf16[128,2048]{1,0:T(8,128)(2,1)} async-done(((bf16[512,2048]{1,0:T(8,128)(2,1)}), bf16[128,2048]{1,0:T(8,128)(2,1)}) %reduce-scatter.5.cloned.1.call-update) | async-done | bytes 524304 | tf_op jit(solution)/shard_map/reduce_scatter | solution.py:1181
  399.6 10.0 %convolution_convert_fusion = bf16[2048,2048]{1,0:T(8,128)(2,1)} fusion(bf16[2048,512]{1,0:T(8,128)(2,1)} %bitcast.204, bf16[512,2048]{1,0:T(8,128)(2,1)} %all-gather.7.cloned.1.call-done), kind=kOutput, calls=%fused_computation.2 | convolution fusion | flops 4299161600 | bytes 12582912 | tf_op jit(solution)/shard_map/dot_general | solution.py:22
  413.5 24.9 %shard_map.224 = bf16[4,2,256,256]{3,2,1,0:T(8,128)(2,1)S(1)} custom-call(f32[4,2,256,256]{3,2,1,0:T(8,128)S(1)} %bitcast.177), custom_call_target="tpu_custom_call" | custom-call | tf_op jit(solution)/shard_map/pallas_call | solution.py:575
  438.4 21.3 %multiply_reduce_fusion.1 = (bf16[512]{0:T(512)(128)(2,1)S(1)}, bf16[512]{0:T(512)(128)(2,1)S(1)}, bf16[512]{0:T(512)(128)(2,1)S(1)}, bf16[512]{0:T(512)(128)(2,...) fusion(f32[256,8,512]{2,1,0:T(8,128)} %fusion.19, ...), kind=kOutput, calls=%fused_computation.39 | convolution fusion | flops 363853312 | bytes 39459840 | tf_op jit(solution)/shard_map/dot_general | solution.py:22
  459.8 6.7 fusion.25
  478.9 4.0 copy.157
  485.6 4.1 copy.158
  493.8 12.6 %fusion.57 = f32[2048,2048]{1,0:T(8,128)} fusion(bf16[2048,512]{1,0:T(8,128)(2,1)} %bitcast.202, bf16[2048,512]{1,0:T(8,128)(2,1)} %bitcast.190), kind=kOutput, calls=%fused_computation.145 | convolution fusion | flops 4294967296 | bytes 20971520 | tf_op jit(solution)/shard_map/dot_general | solution.py:22
  506.4 15.0 %add_convert_fusion = bf16[2048,2048]{1,0:T(8,128)(2,1)} fusion(f32[2048,2048]{1,0:T(8,128)} %fusion.57, bf16[2048,512]{1,0:T(8,128)(2,1)} %bitcast.201, bf16[2048,512]{1,0:T(8,128)(2,1)} %bitcast.223), kind=kOutput, calls=%fused_computation | convolution fusion | flops 4303355904 | bytes 29360128 | tf_op jit(solution)/shard_map/dot_general | solution.py:22
  521.4 10.4 %bitcast_convert_fusion.1 = bf16[2048,512]{1,0:T(8,128)(2,1)} fusion(bf16[8,256,2048]{2,1,0:T(8,128)(2,1)} %copy-done.4, bf16[8,256,512]{2,0,1:T(8,128)(2,1)S(1)} %copy-done.9), kind=kOutput, calls=%fused_computation.21 | convolution fusion | flops 4296015872 | bytes 12582912 | tf_op jit(solution)/shard_map/dot_general | solution.py:22
  531.8 10.5 %bitcast_convert_fusion = bf16[2048,512]{1,0:T(8,128)(2,1)} fusion(bf16[8,256,2048]{2,1,0:T(8,128)(2,1)} %copy-done.4, bf16[8,256,512]{2,0,1:T(8,128)(2,1)S(1)} %copy-done.11), kind=kOutput, calls=%fused_computation.20 | convolution fusion | flops 4296015872 | bytes 12582912 | tf_op jit(solution)/shard_map/dot_general | solution.py:22
  542.4 154.3 %shard_map.225 = (bf16[256,2048]{1,0:T(8,128)(2,1)}, f32[128,8192]{1,0:T(8,128)}, bf16[2,128,384]{2,1,0:T(8,128)(2,1)}, f32[8,128]{1,0:T(8,128)}) custom-call(bf16[4,2,256,2048]{3,2,1,0:T(8,128)(2,1)} %bitcast.196, bf16[4,128,384]{2,1,0:T(8,128)(2,1)} %concatenate.37.small_ref, bf16[4,512,512]{2,1,0:T(8,128)(2,1)} %bitcast.199, ...), custom_call_target="tpu_custom_call" | custom-call | tf_op jit(solution)/shard_map/pallas_call | solution.py:943
  (159 shorter events, 69.1 us)
Async XLA Ops:
  7.2 128.7 %all-gather.7.cloned.1.call-start = ((), (), s32[]{:S(2)}) async-start(), calls=%async_computation.3 | async-start | bytes 2621440 | tf_op jit(solution)/shard_map/all_gather | solution.py:1076
  9.3 126.6 %all-gather.9.cloned.1.call-start = ((), (), s32[]{:S(2)}) async-start(), calls=%async_computation.5 | async-start | bytes 9437184 | tf_op jit(solution)/shard_map/all_gather | solution.py:1079
  10.0 166.9 %all-gather.5.cloned.1.call-start = ((), (), s32[]{:S(2)}) async-start(), calls=%async_computation.2 | async-start | bytes 2621440 | tf_op jit(solution)/shard_map/all_gather | solution.py:1072
  111.0 3.2 copy-start.4
  115.5 5.1 copy-start.6
  115.6 283.8 %reduce-scatter.5.cloned.1.call-start = ((), (), s32[]{:S(2)}) async-start(), calls=%async_computation.6 | async-start | bytes 2621440 | tf_op jit(solution)/shard_map/reduce_scatter | solution.py:1181
  146.4 30.5 %copy-start.22 = (f32[256,8]{1,0:T(8,128)S(1)}, f32[256,8]{1,0:T(8,128)}, u32[]{:S(2)}) copy-start(f32[256,8]{1,0:T(8,128)} %copy.142) | copy-start | bytes 24580
  357.9 348.5 %all-gather.11.cloned.1.call-start = ((), (), s32[]{:S(2)}) async-start(), calls=%async_computation.7 | async-start | bytes 1572864 | tf_op jit(solution)/shard_map/all_gather | solution.py:1186
  399.4 309.8 %reduce-scatter.3.cloned.1.call-start = ((), (), s32[]{:S(2)}) async-start(), calls=%async_computation.4 | async-start | bytes 9437184 | tf_op jit(solution)/shard_map/reduce_scatter | solution.py:1117
  409.6 3.8 copy-start.15
  466.5 5.1 copy-start.10
  466.5 3.1 copy-start.8
  469.6 9.0 %copy-start.21 = (f32[16,8,512]{2,1,0:T(8,128)S(1)}, f32[16,8,512]{2,1,0:T(8,128)}, u32[]{:S(2)}) copy-start(f32[16,8,512]{2,1,0:T(8,128)} %get-tuple-element.40) | copy-start | bytes 786436
  485.4 6.8 copy-start.16
  485.4 6.8 copy-start.17
  485.4 6.8 copy-start.18
  485.4 6.8 copy-start.19
  485.4 6.8 copy-start.20
  506.4 15.0 %copy-start.9 = (bf16[8,256,512]{2,0,1:T(8,128)(2,1)S(1)}, bf16[8,256,512]{2,0,1:T(8,128)(2,1)}, u32[]{:S(2)}) copy-start(bf16[8,256,512]{2,0,1:T(8,128)(2,1)} %get-tuple-element.119) | copy-start | bytes 6291460
  521.4 10.4 %copy-start.11 = (bf16[8,256,512]{2,0,1:T(8,128)(2,1)S(1)}, bf16[8,256,512]{2,0,1:T(8,128)(2,1)}, u32[]{:S(2)}) copy-start(bf16[8,256,512]{2,0,1:T(8,128)(2,1)} %copy-done.10) | copy-start | bytes 6291460
  696.7 12.5 %copy-start.3 = (bf16[256,2048]{1,0:T(8,128)(2,1)S(1)}, bf16[256,2048]{1,0:T(8,128)(2,1)}, u32[]{:S(2)}) copy-start(bf16[256,2048]{1,0:T(8,128)(2,1)} %tokens_ref.3) | copy-start | bytes 3145732
  696.7 15.2 %copy-start.14 = (bf16[256,2048]{1,0:T(8,128)(2,1)S(1)}, bf16[256,2048]{1,0:T(8,128)(2,1)}, u32[]{:S(2)}) copy-start(bf16[256,2048]{1,0:T(8,128)(2,1)} %get-tuple-element.150) | copy-start | bytes 3145732
  709.2 3.7 copy-start.12
  711.9 3.0 copy-start.1
  (14 other events, 27.9 us)
Sparse Core Ops, SparseCore 0:
  10.2 59.8 all-gather.6
  71.9 59.7 all-gather.8
  133.3 43.6 all-gather.4
  358.0 41.2 reduce-scatter.4
  400.8 25.0 all-gather.10
  429.6 73.9 reduce-scatter.2

commit v2 on v1

--- a/solution.py
+++ b/solution.py
@@ -32,6 +32,10 @@
 
 def dot_nt(a, b):
     return dot(a, b, ((1,), (1,)))
+
+
+def busy(micros):
+    return pl.CostEstimate(flops=micros * 10**9, bytes_accessed=micros * 10**6, transcendentals=0)
 
 
 def fwd_kernel(states, dt_ref, dtm_ref, x_ref, bc_ref, rate_ref, y_ref, hist_ref, last_ref, h_ref):
@@ -90,6 +94,7 @@
             jax.ShapeDtypeStruct((states, seqs, width), F32),
         ],
         scratch_shapes=[pltpu.VMEM((states, seqs, width), F32)],
+        cost_estimate=busy(30),
         compiler_params=pltpu.CompilerParams(vmem_limit_bytes=56 << 20),
     )(dt, dtm, x, bc, rate)
 
@@ -219,6 +224,7 @@
             pltpu.VMEM((STEPS * seqs, width // 128 * span), BF16),
             pltpu.VMEM((STEPS * seqs, width // 128 * span), BF16),
         ],
+        cost_estimate=busy(70),
         compiler_params=pltpu.CompilerParams(vmem_limit_bytes=60 << 20),
     )(dt, dtm, x, ds, bc, rate, hist, last, ones)
 
@@ -289,22 +295,154 @@
     return out
 
 
-def start_kernel(
+def z_line(z, z_size, pieces, sems):
+    up_s, up_r, down_s, down_r = sems
+
+    def up(k):
+        return [
+            remote(p(z - k), p(z - k), up_s.at[k, j], up_r.at[k, j], {"z": z + 1})
+            for j, p in enumerate(pieces)
+        ]
+
+    def down(k):
+        return [
+            remote(p(z + k), p(z + k), down_s.at[k, j], down_r.at[k, j], {"z": z - 1})
+            for j, p in enumerate(pieces)
+        ]
+
+    def start(k):
+        @pl.when((z < z_size - 1) & (z >= k))
+        def _():
+            for copy in up(k):
+                copy.start()
+
+        @pl.when((z > 0) & (z + k < z_size))
+        def _():
+            for copy in down(k):
+                copy.start()
+
+    def arrive(k):
+        @pl.when(z > k)
+        def _():
+            for copy in up(k):
+                copy.wait_recv()
+
+        @pl.when(z + k < z_size - 1)
+        def _():
+            for copy in down(k):
+                copy.wait_recv()
+
+    def sent(k):
+        @pl.when((z < z_size - 1) & (z >= k))
+        def _():
+            for copy in up(k):
+                copy.wait_send()
+
+        @pl.when((z > 0) & (z + k < z_size))
+        def _():
+            for copy in down(k):
+                copy.wait_send()
+
+    return start, arrive, sent
+
+
+class Ring:
+    def __init__(self, me, blocks, own, ring_send, ring_recv, sib_send, sib_recv):
+        self.me, self.blocks, self.own = me, blocks, own
+        self.sems = ring_send, ring_recv, sib_send, sib_recv
+        self.at = ring_at(me["x"], me["y"])
+        self.step = 1 + 2 * me["c"]
+        nx, ny = ring_chip((self.at + self.step) % RING)
+        self.following = {"x": nx, "y": ny}
+        self.sibling = {"c": 1 - me["c"]}
+        self.half = blocks.shape[1] // 2
+
+    def slot(self, k):
+        ox, oy = ring_chip((self.at + (RING - self.step) * k) % RING)
+        return ox * 4 + oy * 2 + self.me["c"]
+
+    def hop(self, k):
+        out = []
+        for p in range(2):
+            rows = pl.ds(p * self.half, self.half)
+            dst = self.blocks.at[self.slot(k), rows]
+            src = self.own.at[rows] if k == 0 and self.own is not None else dst
+            out.append(remote(src, dst, self.sems[0].at[k, p], self.sems[1].at[k, p], self.following))
+        return out
+
+    def cross(self, k):
+        dst = self.blocks.at[self.slot(k)]
+        src = self.own if k == 0 and self.own is not None else dst
+        return remote(src, dst, self.sems[2].at[k], self.sems[3].at[k], self.sibling)
+
+    def start(self, k):
+        if k < RING - 1:
+            for copy in self.hop(k):
+                copy.start()
+        self.cross(k).start()
+
+    def arrive(self, k):
+        for copy in self.hop(k):
+            copy.wait_recv()
+
+    def sent(self, k):
+        if k < RING - 1:
+            for copy in self.hop(k):
+                copy.wait_send()
+        self.cross(k).wait()
+
+
+def softplus(v):
+    e = jnp.exp(-jnp.abs(v))
+    small = e * (1.0 - e * (0.5 - e * (1.0 / 3.0)))
+    return jnp.maximum(v, 0.0) + jnp.where(e < 1e-3, small, jnp.log(1.0 + e))
+
+
+def front_kernel(
     z_size,
+    taps,
+    rank,
     tokens_ref,
     gain_ref,
     ids_ref,
+    rows_ref,
+    cot_ref,
     conv_ref,
     gate_ref,
-    small_ref,
+    out_ref,
+    mats_ref,
+    normed_hbm,
+    cot_all,
+    conv_hbm,
+    gate_all,
+    out_all,
+    mats_hbm,
+    keep_hbm,
+    cin_hbm,
+    x_hbm,
+    dt_hbm,
+    pre_hbm,
+    params,
+    gain_all,
+    selection,
     normed_all,
-    conv_all,
-    gate_all,
-    small_all,
+    conv_w,
+    mats,
+    rows_all,
+    gain_got,
     ids_all,
-    gain_all,
-    normed_ref,
-    gain_got,
+    proj,
+    cin,
+    xs,
+    picked,
+    part,
+    dts,
+    pres,
+    keep,
+    first,
+    from_sib,
+    stage,
+    got,
     local_sem,
     gain_send,
     gain_recv,
@@ -318,10 +456,26 @@
     ring_recv,
     sib_send,
     sib_recv,
-    up_send,
-    up_recv,
-    down_send,
-    down_recv,
+    cot_ring_send,
+    cot_ring_recv,
+    cot_sib_send,
+    cot_sib_recv,
+    a_us,
+    a_ur,
+    a_ds,
+    a_dr,
+    b_us,
+    b_ur,
+    b_ds,
+    b_dr,
+    sw_s,
+    sw_r,
+    rs_s,
+    rs_r,
+    ag_s,
+    ag_r,
+    fw_s,
+    fw_r,
 ):
     me = place()
     x, y, z, c = me["x"], me["y"], me["z"], me["c"]
@@ -329,15 +483,34 @@
     share = z * 4 + y * 2 + c
     corner = y * 2 + c
     seq = x * 4 + y * 2 + c
+    sibling = {"c": 1 - c}
+    length, width = tokens_ref.shape
+    chans = conv_ref.shape[2]
+    rows_in = conv_ref.shape[1]
+    half = mats_ref.shape[0]
+    hops = z_size - 1
     greet(plane_others(me) + z_only(me, shares))
 
-    swaps = []
-    for k in range(1, 4):
-        to = (corner + k) % 4
-        device = {"y": to // 2, "c": to % 2}
-        swaps.append(
-            remote(conv_ref.at[to], conv_all.at[z, corner], conv_send.at[k - 1], conv_recv.at[k - 1], device)
-        )
+    def rows_at(ref, index, count):
+        return ref.at[pl.ds(pl.multiple_of(index * count, count), count)]
+
+    def corner_sends(src, dst, send, recv):
+        out = []
+        for k in range(1, 4):
+            to = (corner + k) % 4
+            out.append(
+                remote(
+                    src.at[to],
+                    rows_at(dst, share, rows_in),
+                    send.at[k - 1],
+                    recv.at[k - 1],
+                    {"y": to // 2, "c": to % 2},
+                )
+            )
+        return out
+
+    swaps = corner_sends(conv_ref, conv_w, conv_send, conv_recv)
+    gates = corner_sends(gate_ref, gate_all, gate_send, gate_recv)
     for copy in swaps:
         copy.start()
     gains = [
@@ -346,22 +519,24 @@
     ]
     for copy in gains:
         copy.start()
-    own = [
-        pltpu.make_async_copy(conv_ref.at[corner], conv_all.at[z, corner], local_sem.at[0]),
-        pltpu.make_async_copy(small_ref, small_all.at[z], local_sem.at[1]),
-        pltpu.make_async_copy(gate_ref.at[corner], gate_all.at[corner], local_sem.at[2]),
+    locals_ = [
+        pltpu.make_async_copy(conv_ref.at[corner], rows_at(conv_w, share, rows_in), local_sem.at[0]),
+        pltpu.make_async_copy(mats_ref, rows_at(mats, z, half), local_sem.at[1]),
+        pltpu.make_async_copy(gate_ref.at[corner], rows_at(gate_all, share, rows_in), local_sem.at[2]),
+        pltpu.make_async_copy(out_ref, rows_at(out_all, z, half), local_sem.at[3]),
+        pltpu.make_async_copy(cot_ref, cot_all.at[seq], local_sem.at[4]),
     ]
-    for copy in own:
+    for copy in locals_:
         copy.start()
-    others = plane_others(me)
     ids_copies = [
         remote(ids_ref, ids_all.at[seq], ids_send.at[k], ids_recv.at[k], device)
-        for k, device in enumerate(others)
+        for k, device in enumerate(plane_others(me))
     ]
     for copy in ids_copies:
         copy.start()
     ids_all[seq] = ids_ref[...]
     gain_got[share] = gain_ref[...]
+    rows_all[z] = rows_ref[...]
 
     values = tokens_ref[...].astype(F32)
     rstd = lax.rsqrt(jnp.mean(values * values, axis=-1, keepdims=True) + epsilon)
@@ -370,153 +545,278 @@
     piece = gain_ref.shape[1]
     for f in range(shares):
         cols = pl.ds(f * piece, piece)
-        part = tokens_ref[:, cols].astype(F32) * rstd * gain_got[f, 0:1, :]
-        normed_ref[:, cols] = part.astype(BF16)
+        normed = tokens_ref[:, cols].astype(F32) * rstd * gain_got[f, 0:1, :]
+        normed_all[seq, :, cols] = normed.astype(BF16)
     gain_all[...] = gain_got[...]
 
-    at = ring_at(x, y)
-    step = 1 + 2 * c
-    nx, ny = ring_chip((at + step) % RING)
-    following = {"x": nx, "y": ny}
-    sibling = {"c": 1 - c}
-
-    def slot(k):
-        ox, oy = ring_chip((at + (RING - step) * k) % RING)
-        return ox * 4 + oy * 2 + c
-
-    def ring(k):
-        src = normed_ref if k == 0 else normed_all.at[slot(k)]
-        return remote(src, normed_all.at[slot(k)], ring_send.at[k], ring_recv.at[k], following)
-
-    def sib(k):
-        src = normed_ref if k == 0 else normed_all.at[slot(k)]
-        return remote(src, normed_all.at[slot(k)], sib_send.at[k], sib_recv.at[k], sibling)
-
-    keep = pltpu.make_async_copy(normed_ref, normed_all.at[seq], local_sem.at[3])
-    keep.start()
-    ring(0).start()
-    sib(0).start()
-
+    ring = Ring(me, normed_all, None, ring_send, ring_recv, sib_send, sib_recv)
+    cot_ring = Ring(me, cot_all, cot_ref, cot_ring_send, cot_ring_recv, cot_sib_send, cot_sib_recv)
+    ring.start(0)
     for copy in swaps:
         copy.wait()
-    for copy in own:
+    for copy in locals_:
         copy.wait()
-
-    def upward(k, j):
-        ref = (conv_all, small_all)[j].at[z - k]
-        return remote(ref, ref, up_send.at[k, j], up_recv.at[k, j], {"z": z + 1})
-
-    def downward(k, j):
-        ref = (conv_all, small_all)[j].at[z + k]
-        return remote(ref, ref, down_send.at[k, j], down_recv.at[k, j], {"z": z - 1})
-
-    def send_up(k):
-        @pl.when((z < z_size - 1) & (z >= k))
-        def _():
-            upward(k, 0).start()
-            upward(k, 1).start()
-
-    def send_down(k):
-        @pl.when((z > 0) & (z + k < z_size))
-        def _():
-            downward(k, 0).start()
-            downward(k, 1).start()
-
-    send_up(0)
-    send_down(0)
-    gates = []
-    for k in range(1, 4):
-        to = (corner + k) % 4
-        device = {"y": to // 2, "c": to % 2}
-        gates.append(
-            remote(gate_ref.at[to], gate_all.at[corner], gate_send.at[k - 1], gate_recv.at[k - 1], device)
-        )
+    a_start, a_arrive, a_sent = z_line(
+        z,
+        z_size,
+        [
+            lambda k: rows_at(conv_w, k, 4 * rows_in),
+            lambda k: rows_at(mats, k, half),
+            lambda k: rows_all.at[k],
+        ],
+        (a_us, a_ur, a_ds, a_dr),
+    )
+    b_start, b_arrive, b_sent = z_line(
+        z,
+        z_size,
+        [lambda k: rows_at(gate_all, k, 4 * rows_in), lambda k: rows_at(out_all, k, half)],
+        (b_us, b_ur, b_ds, b_dr),
+    )
+    a_start(0)
     for copy in gates:
         copy.start()
-    for k in range(max(z_size - 1, RING - 1)):
-        if k < z_size - 1:
-            @pl.when(z > k)
-            def _():
-                upward(k, 0).wait_recv()
-                upward(k, 1).wait_recv()
-
-            send_up(k + 1)
-
-            @pl.when(z + k < z_size - 1)
-            def _():
-                downward(k, 0).wait_recv()
-                downward(k, 1).wait_recv()
-
-            send_down(k + 1)
+
+    for copy in ids_copies:
+        copy.wait()
+    ids = jnp.concatenate([ids_all[s, 0:1, :] for s in range(8)], axis=0).astype(F32)
+    before = pltpu.roll(ids, 1, 1)
+    lane = lax.broadcasted_iota(jnp.int32, ids.shape, 1)
+    same = jnp.where((ids == before) & (lane > 0), 1.0, 0.0)
+    for t in range(length):
+        keep[t] = jnp.broadcast_to(same[:, t : t + 1], (8, 128))
+    keep_copy = pltpu.make_async_copy(keep, keep_hbm, local_sem.at[5])
+    keep_copy.start()
+
+    for k in range(max(hops, RING - 1)):
+        if k < hops:
+            a_arrive(k)
+            if k + 1 < hops:
+                a_start(k + 1)
         if k < RING - 1:
-            ring(k).wait_recv()
-            if k + 1 < RING - 1:
-                ring(k + 1).start()
-            sib(k + 1).start()
-
-    for k in range(z_size - 1):
-        @pl.when((z < z_size - 1) & (z >= k))
-        def _():
-            upward(k, 0).wait_send()
-            upward(k, 1).wait_send()
-
-        @pl.when((z > 0) & (z + k < z_size))
-        def _():
-            downward(k, 0).wait_send()
-            downward(k, 1).wait_send()
-
-    for k in range(RING - 1):
-        ring(k).wait_send()
+            ring.arrive(k)
+            ring.start(k + 1)
+        if k == RING - 2:
+            cot_ring.start(0)
+    for copy in gates:
+        copy.wait()
+    b_start(0)
     for k in range(RING):
-        sib(k).wait()
-    for copy in gates + ids_copies + [keep]:
+        ring.sent(k)
+    outs = [
+        pltpu.make_async_copy(normed_all, normed_hbm, local_sem.at[6]),
+        pltpu.make_async_copy(conv_w, conv_hbm, local_sem.at[7]),
+        pltpu.make_async_copy(mats, mats_hbm, local_sem.at[8]),
+    ]
+    for copy in outs:
+        copy.start()
+    for zz in range(z_size):
+        params[:, zz * half : (zz + 1) * half] = rows_all[zz].astype(F32)
+
+    def project(s, carry):
+        proj[s] = dot_nn(normed_all[s], conv_w[...])
+        return carry
+
+    lax.fori_loop(0, 8, project, 0)
+
+    cin[0:3] = jnp.zeros((3, 8, chans), F32)
+    block = 32
+    fine = 4
+
+    def turn(i, carry):
+        t0 = pl.multiple_of(i * block, block)
+        cin[pl.ds(3 + t0, block)] = jnp.swapaxes(proj[:, pl.ds(t0, block), :], 0, 1)
+        return carry
+
+    lax.fori_loop(0, length // block, turn, 0)
+
+    def convolve(i, carry):
+        t0 = i * fine
+        for g in range(chans // 128):
+            lanes = pl.ds(g * 128, 128)
+            tap = [jnp.broadcast_to(params[taps - 1 - j : taps - j, lanes], (8, 128)) for j in range(taps)]
+            offset = jnp.broadcast_to(params[taps : taps + 1, lanes], (8, 128))
+            chosen = []
+            for j in range(fine):
+                t = t0 + j
+                total = tap[3] * cin[t, :, lanes] * keep[jnp.maximum(t - 2, 0)]
+                total = (total + tap[2] * cin[t + 1, :, lanes]) * keep[jnp.maximum(t - 1, 0)]
+                total = (total + tap[1] * cin[t + 2, :, lanes]) * keep[t]
+                v = total + tap[0] * cin[t + 3, :, lanes] + offset
+                chosen.append((v / (1.0 + jnp.exp(-v))).astype(BF16))
+                xs[t, :, lanes] = chosen[-1].astype(F32)
+            rows = pl.ds(pl.multiple_of(t0 * 8, fine * 8), fine * 8)
+            picked[rows, lanes] = jnp.concatenate(chosen, axis=0)
+        return carry
+
+    lax.fori_loop(0, length // fine, convolve, 0)
+    outs += [
+        pltpu.make_async_copy(cin.at[pl.ds(3, length)], cin_hbm, local_sem.at[9]),
+        pltpu.make_async_copy(xs, x_hbm, local_sem.at[10]),
+    ]
+    for copy in outs[3:]:
+        copy.start()
+
+    wide = part.shape[3]
+
+    def select(b, carry):
+        rows = pl.ds(pl.multiple_of(b * length, length), length)
+        part[b // 2, b % 2] = dot_nn(picked[rows, :], mats[:, :wide])
+        return carry
+
+    lax.fori_loop(0, 8, select, 0)
+    first[...] = part[:, 1 - c].astype(BF16)
+    swap = remote(first, from_sib, sw_s.at[0], sw_r.at[0], sibling)
+    swap.start()
+    swap.wait()
+    mine = x * 2 + y
+    chips = [((x + d // 2) % 2, (y + d % 2) % 2) for d in (1, 2, 3)]
+    sends = []
+    for k in (2, 1, 0):
+        ox, oy = chips[k]
+        j = ox * 2 + oy
+        stage[k] = (part[j, c] + from_sib[j].astype(F32)).astype(BF16)
+        copy = remote(stage.at[k], got.at[k], rs_s.at[k], rs_r.at[k], {"x": ox, "y": oy})
+        copy.start()
+        sends.append(copy)
+    total = part[mine, c] + from_sib[mine].astype(F32)
+    for copy in sends:
         copy.wait()
-
-
-def start_gathers(z_size, tokens, gain, ids, conv, gate, small):
+    for k in range(3):
+        total = total + got[k].astype(F32)
+    selection[mine, c] = total.astype(BF16)
+    here = selection.at[mine, c]
+    spreads = []
+    for k in (2, 1, 0):
+        ox, oy = chips[k]
+        copy = remote(here, here, ag_s.at[k], ag_r.at[k], {"x": ox, "y": oy})
+        copy.start()
+        spreads.append((k, copy))
+    forwards = [remote(here, here, fw_s.at[3], fw_r.at[3], sibling)]
+    forwards[0].start()
+    if hops > 1:
+        b_arrive(0)
+        b_start(1)
+    cot_ring.arrive(0)
+    cot_ring.start(1)
+    for k, copy in reversed(spreads):
+        copy.wait_recv()
+        ox, oy = chips[k]
+        there = selection.at[ox * 2 + oy, c]
+        forwards.append(remote(there, there, fw_s.at[k], fw_r.at[k], sibling))
+        forwards[-1].start()
+    for _, copy in spreads:
+        copy.wait_send()
+    for copy in forwards:
+        copy.wait()
+
+    bias = params[taps + 1 : taps + 2, :]
+
+    def steps(i, carry):
+        rows = 64
+        per = length // rows
+        b = i // per
+        at = pl.ds(pl.multiple_of((i % per) * rows, rows), rows)
+        v = dot_nt(selection[b // 2, b % 2, at, :rank], mats[:, wide : wide + rank]) + bias
+        t = pl.ds(i * (rows // 8), rows // 8)
+        pres[t] = v.reshape(rows // 8, 8, chans)
+        dts[t] = softplus(v).reshape(rows // 8, 8, chans)
+        return carry
+
+    lax.fori_loop(0, length * 8 // 64, steps, 0)
+    outs += [
+        pltpu.make_async_copy(dts, dt_hbm, local_sem.at[11]),
+        pltpu.make_async_copy(pres, pre_hbm, local_sem.at[12]),
+    ]
+    for copy in outs[5:]:
+        copy.start()
+
+    cot_ring.arrive(1)
+    cot_ring.start(2)
+    for k in range(1 if hops > 1 else 0, hops):
+        b_arrive(k)
+        if k + 1 < hops:
+            b_start(k + 1)
+    cot_ring.arrive(2)
+    cot_ring.start(3)
+    for k in range(RING):
+        cot_ring.sent(k)
+    for k in range(hops):
+        a_sent(k)
+        b_sent(k)
+    for copy in outs + [keep_copy]:
+        copy.wait()
+
+
+def front(z_size, taps, rank, tokens, gain, ids, rows, cot, conv, gate, out, mats):
     length, width = tokens.shape
     shares = z_size * 4
+    chans = conv.shape[2]
+    wide = mats.shape[1] - rank
     any_space = pl.BlockSpec(memory_space=pl.ANY)
     vmem = pl.BlockSpec(memory_space=pltpu.VMEM)
     dma = pltpu.SemaphoreType.DMA
-    hops = max(z_size - 1, 1)
+    hops = z_size - 1
+    shape = jax.ShapeDtypeStruct
+    everyone = (8,) + tokens.shape
+    per_token = (length, 8, chans)
+    block = (length, wide)
     return pl.pallas_call(
-        functools.partial(start_kernel, z_size),
-        in_specs=[vmem, vmem, vmem, any_space, any_space, any_space],
-        out_specs=[any_space, any_space, any_space, any_space, vmem, vmem],
+        functools.partial(front_kernel, z_size, taps, rank),
+        in_specs=[vmem] * 8 + [any_space],
+        out_specs=[any_space] * 11 + [vmem] * 3,
         out_shape=[
-            jax.ShapeDtypeStruct((8,) + tokens.shape, BF16),
-            jax.ShapeDtypeStruct((z_size,) + conv.shape, BF16),
-            jax.ShapeDtypeStruct(gate.shape, BF16),
-            jax.ShapeDtypeStruct((z_size,) + small.shape, BF16),
-            jax.ShapeDtypeStruct((8,) + ids.shape, ids.dtype),
-            jax.ShapeDtypeStruct((shares,) + gain.shape, F32),
+            shape(everyone, BF16),
+            shape(everyone, BF16),
+            shape((width, chans), BF16),
+            shape((width, chans), BF16),
+            shape((chans, width), BF16),
+            shape((chans, mats.shape[1]), BF16),
+            shape((length, 8, 128), F32),
+            shape(per_token, F32),
+            shape(per_token, F32),
+            shape(per_token, F32),
+            shape(per_token, F32),
+            shape((rows.shape[0], chans), F32),
+            shape((shares,) + gain.shape, F32),
+            shape((4, 2) + block, BF16),
         ],
         scratch_shapes=[
-            pltpu.VMEM(tokens.shape, BF16),
+            pltpu.VMEM(everyone, BF16),
+            pltpu.VMEM((width, chans), BF16),
+            pltpu.VMEM((chans, mats.shape[1]), BF16),
+            pltpu.VMEM((z_size,) + rows.shape, BF16),
             pltpu.VMEM((shares,) + gain.shape, F32),
-            dma((4,)),
+            pltpu.VMEM((8,) + ids.shape, ids.dtype),
+            pltpu.VMEM((8, length, chans), F32),
+            pltpu.VMEM((length + 3, 8, chans), F32),
+            pltpu.VMEM(per_token, F32),
+            pltpu.VMEM((length * 8, chans), BF16),
+            pltpu.VMEM((4, 2) + block, F32),
+            pltpu.VMEM(per_token, F32),
+            pltpu.VMEM(per_token, F32),
+            pltpu.VMEM((length, 8, 128), F32),
+            pltpu.VMEM((4,) + block, BF16),
+            pltpu.VMEM((4,) + block, BF16),
+            pltpu.VMEM((3,) + block, BF16),
+            pltpu.VMEM((3,) + block, BF16),
+            dma((13,)),
             dma((shares - 1,)),
             dma((shares - 1,)),
             dma((7,)),
             dma((7,)),
-            dma((3,)),
-            dma((3,)),
-            dma((3,)),
-            dma((3,)),
-            dma((RING - 1,)),
-            dma((RING - 1,)),
-            dma((RING,)),
-            dma((RING,)),
-            dma((hops, 2)),
-            dma((hops, 2)),
-            dma((hops, 2)),
-            dma((hops, 2)),
-        ],
+        ]
+        + [dma((3,))] * 4
+        + [dma((RING - 1, 2)), dma((RING - 1, 2)), dma((RING,)), dma((RING,))] * 2
+        + [dma((hops, 3))] * 4
+        + [dma((hops, 2))] * 4
+        + [dma((1,))] * 2
+        + [dma((3,))] * 4
+        + [dma((4,))] * 2,
+        cost_estimate=busy(120),
         compiler_params=pltpu.CompilerParams(
-            collective_id=0, has_side_effects=True, vmem_limit_bytes=40 << 20
+            collective_id=0, has_side_effects=True, vmem_limit_bytes=60 << 20
         ),
-    )(tokens, gain, ids, conv, gate, small)
+    )(tokens, gain, ids, rows, cot, conv, gate, out, mats)
 
 
 def total_kernel(part_ref, out_ref, first, from_sib, stage, got, sib_s, sib_r, rs_s, rs_r, ag_s, ag_r, fw_s, fw_r):
@@ -591,6 +891,7 @@
             dma((4,)),
             dma((4,)),
         ],
+        cost_estimate=busy(20),
         compiler_params=pltpu.CompilerParams(
             collective_id=collective_id, has_side_effects=True, vmem_limit_bytes=40 << 20
         ),
@@ -732,30 +1033,33 @@
             down_stages[h].at[k], downs[h].at[k], down_send.at[k, h], down_recv.at[k, h], {"z": z - 1}
         )
 
-    def line(k, h):
+    def line(tau, h):
+        k = tau - z
         high = z_size - 1 - k
 
-        @pl.when((z < high) & (z > 0))
+        @pl.when((k >= 0) & (z < high) & (z > 0))
         def _():
             up_copy(k, h).wait_recv()
             add_rows(up_stages[h].at[k], [owns[h].at[high], ups[h].at[k]], blocks[h])
             up_copy(k, h).start()
 
-        @pl.when((z < high) & (z == 0))
+        @pl.when((k >= 0) & (z < high) & (z == 0))
         def _():
             add_rows(up_stages[h].at[k], [owns[h].at[high]], blocks[h])
             up_copy(k, h).start()
 
-        @pl.when((z > k) & (z < z_size - 1))
+        m = tau - (z_size - 1 - z)
+
+        @pl.when((m >= 0) & (z > m) & (z < z_size - 1))
         def _():
-            down_copy(k, h).wait_recv()
-            add_rows(down_stages[h].at[k], [owns[h].at[k], downs[h].at[k]], blocks[h])
-            down_copy(k, h).start()
-
-        @pl.when((z > k) & (z == z_size - 1))
+            down_copy(m, h).wait_recv()
+            add_rows(down_stages[h].at[m], [owns[h].at[m], downs[h].at[m]], blocks[h])
+            down_copy(m, h).start()
+
+        @pl.when((m >= 0) & (z > m) & (z == z_size - 1))
         def _():
-            add_rows(down_stages[h].at[k], [owns[h].at[k]], blocks[h])
-            down_copy(k, h).start()
+            add_rows(down_stages[h].at[m], [owns[h].at[m]], blocks[h])
+            down_copy(m, h).start()
 
     def settle(h, dst):
         low = z
@@ -835,23 +1139,19 @@
     for copy in locals_:
         copy.wait()
     hops = z_size - 1
+    ring_step(0)
     for h in range(3):
         line(0, h)
-    ring_step(0)
-    line(1, 0)
-    line(1, 1)
     ring_step(1)
-    line(1, 2)
     ring_step(2)
-    line(2, 0)
-    line(2, 1)
+    for h in range(3):
+        line(1, h)
     ring_end()
     for copy in gains:
         copy.start()
-    line(2, 2)
-    for k in range(3, hops):
+    for tau in range(2, hops):
         for h in range(3):
-            line(k, h)
+            line(tau, h)
 
     settle(0, small_out.at[x])
     small_x = remote(small_out.at[x], small_out.at[x], x_send.at[0], x_recv.at[0], over_x)
@@ -987,6 +1287,7 @@
             dma((shares - 1,)),
             dma((shares - 1,)),
         ],
+        cost_estimate=busy(100),
         compiler_params=pltpu.CompilerParams(
             collective_id=3, has_side_effects=True, vmem_limit_bytes=60 << 20
         ),
@@ -1045,18 +1346,21 @@
     def parts(v):
         return [v[:, e - n : e] for e, n in zip(ends, cuts)]
 
-    small = jnp.concatenate(
+    spare = -(rank + 2 * states) % 128
+    wide = rank + 2 * states + spare
+    vectors = jnp.concatenate(
         [
             own_half(conv_taps),
             own_half(conv_offset)[:, None],
             own_half(step_bias)[:, None],
             own_half(skip_gain)[:, None],
             own_half(decay_log),
-            own_half(select_weight),
-            own_half(step_weight),
-            jnp.zeros((half, room), BF16),
         ],
         axis=1,
+    ).T
+    vectors = jnp.pad(vectors, ((0, -vectors.shape[0] % 32), (0, 0)))
+    mats = jnp.concatenate(
+        [jnp.pad(own_half(select_weight), ((0, 0), (0, spare))), own_half(step_weight)], axis=1
     )
     picked = lax.dynamic_index_in_dim(
         in_weight.reshape(in_rows, 2, z_size, 4, 2, half), x_at, 4, keepdims=False
@@ -1064,19 +1368,43 @@
     packed = picked.transpose(1, 3, 0, 2, 4).reshape(2, 4, in_rows, chans)
     gain_tile = jnp.broadcast_to(norm_gain.astype(F32)[None, :], (8, norm_gain.shape[0]))
     ids_tile = jnp.broadcast_to(doc_ids, (8, length))
-    all_normed, w_conv, gate_slab, small_all, ids, gains = start_gathers(
-        z_size, tokens, gain_tile, ids_tile, packed[0], packed[1], small
+    (
+        all_normed,
+        all_cot,
+        w_conv,
+        w_gate,
+        w_out,
+        w_mats,
+        keep,
+        conv_in,
+        x,
+        dt,
+        pre,
+        vectors,
+        gains,
+        selection,
+    ) = front(
+        z_size,
+        taps,
+        rank,
+        tokens,
+        gain_tile,
+        ids_tile,
+        vectors,
+        cotangent,
+        packed[0],
+        packed[1],
+        own_half(out_weight),
+        mats,
     )
     all_normed = all_normed.reshape(-1, width)
-    w_conv = w_conv.reshape(-1, chans)
-    w_gate = lax.all_gather(gate_slab, "z", axis=0, tiled=True).reshape(-1, chans)
-    w_taps, w_offset, w_bias, w_skip, w_decay, w_select, w_step = parts(
-        small_all.reshape(chans, -1)
-    )
-    w_out = lax.all_gather(own_half(out_weight), "z", axis=0, tiled=True)
+    all_cot = all_cot.reshape(-1, width)
+    w_select = w_mats[:, : rank + 2 * states]
+    w_step = w_mats[:, wide:]
+    tap = [vectors[taps - 1 - j] for j in range(taps)]
+    skip = vectors[taps + 2]
+    rates = -jnp.exp(vectors[taps + 3 : taps + 3 + states])
     gain = gains[:, 0, :].reshape(1, width)
-    ids = ids[:, 0, :].T
-    all_cot = lax.all_gather(cotangent, PLANE, axis=0, tiled=True)
     residual = tokens.astype(F32)
 
     def time_major(v):
@@ -1085,43 +1413,41 @@
     def seq_major(v):
         return v.reshape(length, seqs, -1).swapaxes(0, 1).reshape(seqs * length, -1)
 
-    conv_in = time_major(dot_nn(all_normed, w_conv))
     gate_in = time_major(dot_nn(all_normed, w_gate))
-    same = [
-        (shift_down(ids + 1, j) == ids + 1).astype(F32)[:, :, None] for j in range(taps)
-    ]
-    tap = [w_taps[:, taps - 1 - j].astype(F32) for j in range(taps)]
-    conv_out = w_offset[:, 0].astype(F32) + sum(
-        shift_down(conv_in, j) * same[j] * tap[j] for j in range(taps)
-    )
-    selected_f, conv_slope = silu_and_slope(conv_out)
-    selected = selected_f.astype(BF16)
-    x = selected.astype(F32)
+    keep1 = keep[:, :, :1]
+    same = [None, keep1]
+    for j in range(2, taps):
+        same.append(same[-1] * shift_down(keep1, j - 1))
+    conv_out = vectors[taps] + conv_in * tap[0]
+    for j in range(1, taps):
+        conv_out = conv_out + shift_down(conv_in, j) * same[j] * tap[j]
+    conv_slope = silu_and_slope(conv_out)[1]
+    selected = x.astype(BF16)
     flat = lambda v: v.reshape(length * seqs, -1)
-    spare = -(rank + 2 * states) % 128
-    wide_select = jnp.pad(w_select, ((0, 0), (0, spare)))
-    selection = plane_total(dot_nn(flat(selected), wide_select), 1)
+    selection = selection.reshape(length * seqs, wide)
     rank_in = selection[:, :rank]
     bc = selection[:, rank : rank + 2 * states].astype(F32).reshape(length, seqs, 2 * states)
-    pre = dot_nt(rank_in, w_step).reshape(length, seqs, chans) + w_bias[:, 0].astype(F32)
-    dt = jax.nn.softplus(pre)
-    dtm = dt + (1.0 - same[1]) * BIG
-    rates = -jnp.exp(w_decay.astype(F32)).T
+    dtm = dt + (1.0 - keep1) * BIG
     rate2 = jnp.broadcast_to((rates * LOG2E)[:, None, :], (states, seqs, chans))
     y, hist, last = scan_forward(dt, dtm, x, bc, rate2)
-    skip = w_skip[:, 0].astype(F32)
     scanned = y + skip * x
     gate, gate_slope = silu_and_slope(gate_in)
     gated = seq_major((scanned * gate).astype(BF16))
     out_part = dot_nn(gated, w_out).astype(BF16)
-    layer_sum = lax.psum_scatter(out_part, PLANE, scatter_dimension=0, tiled=True)
-    layer_out = (residual + layer_sum.astype(F32)).astype(BF16)
+
+    def shifted(v, j):
+        return shift_down(v, j) * same[j] if j else v
 
     grad_out = dot_tn(gated, all_cot).astype(BF16)
     back_gated = time_major(dot_nt(all_cot, w_out).astype(BF16)).astype(F32)
     back_scan = back_gated * gate
     back_gate_in = back_gated * scanned * gate_slope
+    back_scan, out_part, grad_out = lax.optimization_barrier((back_scan, out_part, grad_out))
+    layer_sum = lax.psum_scatter(out_part, PLANE, scatter_dimension=0, tiled=True)
+    layer_out = (residual + layer_sum.astype(F32)).astype(BF16)
     s1, s2, back_bc, da = scan_backward(dt, dtm, x, back_scan, bc, rate2, hist, last)
+    s1, grad_out = lax.optimization_barrier((s1, grad_out))
+    own_out = lax.psum_scatter(grad_out, "z", scatter_dimension=0, tiled=True)
     back_steps = s1 * (1.0 / LOG2E) + x * s2
     back_x = dt * s2 + skip * back_scan
     grad_decay = da.sum(1).T * rates.T
@@ -1132,7 +1458,7 @@
     grad_step = dot_tn(back_pre, rank_in)
     back_rank = dot_nn(back_pre, w_step)
     back_selection = plane_total(
-        jnp.concatenate([back_rank, back_bc[:, : rank + 2 * states + spare - rank]], axis=1), 2
+        jnp.concatenate([back_rank, back_bc[:, : wide - rank]], axis=1), 2
     )[:, : rank + 2 * states]
     grad_select = dot_tn(flat(selected), back_selection)
     back_selected = dot_nt(back_selection, w_select).reshape(length, seqs, chans) + back_x
@@ -1140,14 +1466,14 @@
     grad_offset = back_conv.sum((0, 1))
     grad_taps = jnp.stack(
         [
-            (back_conv * shift_down(conv_in, j) * same[j]).sum((0, 1))
+            (back_conv * shifted(conv_in, j)).sum((0, 1))
             for j in reversed(range(taps))
         ],
         axis=1,
     )
-    back_conv_in = sum(
-        shift_up(back_conv * same[j], j) * tap[j] for j in range(taps)
-    )
+    back_conv_in = back_conv * tap[0]
+    for j in range(1, taps):
+        back_conv_in = back_conv_in + shift_up(back_conv * same[j], j) * tap[j]
     back_conv_in = seq_major(back_conv_in.astype(BF16))
     back_gate_in = seq_major(back_gate_in.astype(BF16))
     back_part = (dot_nt(back_conv_in, w_conv) + dot_nt(back_gate_in, w_gate)).astype(BF16)
@@ -1178,7 +1504,6 @@
         in_weight.shape[1],
     )
     g_gain = g_gain[0]
-    own_out = lax.psum_scatter(grad_out, "z", scatter_dimension=0, tiled=True)
     if rh_size > 1:
         small_own, g_in, own_out, g_gain = lax.psum(
             (small_own.astype(F32), g_in, own_out, g_gain), "rh"

time: 730 us -> 655 us (0.90)
  matrix products: 154 us -> 122 us
  waiting for transfers between devices: 67.3 us -> 47 us
  Pallas kernels: 392 us -> 372 us
    pallas_call x1, Pallas kernels: 154 us -> 111 us  [last_sums(): pl.pallas_call(functools.partial(finish_kernel, z_size), in_specs=[any_sp...]
    pallas_call x1, Pallas kernels: 92.5 us -> 133 us  [front(): pl.pallas_call(functools.partial(front_kernel, z_size, taps, rank), in_sp...]
    dot_general x15 -> x12, matrix products: 154 us -> 122 us  [dot(): return lax.dot_general(a, b, (dims, ((), ())), preferred_element_type=F32)]
    all_gather x3 -> x0, waiting for transfers between devices: 25.1 us -> none  [the longest x1 25.1 us: shards(): lax.all_gather(gate_slab, 'z', axis=0, tiled=True).reshape(-1, chans)]
    transpose x2 -> x1, other arithmetic: 21.2 us -> 4.57 us  [seq_major(): return v.reshape(length, seqs, -1).swapaxes(0, 1).reshape(seqs * length, -1)]
    pallas_call x2 -> x1, Pallas kernels: 45.7 us -> 29.6 us  [plane_total(): pl.pallas_call(total_kernel, in_specs=[vmem], out_specs=vmem, out_shape=j...]
    dot_general x0 -> x1, other arithmetic: none -> 9.35 us  [dot(): return lax.dot_general(a, b, (dims, ((), ())), preferred_element_type=F32)]
  transfers between devices with their start and end apart: 6 -> 3, of which waited for: 2 -> 1; matrix products, arithmetic and copies ran while one was open for 24% -> 19% of each run, Pallas kernels for 38% -> 22%
where the time goes in v2:
time: 655 us; the launch traced here: 648 us
  Pallas kernels  372 us (57%)
  matrix products  122 us (19%)
  local copies, waits for them, and re-layouts  52.5 us (8%)
  waiting for transfers between devices  47 us (7%)
  other arithmetic  38.5 us (6%)
  between operations  16.2 us (2%)
    pallas_call x1, Pallas kernels, front(): pl.pallas_call(functools.partial(front_kernel, z_size, taps, rank), in_sp...  133 us
    dot_general x12, matrix products, dot(): return lax.dot_general(a, b, (dims, ((), ())), preferred_element_type=F32)  122 us
    pallas_call x1, Pallas kernels, last_sums(): pl.pallas_call(functools.partial(finish_kernel, z_size), in_specs=[any_sp...  111 us
    pallas_call x1, Pallas kernels, scan_backward(): pl.pallas_call(functools.partial(bwd_kernel, states), grid=(chunks,), in_...  68 us
    reduce_scatter x1, waiting for transfers between devices, shards(): own_out = lax.psum_scatter(grad_out, 'z', scatter_dimension=0, tiled=True)  46.6 us
    pallas_call x1, Pallas kernels, scan_forward(): pl.pallas_call(functools.partial(fwd_kernel, states), grid=(length // STE...  30.4 us
    pallas_call x1, Pallas kernels, plane_total(): pl.pallas_call(total_kernel, in_specs=[vmem], out_specs=vmem, out_shape=j...  29.6 us
  transfers between devices with their start and end apart: 3, of which 1 were waited for; matrix products, arithmetic and copies ran while one was open for 19% of the time, Pallas kernels for 22%

profile of v2, /device:TPU:11, one launch (start us, length us, event | category | flops | bytes accessed | tf_op | source)
XLA Modules:
  0.0 647.9 jit_solution(338046763540178666)
XLA Ops:
  12.8 3.2 reshape.221
  24.1 132.9 %shard_map.220 = (bf16[8,256,2048]{2,1,0:T(8,128)(2,1)}, bf16[8,256,2048]{2,1,0:T(8,128)(2,1)}, bf16[2048,512]{1,0:T(8,128)(2,1)}, bf16[2048,512]{1,0:T(8,128)(2...) custom-call(bf16[256,2048]{1,0:T(8,128)(2,1)} %tokens_ref.3, ...), custom_call_target="tpu_custom_call" | custom-call | flops 120000004096 | bytes 120000000 | tf_op jit(solution)/shard_map/pallas_call | solution.py:763
  164.5 8.5 %convolution_convert_fusion.1 = bf16[2048,512]{1,0:T(8,128)(2,1)S(1)} fusion(bf16[2048,2048]{1,0:T(8,128)(2,1)} %bitcast.204, bf16[512,2048]{1,0:T(8,128)(2,1)} %get-tuple-element.43), kind=kOutput, calls=%fused_computation.47 | convolution fusion | flops 4296015872 | bytes 12582912 | tf_op jit(solution)/shard_map/dot_general | solution.py:22
  178.4 30.4 %shard_map.221 = (f32[256,8,512]{2,1,0:T(8,128)}, f32[256,16,8,512]{3,2,1,0:T(8,128)}, f32[16,8,512]{2,1,0:T(8,128)}) custom-call(f32[256,8,512]{2,1,0:T(8,128)} %get-tuple-element.46.dt_ref, f32[256,8,512]{2,1,0:T(8,128)} %broadcast_add_fusion.dtm_ref, f32[256,8,512]{2,1,0:T(8,128)} %get-tuple-element.48.x_ref, f32[256,8,32]{2,1,0:T(8,128)} %fusion.36.bc_ref, ...), custom_call_target="tpu_custom_call" | custom-call | flops 30000001024 | bytes 30000000 | tf_op jit(solution)/shard_map/pallas_call | solution.py:80
  208.8 18.5 %fusion.29 = (bf16[8,256,512]{2,0,1:T(8,128)(2,1)}, bf16[8,256,512]{2,0,1:T(8,128)(2,1)S(1)}, f32[256,8,512]{2,1,0:T(8,128)}, bf16[512,2048]{0,1:T(8,128)(2,1)}) fusion(f32[8,256,512]{2,1,0:T(8,128)S(1)} %convert.58, f32[256,8,512]{2,1,0:T(8,128)} %get-tuple-element.51, f32[256,8,512]{2,1,0:T(8,128)} %get-tuple-element.48.x_ref, f32[512]{0:T(512)S(1)} %bitcast.196, ...), kind=kOutput, calls=%fused_computation.61 | convolution fusion | flops 4312793088 | bytes 33556480 | tf_op jit(solution)/shard_map/dot_general | solution.py:22
  227.3 15.6 %bitcast_convert_fusion.2 = bf16[512,2048]{1,0:T(8,128)(2,1)} fusion(bf16[8,256,512]{2,0,1:T(8,128)(2,1)S(1)} %get-tuple-element.121, bf16[8,256,2048]{2,1,0:T(8,128)(2,1)} %get-tuple-element.42), kind=kOutput, calls=%fused_computation.26 | convolution fusion | flops 4296015872 | bytes 12582912 | tf_op jit(solution)/shard_map/dot_general | solution.py:22
  244.4 6.8 %convolution_convert_fusion = bf16[2048,2048]{1,0:T(8,128)(2,1)} fusion(bf16[2048,512]{1,0:T(8,128)(2,1)S(1)} %bitcast.169, bf16[512,2048]{1,0:T(8,128)(2,1)S(1)} %copy-done.26), kind=kOutput, calls=%fused_computation.5 | convolution fusion | flops 4299161600 | bytes 12582912 | tf_op jit(solution)/shard_map/dot_general | solution.py:22
  253.6 68.0 %shard_map.222 = (f32[256,8,512]{2,1,0:T(8,128)}, f32[256,8,512]{2,1,0:T(8,128)}, f32[2048,128]{1,0:T(8,128)}, f32[16,8,512]{2,1,0:T(8,128)}) custom-call(f32[256,8,512]{2,1,0:T(8,128)} %get-tuple-element.46.dt_ref, f32[256,8,512]{2,1,0:T(8,128)} %broadcast_add_fusion.dtm_ref, f32[256,8,512]{2,1,0:T(8,128)} %get-tuple-element.48.x_ref, ...), custom_call_target="tpu_custom_call" | custom-call | flops 70000001024 | bytes 70000000 | tf_op jit(solution)/shard_map/pallas_call | solution.py:195
  321.6 46.6 %reduce-scatter.5.cloned.1.call-done = bf16[128,2048]{1,0:T(8,128)(2,1)} async-done(((bf16[512,2048]{1,0:T(8,128)(2,1)}), bf16[128,2048]{1,0:T(8,128)(2,1)}) %reduce-scatter.5.cloned.1.call-update) | async-done | bytes 524304 | tf_op jit(solution)/shard_map/reduce_scatter | solution.py:1450
  371.2 9.4 %convert_bitcast_fusion.1 = (bf16[512,2048]{0,1:T(8,128)(2,1)}, f32[256,8,512]{2,1,0:T(8,128)S(1)}, bf16[512]{0:T(512)(128)(2,1)S(1)}) fusion(f32[256,8,512]{2,1,0:T(8,128)} %get-tuple-element.60, f32[256,8,512]{2,1,0:T(8,128)} %get-tuple-element.48.x_ref, f32[256,8,512]{2,1,0:T(8,128)} %get-tuple-element.59, f32[256,8,512]{2,1,0:T(8,128)} %get-tuple-element.58, ...), kind=kLoop, calls=%fused_computation.70 | loop fusion | flops 10485248 | bytes 27264000 | tf_op jit(solution)/shard_map/dot_general | solution.py:22
  383.1 29.6 %shard_map.223 = bf16[4,2,256,256]{3,2,1,0:T(8,128)(2,1)S(1)} custom-call(f32[4,2,256,256]{3,2,1,0:T(8,128)S(1)} %bitcast.162), custom_call_target="tpu_custom_call" | custom-call | flops 20000000000 | bytes 20000000 | tf_op jit(solution)/shard_map/pallas_call | solution.py:875
  416.0 22.7 %multiply_reduce_fusion.1 = (bf16[512]{0:T(512)(128)(2,1)S(1)}, bf16[512]{0:T(512)(128)(2,1)S(1)}, bf16[512]{0:T(512)(128)(2,1)S(1)}, bf16[512]{0:T(512)(128)(2,...) fusion(f32[256,8,512]{2,1,0:T(8,128)} %get-tuple-element.63, ...), kind=kOutput, calls=%fused_computation.40 | convolution fusion | flops 375387648 | bytes 34907136 | tf_op jit(solution)/shard_map/dot_general | solution.py:22
  438.6 4.6 fusion.28
  443.2 10.4 %bitcast_convert_fusion = bf16[2048,512]{1,0:T(8,128)(2,1)} fusion(bf16[8,256,2048]{2,1,0:T(8,128)(2,1)} %get-tuple-element.44, bf16[8,256,512]{2,0,1:T(8,128)(2,1)S(1)} %fusion.28), kind=kOutput, calls=%fused_computation.22 | convolution fusion | flops 4296015872 | bytes 12582912 | tf_op jit(solution)/shard_map/dot_general | solution.py:22
  455.7 2.9 copy.102
  459.6 4.3 copy.103
  464.0 3.2 convolution_convert_fusion.3
  467.2 2.5 reduce_sum.77
  474.3 8.2 %fusion.56 = f32[2048,2048]{1,0:T(8,128)} fusion(bf16[2048,512]{1,0:T(8,128)(2,1)S(1)} %bitcast.168, bf16[2048,512]{1,0:T(8,128)(2,1)S(1)} %copy-done.25), kind=kOutput, calls=%fused_computation.126 | convolution fusion | flops 4294967296 | bytes 20971520 | tf_op jit(solution)/shard_map/dot_general | solution.py:22
  482.5 14.8 %add_convert_fusion = bf16[2048,2048]{1,0:T(8,128)(2,1)} fusion(f32[2048,2048]{1,0:T(8,128)} %fusion.56, bf16[2048,512]{1,0:T(8,128)(2,1)} %bitcast.170, bf16[2048,512]{1,0:T(8,128)(2,1)} %get-tuple-element.45), kind=kOutput, calls=%fused_computation | convolution fusion | flops 4303355904 | bytes 29360128 | tf_op jit(solution)/shard_map/dot_general | solution.py:22
  500.9 10.4 %bitcast_convert_fusion.1 = bf16[2048,512]{1,0:T(8,128)(2,1)} fusion(bf16[8,256,2048]{2,1,0:T(8,128)(2,1)} %get-tuple-element.44, bf16[8,256,512]{2,0,1:T(8,128)(2,1)S(1)} %copy-done.6), kind=kOutput, calls=%fused_computation.23 | convolution fusion | flops 4296015872 | bytes 12582912 | tf_op jit(solution)/shard_map/dot_general | solution.py:22
  511.4 110.7 %shard_map.224 = (bf16[256,2048]{1,0:T(8,128)(2,1)}, f32[128,8192]{1,0:T(8,128)}, bf16[2,128,384]{2,1,0:T(8,128)(2,1)}, f32[8,128]{1,0:T(8,128)}) custom-call(bf16[4,2,256,2048]{3,2,1,0:T(8,128)(2,1)} %bitcast.205, bf16[4,128,384]{2,1,0:T(8,128)(2,1)} %concatenate.41.small_ref, bf16[4,512,512]{2,1,0:T(8,128)(2,1)} %bitcast.207, ...), custom_call_target="tpu_custom_call" | custom-call | flops 99999997952 | bytes 100000000 | tf_op jit(solution)/shard_map/pallas_call | solution.py:1243
  631.8 2.8 convert_element_type.124
  634.6 2.7 add_convert_fusion.1
  (128 shorter events, 61.9 us)
Async XLA Ops:
  8.0 3.9 copy-start
  8.0 360.2 %reduce-scatter.5.cloned.1.call-start = ((), (), s32[]{:S(2)}) async-start(), calls=%async_computation.3 | async-start | bytes 2621440 | tf_op jit(solution)/shard_map/reduce_scatter | solution.py:1450
  18.5 3.0 copy-start.22
  18.5 2.9 copy-start.23
  18.5 4.4 copy-start.21
  18.5 5.0 copy-start.24
  157.1 6.4 copy-start.11
  159.5 49.3 %copy-start.19 = (f32[1,512]{1,0:T(1,128)}, f32[1,512]{1,0:T(1,128)S(1)}, u32[]{:S(2)}) copy-start(f32[1,512]{1,0:T(1,128)S(1)} %get-tuple-element.137) | copy-start | bytes 6148
  321.6 310.2 %all-gather.2.cloned.1.call-start = ((), (), s32[]{:S(2)}) async-start(), calls=%async_computation.4 | async-start | bytes 1572864 | tf_op jit(solution)/shard_map/all_gather | solution.py:1511
  368.3 266.3 %reduce-scatter.3.cloned.1.call-start = ((), (), s32[]{:S(2)}) async-start(), calls=%async_computation.2 | async-start | bytes 9437184 | tf_op jit(solution)/shard_map/reduce_scatter | solution.py:1446
  383.1 32.8 %copy-start.14 = (f32[1,512]{1,0:T(1,128)S(1)}, f32[1,512]{1,0:T(1,128)}, u32[]{:S(2)}) copy-start(f32[1,512]{1,0:T(1,128)} %get-tuple-element.133) | copy-start | bytes 6148
  383.1 32.8 %copy-start.15 = (f32[1,512]{1,0:T(1,128)S(1)}, f32[1,512]{1,0:T(1,128)}, u32[]{:S(2)}) copy-start(f32[1,512]{1,0:T(1,128)} %get-tuple-element.134) | copy-start | bytes 6148
  383.1 32.8 %copy-start.16 = (f32[1,512]{1,0:T(1,128)S(1)}, f32[1,512]{1,0:T(1,128)}, u32[]{:S(2)}) copy-start(f32[1,512]{1,0:T(1,128)} %get-tuple-element.135) | copy-start | bytes 6148
  383.1 32.8 %copy-start.17 = (f32[1,512]{1,0:T(1,128)S(1)}, f32[1,512]{1,0:T(1,128)}, u32[]{:S(2)}) copy-start(f32[1,512]{1,0:T(1,128)} %get-tuple-element.136) | copy-start | bytes 6148
  383.1 32.8 %copy-start.18 = (f32[1,512]{1,0:T(1,128)S(1)}, f32[1,512]{1,0:T(1,128)}, u32[]{:S(2)}) copy-start(f32[1,512]{1,0:T(1,128)} %get-tuple-element.132) | copy-start | bytes 6148
  383.1 32.8 %copy-start.20 = (f32[1,512]{1,0:T(1,128)S(1)}, f32[1,512]{1,0:T(1,128)}, u32[]{:S(2)}) copy-start(f32[1,512]{1,0:T(1,128)} %copy-done.19) | copy-start | bytes 6148
  464.0 5.7 copy-start.12
  464.0 5.8 copy-start.13
  464.0 7.3 %copy-start.6 = (bf16[8,256,512]{2,0,1:T(8,128)(2,1)S(1)}, bf16[8,256,512]{2,0,1:T(8,128)(2,1)}, u32[]{:S(2)}) copy-start(bf16[8,256,512]{2,0,1:T(8,128)(2,1)} %get-tuple-element.120) | copy-start | bytes 6291460
  471.3 3.0 copy-start.25
  622.0 12.5 %copy-start.8 = (bf16[256,2048]{1,0:T(8,128)(2,1)S(1)}, bf16[256,2048]{1,0:T(8,128)(2,1)}, u32[]{:S(2)}) copy-start(bf16[256,2048]{1,0:T(8,128)(2,1)} %tokens_ref.3) | copy-start | bytes 3145732
  622.0 15.3 %copy-start.9 = (bf16[256,2048]{1,0:T(8,128)(2,1)S(1)}, bf16[256,2048]{1,0:T(8,128)(2,1)}, u32[]{:S(2)}) copy-start(bf16[256,2048]{1,0:T(8,128)(2,1)} %get-tuple-element.156) | copy-start | bytes 3145732
  634.6 3.7 copy-start.5
  637.3 3.0 copy-start.1
  (6 other events, 11.8 us)
Sparse Core Ops, SparseCore 0:
  321.7 46.4 reduce-scatter.4
  369.8 24.0 all-gather.1
Sparse Core Ops, SparseCore 1:
  372.2 77.6 reduce-scatter.2

commit v3 on v2

v3 whole, which is shorter than its diff:
```python
import functools

import jax
import jax.numpy as jnp
from jax import lax
from jax.experimental import pallas as pl
from jax.experimental.pallas import tpu as pltpu
from jax.sharding import Mesh
from jax.sharding import PartitionSpec as P

F32 = jnp.float32
BF16 = jnp.bfloat16
epsilon = 1e-05
PLANE = ("x", "y", "c")
BIG = 1e30
STEPS = 32
INNER = 4
LOG2E = 1.4426950408889634


def dot(a, b, dims):
    return lax.dot_general(a, b, (dims, ((), ())), preferred_element_type=F32)


def dot_nn(a, b):
    return dot(a, b, ((1,), (0,)))


def dot_tn(a, b):
    return dot(a, b, ((0,), (0,)))


def dot_nt(a, b):
    return dot(a, b, ((1,), (1,)))


def busy(micros):
    return pl.CostEstimate(flops=micros * 10**9, bytes_accessed=micros * 10**6, transcendentals=0)


MESH = pl.DeviceIdType.MESH
RING = 4


def place():
    return {a: lax.axis_index(a) for a in ("x", "z", "y", "c")}


def ring_chip(p):
    y = p // 2
    return (p + y) % 2, y


def ring_at(x, y):
    return 2 * y + (x + y) % 2


def share_at(f):
    return {"z": f // 4, "y": f // 2 % 2, "c": f % 2}


def remote(src, dst, send, recv, device):
    return pltpu.make_async_remote_copy(
        src_ref=src, dst_ref=dst, send_sem=send, recv_sem=recv, device_id=device, device_id_type=MESH
    )


def greet(devices):
    barrier = pltpu.get_barrier_semaphore()
    for device in devices:
        pl.semaphore_signal(barrier, inc=1, device_id=device, device_id_type=MESH)
    pl.semaphore_wait(barrier, len(devices))


def plane_others(me):
    out = []
    for dx in range(2):
        for dy in range(2):
            for dc in range(2):
                if dx + dy + dc:
                    out.append(
                        {"x": (me["x"] + dx) % 2, "y": (me["y"] + dy) % 2, "c": (me["c"] + dc) % 2}
                    )
    return out


def share_others(me, shares):
    f = me["z"] * 4 + me["y"] * 2 + me["c"]
    return [share_at((f + k) % shares) for k in range(1, shares)]


def z_only(me, shares):
    f = me["c"] + 2 * me["y"]
    out = []
    for dz in range(1, shares // 4):
        for k in range(4):
            out.append(
                {
                    "z": (me["z"] + dz) % (shares // 4),
                    "y": (f + k) % 4 // 2,
                    "c": (f + k) % 2,
                }
            )
    return out


def z_line(z, z_size, pieces, sems):
    up_s, up_r, down_s, down_r = sems

    def up(k):
        return [
            remote(p(z - k), p(z - k), up_s.at[k, j], up_r.at[k, j], {"z": z + 1})
            for j, p in enumerate(pieces)
        ]

    def down(k):
        return [
            remote(p(z + k), p(z + k), down_s.at[k, j], down_r.at[k, j], {"z": z - 1})
            for j, p in enumerate(pieces)
        ]

    def start(k):
        @pl.when((z < z_size - 1) & (z >= k))
        def _():
            for copy in up(k):
                copy.start()

        @pl.when((z > 0) & (z + k < z_size))
        def _():
            for copy in down(k):
                copy.start()

    def arrive(k):
        @pl.when(z > k)
        def _():
            for copy in up(k):
                copy.wait_recv()

        @pl.when(z + k < z_size - 1)
        def _():
            for copy in down(k):
                copy.wait_recv()

    def sent(k):
        @pl.when((z < z_size - 1) & (z >= k))
        def _():
            for copy in up(k):
                copy.wait_send()

        @pl.when((z > 0) & (z + k < z_size))
        def _():
            for copy in down(k):
                copy.wait_send()

    return start, arrive, sent


class Ring:
    def __init__(self, me, blocks, own, ring_send, ring_recv, sib_send, sib_recv):
        self.me, self.blocks, self.own = me, blocks, own
        self.sems = ring_send, ring_recv, sib_send, sib_recv
        self.at = ring_at(me["x"], me["y"])
        self.step = 1 + 2 * me["c"]
        nx, ny = ring_chip((self.at + self.step) % RING)
        self.following = {"x": nx, "y": ny}
        self.sibling = {"c": 1 - me["c"]}
        self.half = blocks.shape[1] // 2

    def slot(self, k):
        ox, oy = ring_chip((self.at + (RING - self.step) * k) % RING)
        return ox * 4 + oy * 2 + self.me["c"]

    def hop(self, k):
        out = []
        for p in range(2):
            rows = pl.ds(p * self.half, self.half)
            dst = self.blocks.at[self.slot(k), rows]
            src = self.own.at[rows] if k == 0 and self.own is not None else dst
            out.append(remote(src, dst, self.sems[0].at[k, p], self.sems[1].at[k, p], self.following))
        return out

    def cross(self, k):
        dst = self.blocks.at[self.slot(k)]
        src = self.own if k == 0 and self.own is not None else dst
        return remote(src, dst, self.sems[2].at[k], self.sems[3].at[k], self.sibling)

    def start(self, k):
        if k < RING - 1:
            for copy in self.hop(k):
                copy.start()
        self.cross(k).start()

    def arrive(self, k):
        for copy in self.hop(k):
            copy.wait_recv()

    def sent(self, k):
        if k < RING - 1:
            for copy in self.hop(k):
                copy.wait_send()
        self.cross(k).wait()


def softplus(v):
    e = jnp.exp(-jnp.abs(v))
    small = e * (1.0 - e * (0.5 - e * (1.0 / 3.0)))
    return jnp.maximum(v, 0.0) + jnp.where(e < 1e-3, small, jnp.log(1.0 + e))


def front_kernel(
    z_size,
    taps,
    rank,
    tokens_ref,
    gain_ref,
    ids_ref,
    rows_ref,
    cot_ref,
    conv_ref,
    gate_ref,
    out_ref,
    mats_ref,
    normed_hbm,
    cot_all,
    conv_hbm,
    gate_all,
    out_all,
    mats_hbm,
    keep_hbm,
    cin_hbm,
    x_hbm,
    dt_hbm,
    pre_hbm,
    picked_hbm,
    params,
    gain_all,
    selection,
    normed_all,
    conv_w,
    mats,
    rows_all,
    gain_got,
    ids_all,
    proj,
    cin,
    xs,
    picked,
    part,
    dts,
    pres,
    keep,
    first,
    from_sib,
    stage,
    got,
    local_sem,
    gain_send,
    gain_recv,
    ids_send,
    ids_recv,
    conv_send,
    conv_recv,
    gate_send,
    gate_recv,
    ring_send,
    ring_recv,
    sib_send,
    sib_recv,
    cot_ring_send,
    cot_ring_recv,
    cot_sib_send,
    cot_sib_recv,
    a_us,
    a_ur,
    a_ds,
    a_dr,
    b_us,
    b_ur,
    b_ds,
    b_dr,
    sw_s,
    sw_r,
    rs_s,
    rs_r,
    ag_s,
    ag_r,
    fw_s,
    fw_r,
):
    me = place()
    x, y, z, c = me["x"], me["y"], me["z"], me["c"]
    shares = z_size * 4
    share = z * 4 + y * 2 + c
    corner = y * 2 + c
    seq = x * 4 + y * 2 + c
    sibling = {"c": 1 - c}
    length, width = tokens_ref.shape
    chans = conv_ref.shape[2]
    rows_in = conv_ref.shape[1]
    half = mats_ref.shape[0]
    hops = z_size - 1
    greet(plane_others(me) + z_only(me, shares))

    def rows_at(ref, index, count):
        return ref.at[pl.ds(pl.multiple_of(index * count, count), count)]

    def corner_sends(src, dst, send, recv):
        out = []
        for k in range(1, 4):
            to = (corner + k) % 4
            out.append(
                remote(
                    src.at[to],
                    rows_at(dst, share, rows_in),
                    send.at[k - 1],
                    recv.at[k - 1],
                    {"y": to // 2, "c": to % 2},
                )
            )
        return out

    swaps = corner_sends(conv_ref, conv_w, conv_send, conv_recv)
    gates = corner_sends(gate_ref, gate_all, gate_send, gate_recv)
    for copy in swaps:
        copy.start()
    gains = [
        remote(gain_ref, gain_got.at[share], gain_send.at[k], gain_recv.at[k], device)
        for k, device in enumerate(share_others(me, shares))
    ]
    for copy in gains:
        copy.start()
    locals_ = [
        pltpu.make_async_copy(conv_ref.at[corner], rows_at(conv_w, share, rows_in), local_sem.at[0]),
        pltpu.make_async_copy(mats_ref, rows_at(mats, z, half), local_sem.at[1]),
        pltpu.make_async_copy(gate_ref.at[corner], rows_at(gate_all, share, rows_in), local_sem.at[2]),
        pltpu.make_async_copy(out_ref, rows_at(out_all, z, half), local_sem.at[3]),
        pltpu.make_async_copy(cot_ref, cot_all.at[seq], local_sem.at[4]),
    ]
    for copy in locals_:
        copy.start()
    ids_copies = [
        remote(ids_ref, ids_all.at[seq], ids_send.at[k], ids_recv.at[k], device)
        for k, device in enumerate(plane_others(me))
    ]
    for copy in ids_copies:
        copy.start()
    ids_all[seq] = ids_ref[...]
    gain_got[share] = gain_ref[...]
    rows_all[z] = rows_ref[...]

    values = tokens_ref[...].astype(F32)
    rstd = lax.rsqrt(jnp.mean(values * values, axis=-1, keepdims=True) + epsilon)
    for copy in gains:
        copy.wait()
    piece = gain_ref.shape[1]
    for f in range(shares):
        cols = pl.ds(f * piece, piece)
        normed = tokens_ref[:, cols].astype(F32) * rstd * gain_got[f, 0:1, :]
        normed_all[seq, :, cols] = normed.astype(BF16)
    gain_all[...] = gain_got[...]

    ring = Ring(me, normed_all, None, ring_send, ring_recv, sib_send, sib_recv)
    cot_ring = Ring(me, cot_all, cot_ref, cot_ring_send, cot_ring_recv, cot_sib_send, cot_sib_recv)
    ring.start(0)
    for copy in swaps:
        copy.wait()
    for copy in locals_:
        copy.wait()
    a_start, a_arrive, a_sent = z_line(
        z,
        z_size,
        [
            lambda k: rows_at(conv_w, k, 4 * rows_in),
            lambda k: rows_at(mats, k, half),
            lambda k: rows_all.at[k],
        ],
        (a_us, a_ur, a_ds, a_dr),
    )
    b_start, b_arrive, b_sent = z_line(
        z,
        z_size,
        [lambda k: rows_at(gate_all, k, 4 * rows_in), lambda k: rows_at(out_all, k, half)],
        (b_us, b_ur, b_ds, b_dr),
    )
    a_start(0)
    for copy in gates:
        copy.start()

    for copy in ids_copies:
        copy.wait()
    ids = jnp.concatenate([ids_all[s, 0:1, :] for s in range(8)], axis=0).astype(F32)
    before = pltpu.roll(ids, 1, 1)
    lane = lax.broadcasted_iota(jnp.int32, ids.shape, 1)
    same = jnp.where((ids == before) & (lane > 0), 1.0, 0.0)
    for t in range(length):
        keep[t] = jnp.broadcast_to(same[:, t : t + 1], (8, 128))
    keep_copy = pltpu.make_async_copy(keep, keep_hbm, local_sem.at[5])
    keep_copy.start()

    for k in range(max(hops, RING - 1)):
        if k < hops:
            a_arrive(k)
            if k + 1 < hops:
                a_start(k + 1)
        if k < RING - 1:
            ring.arrive(k)
            ring.start(k + 1)
        if k == RING - 2:
            cot_ring.start(0)
    for copy in gates:
        copy.wait()
    b_start(0)
    for k in range(RING):
        ring.sent(k)
    outs = [
        pltpu.make_async_copy(normed_all, normed_hbm, local_sem.at[6]),
        pltpu.make_async_copy(conv_w, conv_hbm, local_sem.at[7]),
        pltpu.make_async_copy(mats, mats_hbm, local_sem.at[8]),
    ]
    for copy in outs:
        copy.start()
    for zz in range(z_size):
        params[:, zz * half : (zz + 1) * half] = rows_all[zz].astype(F32)

    def project(s, carry):
        proj[s] = dot_nn(normed_all[s], conv_w[...])
        return carry

    lax.fori_loop(0, 8, project, 0)

    cin[0:3] = jnp.zeros((3, 8, chans), F32)
    block = 32
    fine = 4

    def turn(i, carry):
        t0 = pl.multiple_of(i * block, block)
        cin[pl.ds(3 + t0, block)] = jnp.swapaxes(proj[:, pl.ds(t0, block), :], 0, 1)
        return carry

    lax.fori_loop(0, length // block, turn, 0)

    def convolve(i, carry):
        t0 = i * fine
        for g in range(chans // 128):
            lanes = pl.ds(g * 128, 128)
            tap = [jnp.broadcast_to(params[taps - 1 - j : taps - j, lanes], (8, 128)) for j in range(taps)]
            offset = jnp.broadcast_to(params[taps : taps + 1, lanes], (8, 128))
            chosen = []
            for j in range(fine):
                t = t0 + j
                total = tap[3] * cin[t, :, lanes] * keep[jnp.maximum(t - 2, 0)]
                total = (total + tap[2] * cin[t + 1, :, lanes]) * keep[jnp.maximum(t - 1, 0)]
                total = (total + tap[1] * cin[t + 2, :, lanes]) * keep[t]
                v = total + tap[0] * cin[t + 3, :, lanes] + offset
                chosen.append((v / (1.0 + jnp.exp(-v))).astype(BF16))
                xs[t, :, lanes] = chosen[-1].astype(F32)
            rows = pl.ds(pl.multiple_of(t0 * 8, fine * 8), fine * 8)
            picked[rows, lanes] = jnp.concatenate(chosen, axis=0)
        return carry

    lax.fori_loop(0, length // fine, convolve, 0)
    outs += [
        pltpu.make_async_copy(cin.at[pl.ds(3, length)], cin_hbm, local_sem.at[9]),
        pltpu.make_async_copy(xs, x_hbm, local_sem.at[10]),
        pltpu.make_async_copy(picked, picked_hbm, local_sem.at[13]),
    ]
    for copy in outs[3:]:
        copy.start()

    wide = part.shape[3]

    def select(b, carry):
        rows = pl.ds(pl.multiple_of(b * length, length), length)
        part[b // 2, b % 2] = dot_nn(picked[rows, :], mats[:, :wide])
        return carry

    lax.fori_loop(0, 8, select, 0)
    first[...] = part[:, 1 - c].astype(BF16)
    swap = remote(first, from_sib, sw_s.at[0], sw_r.at[0], sibling)
    swap.start()
    swap.wait()
    mine = x * 2 + y
    chips = [((x + d // 2) % 2, (y + d % 2) % 2) for d in (1, 2, 3)]
    sends = []
    for k in (2, 1, 0):
        ox, oy = chips[k]
        j = ox * 2 + oy
        stage[k] = (part[j, c] + from_sib[j].astype(F32)).astype(BF16)
        copy = remote(stage.at[k], got.at[k], rs_s.at[k], rs_r.at[k], {"x": ox, "y": oy})
        copy.start()
        sends.append(copy)
    total = part[mine, c] + from_sib[mine].astype(F32)
    for copy in sends:
        copy.wait()
    for k in range(3):
        total = total + got[k].astype(F32)
    selection[mine, c] = total.astype(BF16)
    here = selection.at[mine, c]
    spreads = []
    for k in (2, 1, 0):
        ox, oy = chips[k]
        copy = remote(here, here, ag_s.at[k], ag_r.at[k], {"x": ox, "y": oy})
        copy.start()
        spreads.append((k, copy))
    forwards = [remote(here, here, fw_s.at[3], fw_r.at[3], sibling)]
    forwards[0].start()
    if hops > 1:
        b_arrive(0)
        b_start(1)
    cot_ring.arrive(0)
    cot_ring.start(1)
    for k, copy in reversed(spreads):
        copy.wait_recv()
        ox, oy = chips[k]
        there = selection.at[ox * 2 + oy, c]
        forwards.append(remote(there, there, fw_s.at[k], fw_r.at[k], sibling))
        forwards[-1].start()
    for _, copy in spreads:
        copy.wait_send()
    for copy in forwards:
        copy.wait()

    bias = params[taps + 1 : taps + 2, :]

    def steps(i, carry):
        rows = 64
        per = length // rows
        b = i // per
        at = pl.ds(pl.multiple_of((i % per) * rows, rows), rows)
        v = dot_nt(selection[b // 2, b % 2, at, :rank], mats[:, wide : wide + rank]) + bias
        t = pl.ds(i * (rows // 8), rows // 8)
        pres[t] = v.reshape(rows // 8, 8, chans)
        dts[t] = softplus(v).reshape(rows // 8, 8, chans)
        return carry

    lax.fori_loop(0, length * 8 // 64, steps, 0)
    outs += [
        pltpu.make_async_copy(dts, dt_hbm, local_sem.at[11]),
        pltpu.make_async_copy(pres, pre_hbm, local_sem.at[12]),
    ]
    for copy in outs[6:]:
        copy.start()

    cot_ring.arrive(1)
    cot_ring.start(2)
    for k in range(1 if hops > 1 else 0, hops):
        b_arrive(k)
        if k + 1 < hops:
            b_start(k + 1)
    cot_ring.arrive(2)
    cot_ring.start(3)
    for k in range(RING):
        cot_ring.sent(k)
    for k in range(hops):
        a_sent(k)
        b_sent(k)
    for copy in outs + [keep_copy]:
        copy.wait()


def front(z_size, taps, rank, tokens, gain, ids, rows, cot, conv, gate, out, mats):
    length, width = tokens.shape
    shares = z_size * 4
    chans = conv.shape[2]
    wide = mats.shape[1] - rank
    any_space = pl.BlockSpec(memory_space=pl.ANY)
    vmem = pl.BlockSpec(memory_space=pltpu.VMEM)
    dma = pltpu.SemaphoreType.DMA
    hops = z_size - 1
    shape = jax.ShapeDtypeStruct
    everyone = (8,) + tokens.shape
    per_token = (length, 8, chans)
    block = (length, wide)
    return pl.pallas_call(
        functools.partial(front_kernel, z_size, taps, rank),
        in_specs=[vmem] * 8 + [any_space],
        out_specs=[any_space] * 12 + [vmem] * 3,
        out_shape=[
            shape(everyone, BF16),
            shape(everyone, BF16),
            shape((width, chans), BF16),
            shape((width, chans), BF16),
            shape((chans, width), BF16),
            shape((chans, mats.shape[1]), BF16),
            shape((length, 8, 128), F32),
            shape(per_token, F32),
            shape(per_token, F32),
            shape(per_token, F32),
            shape(per_token, F32),
            shape((length * 8, chans), BF16),
            shape((rows.shape[0], chans), F32),
            shape((shares,) + gain.shape, F32),
            shape((4, 2) + block, BF16),
        ],
        scratch_shapes=[
            pltpu.VMEM(everyone, BF16),
            pltpu.VMEM((width, chans), BF16),
            pltpu.VMEM((chans, mats.shape[1]), BF16),
            pltpu.VMEM((z_size,) + rows.shape, BF16),
            pltpu.VMEM((shares,) + gain.shape, F32),
            pltpu.VMEM((8,) + ids.shape, ids.dtype),
            pltpu.VMEM((8, length, chans), F32),
            pltpu.VMEM((length + 3, 8, chans), F32),
            pltpu.VMEM(per_token, F32),
            pltpu.VMEM((length * 8, chans), BF16),
            pltpu.VMEM((4, 2) + block, F32),
            pltpu.VMEM(per_token, F32),
            pltpu.VMEM(per_token, F32),
            pltpu.VMEM((length, 8, 128), F32),
            pltpu.VMEM((4,) + block, BF16),
            pltpu.VMEM((4,) + block, BF16),
            pltpu.VMEM((3,) + block, BF16),
            pltpu.VMEM((3,) + block, BF16),
            dma((14,)),
            dma((shares - 1,)),
            dma((shares - 1,)),
            dma((7,)),
            dma((7,)),
        ]
        + [dma((3,))] * 4
        + [dma((RING - 1, 2)), dma((RING - 1, 2)), dma((RING,)), dma((RING,))] * 2
        + [dma((hops, 3))] * 4
        + [dma((hops, 2))] * 4
        + [dma((1,))] * 2
        + [dma((3,))] * 4
        + [dma((4,))] * 2,
        cost_estimate=busy(120),
        compiler_params=pltpu.CompilerParams(
            collective_id=0, has_side_effects=True, vmem_limit_bytes=60 << 20
        ),
    )(tokens, gain, ids, rows, cot, conv, gate, out, mats)


def add_rows(dst, srcs, rows):
    count = dst.shape[0] // rows

    def body(i, carry):
        at = pl.ds(pl.multiple_of(i * rows, rows), rows)
        total = srcs[0][at].astype(F32)
        for src in srcs[1:]:
            total = total + src[at].astype(F32)
        dst[at] = total.astype(dst.dtype)
        return carry

    lax.fori_loop(0, count, body, 0)


def forward_kernel(
    states,
    rank,
    skip_row,
    dt_ref,
    x_ref,
    sel_ref,
    keep_ref,
    rate_ref,
    normed_ref,
    cot_ref,
    gate_w_ref,
    out_w_ref,
    params_ref,
    hist_ref,
    last_ref,
    ds_ref,
    bgi_ref,
    part_ref,
    gout_ref,
    ggate_ref,
    h_ref,
    bc_ref,
    y_ref,
    ys_ref,
    gate_ref,
    bg_ref,
    gated_ref,
    gout_acc,
    ggate_acc,
):
    chunk = pl.program_id(0)

    @pl.when(chunk == 0)
    def _():
        h_ref[...] = jnp.zeros_like(h_ref)
        gout_acc[...] = jnp.zeros_like(gout_acc)
        ggate_acc[...] = jnp.zeros_like(ggate_acc)

    steps, seqs, width = dt_ref.shape
    groups = width // 128
    rows = steps * seqs
    bc_ref[...] = sel_ref[:, rank:].astype(F32).reshape(bc_ref.shape)

    def body(tb, carry):
        t0 = tb * INNER
        bc = [bc_ref[t0 + i] for i in range(INNER)]
        off = [(1.0 - keep_ref[t0 + i]) * BIG for i in range(INNER)]
        for g in range(groups):
            lanes = pl.ds(g * 128, 128)
            dt = [dt_ref[t0 + i, :, lanes] for i in range(INNER)]
            dtm = [dt[i] + off[i] for i in range(INNER)]
            u = [dt[i] * x_ref[t0 + i, :, lanes] for i in range(INNER)]
            y = [None] * INNER
            for n in range(states):
                h = h_ref[n, :, lanes]
                rate = rate_ref[n, :, lanes]
                for i in range(INNER):
                    hist_ref[t0 + i, n, :, lanes] = h
                    a = jnp.exp2(dtm[i] * rate)
                    h = a * h + u[i] * bc[i][:, n : n + 1]
                    term = h * bc[i][:, states + n : states + n + 1]
                    y[i] = term if y[i] is None else y[i] + term
                h_ref[n, :, lanes] = h
            skip = params_ref[skip_row : skip_row + 1, lanes]
            for i in range(INNER):
                y_ref[t0 + i, :, lanes] = y[i] + skip * x_ref[t0 + i, :, lanes]
        return carry

    lax.fori_loop(0, steps // INNER, body, 0)
    last_ref[...] = h_ref[...]

    normed = normed_ref[...].reshape(rows, normed_ref.shape[2])
    cot = cot_ref[...].reshape(rows, cot_ref.shape[2])
    gate_ref[...] = dot_nn(normed, gate_w_ref[...])
    bg_ref[...] = dot_nt(cot, out_w_ref[...]).astype(BF16).astype(F32)
    ys_ref[...] = jnp.swapaxes(y_ref[...], 0, 1).reshape(rows, width)
    fine = 16

    def gating(i, carry):
        r = pl.ds(pl.multiple_of(i * fine, fine), fine)
        v = gate_ref[r, :]
        bg = bg_ref[r, :]
        y = ys_ref[r, :]
        s = 1.0 / (1.0 + jnp.exp(-v))
        gate = v * s
        gated_ref[r, :] = (y * gate).astype(BF16)
        bg_ref[r, :] = bg * gate
        gate_ref[r, :] = bg * y * (s * (1.0 + v * (1.0 - s)))
        return carry

    lax.fori_loop(0, rows // fine, gating, 0)
    ds_ref[...] = jnp.swapaxes(bg_ref[...].reshape(seqs, steps, width), 0, 1)
    bgi = gate_ref[...].astype(BF16)
    bgi_ref[...] = bgi.reshape(bgi_ref.shape)
    gated = gated_ref[...]
    part_ref[...] = dot_nn(gated, out_w_ref[...]).astype(BF16).reshape(part_ref.shape)
    gout_acc[...] += dot_tn(gated, cot)
    ggate_acc[...] += dot_tn(normed, bgi)

    @pl.when(chunk == pl.num_programs(0) - 1)
    def _():
        gout_ref[...] = gout_acc[...].astype(BF16)
        ggate_ref[...] = ggate_acc[...].astype(BF16)


def scan_forward(rank, skip_row, dt, x, selection, keep, rate, normed, cot, gate_w, out_w, params):
    length, seqs, width = dt.shape
    model = normed.shape[2]
    states = rate.shape[0]
    wide = selection.shape[1]
    block = lambda *tail: pl.BlockSpec((STEPS,) + tail, lambda i: (i,) + (0,) * len(tail))
    across = lambda n: pl.BlockSpec((seqs, STEPS, n), lambda i: (0, i, 0))
    whole = lambda *dims: pl.BlockSpec(dims, lambda i: (0,) * len(dims))
    rows = STEPS * seqs
    shape = jax.ShapeDtypeStruct
    return pl.pallas_call(
        functools.partial(forward_kernel, states, rank, skip_row),
        grid=(length // STEPS,),
        in_specs=[
            block(seqs, width),
            block(seqs, width),
            pl.BlockSpec((rows, wide), lambda i: (i, 0)),
            block(seqs, 128),
            whole(states, seqs, width),
            across(model),
            across(model),
            whole(model, width),
            whole(width, model),
            whole(*params.shape),
        ],
        out_specs=[
            block(states, seqs, width),
            whole(states, seqs, width),
            block(seqs, width),
            across(width),
            across(model),
            whole(width, model),
            whole(model, width),
        ],
        out_shape=[
            shape((length, states, seqs, width), F32),
            shape((states, seqs, width), F32),
            shape(dt.shape, F32),
            shape((seqs, length, width), BF16),
            shape((seqs, length, model), BF16),
            shape((width, model), BF16),
            shape((model, width), BF16),
        ],
        scratch_shapes=[
            pltpu.VMEM((states, seqs, width), F32),
            pltpu.VMEM((STEPS, seqs, wide - rank), F32),
            pltpu.VMEM((STEPS, seqs, width), F32),
            pltpu.VMEM((rows, width), F32),
            pltpu.VMEM((rows, width), F32),
            pltpu.VMEM((rows, width), F32),
            pltpu.VMEM((rows, width), BF16),
            pltpu.VMEM((width, model), F32),
            pltpu.VMEM((model, width), F32),
        ],
        cost_estimate=busy(60),
        compiler_params=pltpu.CompilerParams(vmem_limit_bytes=60 << 20),
    )(dt, x, selection, keep, rate, normed, cot, gate_w, out_w, params)


def z_sums(z, z_size, owns, ups, downs, sems, blocks):
    up_s, up_r, down_s, down_r = sems

    def up_copy(k, j, own):
        src = owns[j].at[z_size - 1 - k] if own else ups[j].at[k]
        return remote(src, ups[j].at[k], up_s.at[k, j], up_r.at[k, j], {"z": z + 1})

    def down_copy(k, j, own):
        src = owns[j].at[k] if own else downs[j].at[k]
        return remote(src, downs[j].at[k], down_s.at[k, j], down_r.at[k, j], {"z": z - 1})

    def line(tau, j):
        k = tau - z
        high = z_size - 1 - k

        @pl.when((k >= 0) & (z < high) & (z > 0))
        def _():
            up_copy(k, j, False).wait_recv()
            add_rows(ups[j].at[k], [owns[j].at[high], ups[j].at[k]], blocks[j])
            up_copy(k, j, False).start()

        @pl.when((k >= 0) & (z < high) & (z == 0))
        def _():
            up_copy(k, j, True).start()

        m = tau - (z_size - 1 - z)

        @pl.when((m >= 0) & (z > m) & (z < z_size - 1))
        def _():
            down_copy(m, j, False).wait_recv()
            add_rows(downs[j].at[m], [owns[j].at[m], downs[j].at[m]], blocks[j])
            down_copy(m, j, False).start()

        @pl.when((m >= 0) & (z > m) & (z == z_size - 1))
        def _():
            down_copy(m, j, True).start()

    def settle(j, dst):
        low = z
        high = z_size - 1 - z

        @pl.when(z == 0)
        def _():
            down_copy(low, j, False).wait_recv()
            add_rows(dst, [owns[j].at[z], downs[j].at[low]], blocks[j])

        @pl.when(z == z_size - 1)
        def _():
            up_copy(high, j, False).wait_recv()
            add_rows(dst, [owns[j].at[z], ups[j].at[high]], blocks[j])

        @pl.when((z > 0) & (z < z_size - 1))
        def _():
            down_copy(low, j, False).wait_recv()
            up_copy(high, j, False).wait_recv()
            add_rows(dst, [owns[j].at[z], downs[j].at[low], ups[j].at[high]], blocks[j])

    def sent(j):
        for k in range(z_size - 1):

            @pl.when(z < z_size - 1 - k)
            def _():
                up_copy(k, j, False).wait_send()

            @pl.when(z > k)
            def _():
                down_copy(k, j, False).wait_send()

    return line, settle, sent


def backward_kernel(
    chunks_all,
    z_size,
    states,
    rank,
    skip_row,
    dt_ref,
    x_ref,
    ds_ref,
    pre_ref,
    sel_ref,
    keep_ref,
    rate_ref,
    hist_ref,
    last_ref,
    ones_ref,
    params_ref,
    step_w_ref,
    gate_hbm,
    out_hbm,
    bx_ref,
    part_ref,
    da_ref,
    gstep_ref,
    bias_ref,
    skip_ref,
    gate_fin,
    out_fin,
    ag_ref,
    h_ref,
    pb_ref,
    pc_ref,
    bc_ref,
    bp_ref,
    gate_own,
    out_own,
    gate_up,
    out_up,
    gate_down,
    out_down,
    local_sem,
    up_s,
    up_r,
    down_s,
    down_r,
):
    chunk = pl.program_id(0)
    chunks = pl.num_programs(0)
    me = place()
    z = me["z"]
    hops = z_size - 1
    line, settle, sent = z_sums(
        z,
        z_size,
        (gate_own, out_own),
        (gate_up, out_up),
        (gate_down, out_down),
        (up_s, up_r, down_s, down_r),
        (64, 16),
    )

    @pl.when(chunk == 0)
    def _():
        greet([{"z": (z + 1) % z_size}, {"z": (z + z_size - 1) % z_size}])
        loads = [
            pltpu.make_async_copy(gate_hbm, gate_own, local_sem.at[0]),
            pltpu.make_async_copy(out_hbm, out_own, local_sem.at[1]),
        ]
        for copy in loads:
            copy.start()
        ag_ref[...] = jnp.zeros_like(ag_ref)
        da_ref[...] = jnp.zeros_like(da_ref)
        gstep_ref[...] = jnp.zeros_like(gstep_ref)
        bias_ref[...] = jnp.zeros_like(bias_ref)
        skip_ref[...] = jnp.zeros_like(skip_ref)
        h_ref[...] = last_ref[...]
        for copy in loads:
            copy.wait()

    for tau in range(hops):

        @pl.when(chunk == -(-tau * chunks_all // hops))
        def _():
            line(tau, 0)
            line(tau, 1)

    steps, seqs, width = dt_ref.shape
    groups = width // 128
    blocks = steps // INNER
    bc_ref[...] = sel_ref[:, rank:].astype(F32).reshape(bc_ref.shape)

    def body(back, carry):
        t0 = (blocks - 1 - back) * INNER
        rows = pl.ds(pl.multiple_of(t0 * seqs, INNER * seqs), INNER * seqs)
        bc = [bc_ref[t0 + i] for i in range(INNER)]
        off = [(1.0 - keep_ref[t0 + i]) * BIG for i in range(INNER)]
        for g in range(groups):
            lanes = pl.ds(g * 128, 128)
            dt = [dt_ref[t0 + i, :, lanes] for i in range(INNER)]
            dtm = [dt[i] + off[i] for i in range(INNER)]
            ds = [ds_ref[t0 + i, :, lanes] for i in range(INNER)]
            u = [dt[i] * x_ref[t0 + i, :, lanes] for i in range(INNER)]
            s1 = [None] * INNER
            s2 = [None] * INNER
            for n in range(states):
                ag = ag_ref[n, :, lanes]
                h = h_ref[n, :, lanes]
                rate = rate_ref[n, :, lanes]
                da = da_ref[n, :, lanes]
                pb = [None] * INNER
                pc = [None] * INNER
                for i in reversed(range(INNER)):
                    prev = hist_ref[t0 + i, n, :, lanes]
                    a = jnp.exp2(dtm[i] * rate)
                    adj = ds[i] * bc[i][:, states + n : states + n + 1] + ag
                    pc[i] = ds[i] * h
                    pb[i] = adj * u[i]
                    ag = a * adj
                    w = ag * prev
                    rw = rate * w
                    gb = adj * bc[i][:, n : n + 1]
                    s1[i] = rw if s1[i] is None else s1[i] + rw
                    s2[i] = gb if s2[i] is None else s2[i] + gb
                    da = da + dt[i] * w
                    h = prev
                ag_ref[n, :, lanes] = ag
                h_ref[n, :, lanes] = h
                da_ref[n, :, lanes] = da
                cols = pl.ds((g * states + n) * 128, 128)
                pb_ref[rows, cols] = jnp.concatenate(pb, axis=0).astype(BF16)
                pc_ref[rows, cols] = jnp.concatenate(pc, axis=0).astype(BF16)
            skip = params_ref[skip_row : skip_row + 1, lanes]
            bias = bias_ref[:, lanes]
            direct = skip_ref[:, lanes]
            low = []
            for i in range(INNER):
                x = x_ref[t0 + i, :, lanes]
                bx_ref[t0 + i, :, lanes] = dt[i] * s2[i] + skip * ds[i]
                back = (s1[i] * (1.0 / LOG2E) + x * s2[i]) / (1.0 + jnp.exp(-pre_ref[t0 + i, :, lanes]))
                low.append(back)
                bias = bias + back
                direct = direct + ds[i] * x
            bias_ref[:, lanes] = bias
            skip_ref[:, lanes] = direct
            bp_ref[rows, lanes] = jnp.concatenate(low, axis=0).astype(BF16)
        return carry

    lax.fori_loop(0, blocks, body, 0)
    span = states * 128
    total = jnp.zeros((steps * seqs, 128), F32)
    for g in range(groups):
        total = total + dot_nn(pb_ref[:, pl.ds(g * span, span)], ones_ref[0])
        total = total + dot_nn(pc_ref[:, pl.ds(g * span, span)], ones_ref[1])
    part_ref[:, rank:] = total
    part_ref[:, :rank] = dot_nn(bp_ref[...], step_w_ref[...])
    gstep_ref[...] += dot_tn(bp_ref[...], sel_ref[:, :rank])

    @pl.when(chunk == chunks - 1)
    def _():
        settle(0, gate_fin)
        settle(1, out_fin)
        sent(0)
        sent(1)


def scan_backward(
    z_size, rank, skip_row, dt, x, ds, pre, selection, keep, rate, hist, last, params, step_w, gate, out
):
    length, seqs, width = dt.shape
    states = rate.shape[0]
    chunks = length // STEPS
    wide = selection.shape[1]
    rows = STEPS * seqs
    block = lambda *tail: pl.BlockSpec((STEPS,) + tail, lambda i: (chunks - 1 - i,) + (0,) * len(tail))
    flat = lambda n: pl.BlockSpec((rows, n), lambda i: (chunks - 1 - i, 0))
    whole = lambda *dims: pl.BlockSpec(dims, lambda i: (0,) * len(dims))
    any_space = pl.BlockSpec(memory_space=pl.ANY)
    span = states * 128
    entry = jnp.arange(span)[:, None] // 128
    column = jnp.arange(128)[None, :]
    ones = jnp.stack([entry == column, entry + states == column]).astype(BF16)
    hops = z_size - 1
    gate_shape, out_shape = gate.shape[1:], out.shape[1:]
    shape = jax.ShapeDtypeStruct
    dma = pltpu.SemaphoreType.DMA
    return pl.pallas_call(
        functools.partial(backward_kernel, chunks, z_size, states, rank, skip_row),
        grid=(chunks,),
        in_specs=[
            block(seqs, width),
            block(seqs, width),
            block(seqs, width),
            block(seqs, width),
            flat(wide),
            block(seqs, 128),
            whole(states, seqs, width),
            block(states, seqs, width),
            whole(states, seqs, width),
            whole(2, span, 128),
            whole(*params.shape),
            whole(width, rank),
            any_space,
            any_space,
        ],
        out_specs=[
            block(seqs, width),
            flat(wide),
            whole(states, seqs, width),
            whole(width, rank),
            whole(seqs, width),
            whole(seqs, width),
            whole(*gate_shape),
            whole(*out_shape),
        ],
        out_shape=[
            shape(dt.shape, F32),
            shape((length * seqs, wide), F32),
            shape((states, seqs, width), F32),
            shape((width, rank), F32),
            shape((seqs, width), F32),
            shape((seqs, width), F32),
            shape(gate_shape, BF16),
            shape(out_shape, BF16),
        ],
        scratch_shapes=[
            pltpu.VMEM((states, seqs, width), F32),
            pltpu.VMEM((states, seqs, width), F32),
            pltpu.VMEM((rows, width // 128 * span), BF16),
            pltpu.VMEM((rows, width // 128 * span), BF16),
            pltpu.VMEM((STEPS, seqs, wide - rank), F32),
            pltpu.VMEM((rows, width), BF16),
            pltpu.VMEM(gate.shape, BF16),
            pltpu.VMEM(out.shape, BF16),
            pltpu.VMEM((hops,) + gate_shape, BF16),
            pltpu.VMEM((hops,) + out_shape, BF16),
            pltpu.VMEM((hops,) + gate_shape, BF16),
            pltpu.VMEM((hops,) + out_shape, BF16),
            dma((2,)),
            dma((hops, 2)),
            dma((hops, 2)),
            dma((hops, 2)),
            dma((hops, 2)),
        ],
        cost_estimate=busy(80),
        compiler_params=pltpu.CompilerParams(
            collective_id=4, has_side_effects=True, vmem_limit_bytes=62 << 20
        ),
    )(dt, x, ds, pre, selection, keep, rate, hist, last, ones, params, step_w, gate, out)


def last_kernel(
    z_size,
    taps,
    part_ref,
    keep_ref,
    mats_ref,
    params_ref,
    gate_fin,
    out_fin,
    da_ref,
    gstep_ref,
    bias_ref,
    skip_ref,
    tokens_ref,
    cot_ref,
    gain_ref,
    bx_hbm,
    cin_hbm,
    picked_hbm,
    normed_hbm,
    conv_hbm,
    gate_hbm,
    bgi_hbm,
    tgrad_ref,
    in_ref,
    out_ref,
    small_out,
    vec_out,
    gain_out,
    chosen,
    first,
    from_sib,
    stage,
    got,
    bx,
    cin,
    picked,
    conv_w,
    gate_w,
    bgi,
    turned,
    bci,
    gsel,
    sums,
    columns,
    own_back,
    sib_stage,
    sib_back,
    ring_got,
    own_small,
    own_vec,
    own_conv,
    up_small,
    up_vec,
    up_conv,
    down_small,
    down_vec,
    down_conv,
    fin_conv,
    both_gate,
    both_conv,
    gain_parts,
    gain_got,
    gain_half,
    gain_pair,
    local_sem,
    column_sem,
    sw_s,
    sw_r,
    rs_s,
    rs_r,
    ag_s,
    ag_r,
    fw_s,
    fw_r,
    sib_send,
    sib_recv,
    ring_send,
    ring_recv,
    up_send,
    up_recv,
    down_send,
    down_recv,
    swap_send,
    swap_recv,
    x_send,
    x_recv,
    gain_send,
    gain_recv,
):
    me = place()
    x, y, z, c = me["x"], me["y"], me["z"], me["c"]
    shares = z_size * 4
    share = z * 4 + y * 2 + c
    corner = y * 2 + c
    sibling = {"c": 1 - c}
    over_x = {"x": 1 - x}
    length, width = tokens_ref.shape
    chans = bx.shape[2]
    rows_in = in_ref.shape[0]
    half = out_fin.shape[0]
    hops = z_size - 1
    wide = part_ref.shape[3]
    greet(plane_others(me) + z_only(me, shares))

    loads = [
        pltpu.make_async_copy(src, dst, local_sem.at[i])
        for i, (src, dst) in enumerate(
            [
                (cin_hbm, cin.at[pl.ds(3, length)]),
                (bx_hbm, bx.at[pl.ds(0, length)]),
                (picked_hbm, picked),
                (bgi_hbm, bgi),
                (conv_hbm, conv_w),
                (gate_hbm, gate_w),
            ]
        )
    ]
    for copy in loads:
        copy.start()

    first[...] = part_ref[:, 1 - c].astype(BF16)
    swap = remote(first, from_sib, sw_s.at[0], sw_r.at[0], sibling)
    swap.start()
    cin[0:3] = jnp.zeros((3, 8, chans), F32)
    bx[length : length + 3] = jnp.zeros((3, 8, chans), F32)
    sums[...] = jnp.zeros_like(sums)
    gsel[...] = jnp.zeros_like(gsel)
    swap.wait()
    mine = x * 2 + y
    chips = [((x + d // 2) % 2, (y + d % 2) % 2) for d in (1, 2, 3)]
    sends = []
    for k in (2, 1, 0):
        ox, oy = chips[k]
        j = ox * 2 + oy
        stage[k] = (part_ref[j, c] + from_sib[j].astype(F32)).astype(BF16)
        copy = remote(stage.at[k], got.at[k], rs_s.at[k], rs_r.at[k], {"x": ox, "y": oy})
        copy.start()
        sends.append(copy)
    total = part_ref[mine, c] + from_sib[mine].astype(F32)
    for copy in sends:
        copy.wait()
    for k in range(3):
        total = total + got[k].astype(F32)
    chosen[mine, c] = total.astype(BF16)
    here = chosen.at[mine, c]
    spreads = []
    for k in (2, 1, 0):
        ox, oy = chips[k]
        copy = remote(here, here, ag_s.at[k], ag_r.at[k], {"x": ox, "y": oy})
        copy.start()
        spreads.append((k, copy))
    forwards = [remote(here, here, fw_s.at[3], fw_r.at[3], sibling)]
    forwards[0].start()

    def corner_sends(src, dst, index):
        out = []
        for k in range(1, 4):
            to = (corner + k) % 4
            out.append(
                remote(
                    src.at[pl.ds(pl.multiple_of(to * rows_in, rows_in), rows_in)],
                    dst.at[x, corner],
                    swap_send.at[index, k - 1],
                    swap_recv.at[index, k - 1],
                    {"y": to // 2, "c": to % 2},
                )
            )
        return out

    gate_swaps = corner_sends(gate_fin, both_gate, 0)
    conv_swaps = corner_sends(fin_conv, both_conv, 1)
    for copy in gate_swaps:
        copy.start()
    both_gate[x, corner] = gate_fin[pl.ds(pl.multiple_of(corner * rows_in, rows_in), rows_in)]
    out_ref[x] = out_fin[...]
    out_x = remote(out_ref.at[x], out_ref.at[x], x_send.at[0], x_recv.at[0], over_x)
    for k, copy in reversed(spreads):
        copy.wait_recv()
        ox, oy = chips[k]
        there = chosen.at[ox * 2 + oy, c]
        forwards.append(remote(there, there, fw_s.at[k], fw_r.at[k], sibling))
        forwards[-1].start()
    out_x.start()
    for copy in loads:
        copy.wait()
    for _, copy in spreads:
        copy.wait_send()
    for copy in forwards:
        copy.wait()

    fine = 4
    block = length // 8

    def taps_of(lanes):
        return [
            jnp.broadcast_to(params_ref[taps - 1 - j : taps - j, lanes], (8, 128)) for j in range(taps)
        ]

    def select(b, carry):
        rows = pl.ds(pl.multiple_of(b * length, length), length)
        back = chosen[b // 2, b % 2]
        t0 = b * block
        bx[pl.ds(t0, block)] += dot_nt(back, mats_ref[:, :wide]).reshape(block, 8, chans)
        gsel[...] += dot_tn(picked[rows, :], back)

        def convolve(i, carry):
            for g in range(chans // 128):
                lanes = pl.ds(g * 128, 128)
                tap = taps_of(lanes)
                offset = jnp.broadcast_to(params_ref[taps : taps + 1, lanes], (8, 128))
                acc = [sums[r, :, lanes] for r in range(taps + 1)]
                for j in range(fine):
                    t = t0 + i * fine + j
                    k0 = keep_ref[t]
                    k1 = k0 * keep_ref[jnp.maximum(t - 1, 0)]
                    k2 = k1 * keep_ref[jnp.maximum(t - 2, 0)]
                    v0 = cin[t + 3, :, lanes]
                    v1 = cin[t + 2, :, lanes] * k0
                    v2 = cin[t + 1, :, lanes] * k1
                    v3 = cin[t, :, lanes] * k2
                    v = offset + tap[0] * v0 + tap[1] * v1 + tap[2] * v2 + tap[3] * v3
                    s = 1.0 / (1.0 + jnp.exp(-v))
                    back = bx[t, :, lanes] * (s * (1.0 + v * (1.0 - s)))
                    bx[t, :, lanes] = back
                    acc[0] = acc[0] + back * v0
                    acc[1] = acc[1] + back * v1
                    acc[2] = acc[2] + back * v2
                    acc[3] = acc[3] + back * v3
                    acc[4] = acc[4] + back
                for r in range(taps + 1):
                    sums[r, :, lanes] = acc[r]
            return carry

        lax.fori_loop(0, block // fine, convolve, 0)
        return carry

    lax.fori_loop(0, 8, select, 0)
    for copy in gate_swaps:
        copy.wait()
    gate_x = remote(both_gate.at[x], both_gate.at[x], x_send.at[1], x_recv.at[1], over_x)
    gate_x.start()

    def unfold(b, carry):
        t0 = b * block

        def convolve(i, carry):
            for g in range(chans // 128):
                lanes = pl.ds(g * 128, 128)
                tap = taps_of(lanes)
                for j in range(fine):
                    t = t0 + i * fine + j
                    total = tap[3] * bx[t + 3, :, lanes] * keep_ref[jnp.minimum(t + 3, length - 1)]
                    total = (total + tap[2] * bx[t + 2, :, lanes]) * keep_ref[
                        jnp.minimum(t + 2, length - 1)
                    ]
                    total = (total + tap[1] * bx[t + 1, :, lanes]) * keep_ref[
                        jnp.minimum(t + 1, length - 1)
                    ]
                    turned[i * fine + j, :, lanes] = total + tap[0] * bx[t, :, lanes]
            return carry

        lax.fori_loop(0, block // fine, convolve, 0)
        bci[:, pl.ds(pl.multiple_of(t0, block), block), :] = jnp.swapaxes(turned[...], 0, 1).astype(BF16)
        return carry

    def column(i, slot):
        zz = jnp.where(z * 2 < z_size, z_size - 1 - i, i)
        cols = pl.ds(pl.multiple_of(zz * 4 * rows_in, 4 * rows_in), 4 * rows_in)
        return zz, pltpu.make_async_copy(normed_hbm.at[:, :, cols], columns.at[slot], column_sem.at[slot])

    column(0, 0)[1].start()
    lax.fori_loop(0, 8, unfold, 0)

    owns = (own_small, own_vec, own_conv)
    line, settle, sent = z_sums(
        z,
        z_size,
        owns,
        (up_small, up_vec, up_conv),
        (down_small, down_vec, down_conv),
        (up_send, up_recv, down_send, down_recv),
        (16, 16, 64),
    )

    rates = -jnp.exp(params_ref[taps + 3 : taps + 3 + da_ref.shape[0], :])
    vectors = (
        [jnp.sum(sums[taps - 1 - r], axis=0, keepdims=True) for r in range(taps)]
        + [
            jnp.sum(sums[taps], axis=0, keepdims=True),
            jnp.sum(bias_ref[...], axis=0, keepdims=True),
            jnp.sum(skip_ref[...], axis=0, keepdims=True),
        ]
        + [jnp.sum(da_ref[...], axis=1) * rates]
    )
    used = taps + 3 + da_ref.shape[0]
    vectors = jnp.concatenate(
        vectors + [jnp.zeros((own_vec.shape[1] - used, chans), F32)], axis=0
    ).astype(BF16)
    for zz in range(z_size):
        own_vec[zz] = vectors[:, zz * half : (zz + 1) * half]
        own_small[zz, :, :wide] = gsel[zz * half : (zz + 1) * half, :].astype(BF16)
        own_small[zz, :, wide:] = gstep_ref[zz * half : (zz + 1) * half, :].astype(BF16)

    at = ring_at(x, y)
    step = 1 + 2 * c
    sib_step = 3 - 2 * c
    nx, ny = ring_chip((at + step) % RING)
    following = {"x": nx, "y": ny}

    def grad_column(i):
        slot = i % 2
        zz, copy = column(i, slot)
        copy.wait()
        if i + 1 < z_size:
            column(i + 1, 1 - slot)[1].start()
        tall = columns[slot].reshape(8 * length, 4 * rows_in)
        own_conv[zz] = dot_tn(tall, bci[...].reshape(8 * length, chans)).astype(BF16)

    def back_block(dst, p, core):
        cx, cy = ring_chip(p % RING)
        s = cx * 4 + cy * 2 + core

        def cols(i, carry):
            n = pl.ds(pl.multiple_of(i * 512, 512), 512)
            total = dot_nt(bci[s], conv_w[n, :]) + dot_nt(bgi[s], gate_w[n, :])
            dst[:, n] = total.astype(BF16)
            return carry

        lax.fori_loop(0, width // 512, cols, 0)

    def cross(k):
        slot = k % 2
        return remote(sib_stage.at[slot], sib_back.at[k], sib_send.at[k], sib_recv.at[k], sibling)

    def ring(k, p):
        r = pl.ds(p * (length // 2), length // 2)
        return remote(
            own_back.at[k, r], ring_got.at[k, r], ring_send.at[k, p], ring_recv.at[k, p], following
        )

    def blocks_for(k):
        if k >= 2:
            cross(k - 2).wait_send()
        back_block(sib_stage.at[k % 2], at + sib_step * (RING - 1 - k), 1 - c)
        cross(k).start()
        back_block(own_back.at[k], at + step * (RING - 1 - k), c)

    def ring_step(k):
        cross(k).wait_recv()
        srcs = [own_back.at[k], sib_back.at[k]]
        if k:
            for p in range(2):
                ring(k - 1, p).wait_recv()
            srcs.append(ring_got.at[k - 1])
        add_rows(own_back.at[k], srcs, 16)
        for p in range(2):
            ring(k, p).start()

    def ring_end():
        last = RING - 1
        cross(last).wait_recv()
        for p in range(2):
            ring(last - 1, p).wait_recv()
        rows = 16

        def body(i, total):
            r = pl.ds(pl.multiple_of(i * rows, rows), rows)
            back = (
                own_back[last, r].astype(F32)
                + sib_back[last, r].astype(F32)
                + ring_got[last - 1, r].astype(F32)
            )
            values = tokens_ref[r].astype(F32)
            rstd = lax.rsqrt(jnp.mean(values * values, axis=-1, keepdims=True) + epsilon)
            scaled = back * gain_ref[...]
            inner = jnp.mean(scaled * values, axis=-1, keepdims=True)
            grad = cot_ref[r].astype(F32) + rstd * scaled - values * (rstd * rstd * rstd * inner)
            tgrad_ref[r] = grad.astype(BF16)
            terms = back * values * rstd
            return total + terms[:8] + terms[8:]

        total = lax.fori_loop(0, length // rows, body, jnp.zeros((8, width), F32))
        total = jnp.broadcast_to(jnp.sum(total, axis=0, keepdims=True), (8, width))
        piece = gain_parts.shape[2]
        for f in range(shares):
            gain_parts[f] = total[:, f * piece : (f + 1) * piece]
        gain_got[share] = gain_parts[share]

    gains = []
    for k in range(1, shares):
        f = (share + k) % shares
        gains.append(
            remote(
                gain_parts.at[f], gain_got.at[share], gain_send.at[k - 1], gain_recv.at[k - 1], share_at(f)
            )
        )

    def lines(tau):
        for j in (2, 0, 1):
            line(tau, j)

    blocks_for(0)
    ring_step(0)
    grad_column(0)
    lines(0)
    for i in range(1, z_size):
        grad_column(i)
    blocks_for(1)
    ring_step(1)
    blocks_for(2)
    lines(1)
    blocks_for(3)
    ring_step(2)
    for tau in range(2, hops):
        lines(tau)
    ring_end()
    for copy in gains:
        copy.start()

    settle(2, fin_conv)
    for copy in conv_swaps:
        copy.start()
    both_conv[x, corner] = fin_conv[pl.ds(pl.multiple_of(corner * rows_in, rows_in), rows_in)]
    settle(0, small_out.at[x])
    settle(1, vec_out.at[x])
    small_x = remote(small_out.at[x], small_out.at[x], x_send.at[2], x_recv.at[2], over_x)
    vec_x = remote(vec_out.at[x], vec_out.at[x], x_send.at[3], x_recv.at[3], over_x)
    for copy in conv_swaps:
        copy.wait()
    conv_x = remote(both_conv.at[x], both_conv.at[x], x_send.at[4], x_recv.at[4], over_x)
    conv_x.start()
    small_x.start()
    vec_x.start()

    branch = 8 * half * z_size

    def lay(first, both):
        for zz in range(z_size):
            for j in range(4):
                for xx in range(2):
                    col = first + (zz * 4 + j) * 2 * half + xx * half
                    in_ref[:, col : col + half] = both[xx, j, :, zz * half : (zz + 1) * half].astype(F32)

    for copy in gains:
        copy.wait()
    gain_half[...] = jnp.sum(gain_got[...], axis=0)
    gain_x = remote(gain_half, gain_pair, x_send.at[5], x_recv.at[5], over_x)
    gain_x.start()
    gate_x.wait()
    lay(branch, both_gate)
    gain_x.wait()
    gain_out[...] = gain_half[...] + gain_pair[...]
    conv_x.wait()
    lay(0, both_conv)
    for copy in (out_x, small_x, vec_x):
        copy.wait()
    for j in range(3):
        sent(j)
    for k in range(RING - 1):
        for p in range(2):
            ring(k, p).wait_send()
    for k in range(2, RING):
        cross(k).wait_send()


def last_part(
    z_size,
    taps,
    part,
    keep,
    mats,
    params,
    gate_fin,
    out_fin,
    da,
    gstep,
    bias,
    skip,
    tokens,
    cot,
    gain,
    bx,
    cin,
    picked,
    normed,
    conv,
    gate,
    bgi,
    in_width,
):
    length, width = tokens.shape
    chans = bx.shape[2]
    shares = z_size * 4
    hops = z_size - 1
    rows_in = gate_fin.shape[0] // 4
    half = out_fin.shape[0]
    wide = part.shape[3]
    any_space = pl.BlockSpec(memory_space=pl.ANY)
    vmem = pl.BlockSpec(memory_space=pltpu.VMEM)
    dma = pltpu.SemaphoreType.DMA
    shape = jax.ShapeDtypeStruct
    block = (length, width)
    slabs = [(half, mats.shape[1]), (params.shape[0], half), (4 * rows_in, chans)]
    bufs = lambda n: [pltpu.VMEM((n,) + s, BF16) for s in slabs]
    both = pltpu.VMEM((2, 4, rows_in, chans), BF16)
    piece = (8, width // shares)
    few = (length, wide)
    return pl.pallas_call(
        functools.partial(last_kernel, z_size, taps),
        in_specs=[vmem] * 13 + [any_space] * 7,
        out_specs=[vmem] * 6,
        out_shape=[
            shape(tokens.shape, BF16),
            shape((rows_in, in_width), F32),
            shape((2,) + out_fin.shape, BF16),
            shape((2,) + slabs[0], BF16),
            shape((2,) + slabs[1], BF16),
            shape(piece, F32),
        ],
        scratch_shapes=[
            pltpu.VMEM((4, 2) + few, BF16),
            pltpu.VMEM((4,) + few, BF16),
            pltpu.VMEM((4,) + few, BF16),
            pltpu.VMEM((3,) + few, BF16),
            pltpu.VMEM((3,) + few, BF16),
            pltpu.VMEM((length + 3, 8, chans), F32),
            pltpu.VMEM((length + 3, 8, chans), F32),
            pltpu.VMEM(picked.shape, BF16),
            pltpu.VMEM(conv.shape, BF16),
            pltpu.VMEM(gate.shape, BF16),
            pltpu.VMEM(bgi.shape, BF16),
            pltpu.VMEM((length // 8, 8, chans), F32),
            pltpu.VMEM(bgi.shape, BF16),
            pltpu.VMEM((chans, wide), F32),
            pltpu.VMEM((taps + 1, 8, chans), F32),
            pltpu.VMEM((2, 8, length, 4 * rows_in), BF16),
            pltpu.VMEM((RING,) + block, BF16),
            pltpu.VMEM((2,) + block, BF16),
            pltpu.VMEM((RING,) + block, BF16),
            pltpu.VMEM((RING - 1,) + block, BF16),
        ]
        + bufs(z_size)
        + bufs(hops)
        + bufs(hops)
        + [
            pltpu.VMEM(slabs[2], BF16),
            both,
            both,
            pltpu.VMEM((shares,) + piece, F32),
            pltpu.VMEM((shares,) + piece, F32),
            pltpu.VMEM(piece, F32),
            pltpu.VMEM(piece, F32),
            dma((6,)),
            dma((2,)),
            dma((1,)),
            dma((1,)),
        ]
        + [dma((3,))] * 4
        + [dma((4,))] * 2
        + [dma((RING,))] * 2
        + [dma((RING - 1, 2))] * 2
        + [dma((hops, 3))] * 4
        + [dma((2, 3))] * 2
        + [dma((6,))] * 2
        + [dma((shares - 1,))] * 2,
        cost_estimate=busy(120),
        compiler_params=pltpu.CompilerParams(
            collective_id=3, has_side_effects=True, vmem_limit_bytes=63 << 20
        ),
    )(
        part,
        keep,
        mats,
        params,
        gate_fin,
        out_fin,
        da,
        gstep,
        bias,
        skip,
        tokens,
        cot,
        gain,
        bx,
        cin,
        picked,
        normed,
        conv,
        gate,
        bgi,
    )


def shards(
    tokens,
    doc_ids,
    norm_gain,
    in_weight,
    conv_taps,
    conv_offset,
    select_weight,
    step_weight,
    step_bias,
    decay_log,
    skip_gain,
    out_weight,
    cotangent,
):
    z_size = lax.axis_size("z")
    rh_size = lax.axis_size("rh")
    seqs = 8
    length = doc_ids.shape[1]
    width = tokens.shape[1]
    in_rows = in_weight.shape[0]
    rows = out_weight.shape[0]
    half = rows // 2
    chans = half * z_size
    taps = conv_taps.shape[1]
    rank = step_weight.shape[1]
    states = decay_log.shape[1]
    x_at = lax.axis_index("x")

    def own_half(w):
        return lax.dynamic_slice_in_dim(w, x_at * half, half, 0)

    spare = -(rank + 2 * states) % 128
    wide = rank + 2 * states + spare
    vectors = jnp.concatenate(
        [
            own_half(conv_taps),
            own_half(conv_offset)[:, None],
            own_half(step_bias)[:, None],
            own_half(skip_gain)[:, None],
            own_half(decay_log),
        ],
        axis=1,
    ).T
    vectors = jnp.pad(vectors, ((0, -vectors.shape[0] % 32), (0, 0)))
    mats = jnp.concatenate(
        [jnp.pad(own_half(select_weight), ((0, 0), (0, spare))), own_half(step_weight)], axis=1
    )
    columns = lax.dynamic_index_in_dim(
        in_weight.reshape(in_rows, 2, z_size, 4, 2, half), x_at, 4, keepdims=False
    )
    packed = columns.transpose(1, 3, 0, 2, 4).reshape(2, 4, in_rows, chans)
    gain_tile = jnp.broadcast_to(norm_gain.astype(F32)[None, :], (8, norm_gain.shape[0]))
    ids_tile = jnp.broadcast_to(doc_ids, (8, length))
    (
        all_normed,
        all_cot,
        w_conv,
        w_gate,
        w_out,
        w_mats,
        keep,
        conv_in,
        x,
        dt,
        pre,
        picked,
        vectors,
        gains,
        selection,
    ) = front(
        z_size,
        taps,
        rank,
        tokens,
        gain_tile,
        ids_tile,
        vectors,
        cotangent,
        packed[0],
        packed[1],
        own_half(out_weight),
        mats,
    )
    gain = gains[:, 0, :].reshape(1, width)
    selection = selection.reshape(length * seqs, wide)
    rates = -jnp.exp(vectors[taps + 3 : taps + 3 + states])
    rate2 = jnp.broadcast_to((rates * LOG2E)[:, None, :], (states, seqs, chans))

    hist, last, back_scan, back_gate_in, out_part, grad_out, grad_gate = scan_forward(
        rank, taps + 2, dt, x, selection, keep, rate2, all_normed, all_cot, w_gate, w_out, vectors
    )
    layer_sum = lax.psum_scatter(
        out_part.reshape(-1, width), PLANE, scatter_dimension=0, tiled=True
    )
    layer_out = (tokens.astype(F32) + layer_sum.astype(F32)).astype(BF16)
    back_x, part, da, g_step, g_bias, g_skip, gate_fin, out_fin = scan_backward(
        z_size,
        rank,
        taps + 2,
        dt,
        x,
        back_scan,
        pre,
        selection,
        keep,
        rate2,
        hist,
        last,
        vectors,
        w_mats[:, wide:],
        grad_gate.reshape(z_size, -1, chans),
        grad_out.reshape(z_size, half, width),
    )
    tokens_grad, g_in, g_out, g_mats, g_vectors, g_gain = last_part(
        z_size,
        taps,
        part.reshape(4, 2, length, wide),
        keep,
        w_mats,
        vectors,
        gate_fin,
        out_fin,
        da,
        g_step,
        g_bias,
        g_skip,
        tokens,
        cotangent,
        gain,
        back_x,
        conv_in,
        picked,
        all_normed,
        w_conv,
        w_gate,
        back_gate_in,
        in_weight.shape[1],
    )
    g_gain = g_gain[0]
    g_out = g_out.reshape(rows, width).astype(F32)
    g_mats = g_mats.reshape(rows, -1).astype(F32)
    g_vectors = g_vectors.transpose(0, 2, 1).reshape(rows, -1).astype(F32)
    if rh_size > 1:
        g_mats, g_vectors, g_in, g_out, g_gain = lax.psum(
            (g_mats, g_vectors, g_in, g_out, g_gain), "rh"
        )
    return (
        layer_out,
        tokens_grad,
        g_gain,
        g_in,
        g_vectors[:, :taps],
        g_vectors[:, taps],
        g_mats[:, : rank + 2 * states],
        g_mats[:, wide:],
        g_vectors[:, taps + 1],
        g_vectors[:, taps + 3 : taps + 3 + states],
        g_vectors[:, taps + 2],
        g_out,
    )


def solution(mesh):
    replicas = mesh.shape["replica"]
    shares = mesh.shape["fsdp"]
    grid = Mesh(
        mesh.devices.reshape(replicas // 2, 2, shares // 4, 2, 2), ("rh", "x", "z", "y", "c")
    )
    tok = ("rh", "x", "z", "y", "c")
    own = ("z", "y", "c")
    return jax.shard_map(
        shards,
        mesh=grid,
        in_specs=(
            P(tok, None),
            P(tok, None),
            P(own),
            P(own, None),
            P(own, None),
            P(own),
            P(own, None),
            P(own, None),
            P(own),
            P(own, None),
            P(own),
            P(own, None),
            P(tok, None),
        ),
        out_specs=(
            P(tok, None),
            P(tok, None),
            P(own),
            P(own, None),
            P(own, None),
            P(own),
            P(own, None),
            P(own, None),
            P(own),
            P(own, None),
            P(own),
            P(own, None),
        ),
        check_vma=False,
    )
```

time: 655 us -> 454 us (0.69)
  matrix products: 122 us -> 0 us
  waiting for transfers between devices: 47 us -> 0.02 us
  other arithmetic: 38.5 us -> 9.99 us
  Pallas kernels: 372 us -> 400 us
  local copies, waits for them, and re-layouts: 52.5 us -> 26.7 us
    dot_general x12 -> x0, matrix products: 122 us -> none  [dot(): return lax.dot_general(a, b, (dims, ((), ())), preferred_element_type=F32)]
    reduce_scatter x2 -> x1, waiting for transfers between devices: 46.6 us -> 0.01 us  [shards(): lax.psum_scatter(out_part.reshape(-1, width), PLANE, scatter_dimension=0,...]
    pallas_call x4 -> x3, Pallas kernels: 239 us -> 267 us  [the longest x1 113 us: last_part(): pl.pallas_call(functools.partial(last_kernel, z_size, taps), in_specs=[vm...]
    dot_general x1 -> x0, other arithmetic: 9.35 us -> none  [dot(): return lax.dot_general(a, b, (dims, ((), ())), preferred_element_type=F32)]
    dot_general x2 -> x0, local copies, waits for them, and re-layouts: 7.27 us -> none  [dot(): return lax.dot_general(a, b, (dims, ((), ())), preferred_element_type=F32)]
  transfers between devices with their start and end apart: 3 -> 1, of which waited for: 1 -> 0; matrix products, arithmetic and copies ran while one was open for 19% -> 3% of each run, Pallas kernels for 22% -> 46%
where the time goes in v3:
time: 454 us; the launch traced here: 451 us
  Pallas kernels  400 us (88%)
  local copies, waits for them, and re-layouts  26.7 us (6%)
  between operations  14.2 us (3%)
  other arithmetic  9.99 us (2%)
    pallas_call x1, Pallas kernels, front(): pl.pallas_call(functools.partial(front_kernel, z_size, taps, rank), in_sp...  133 us
    pallas_call x1, Pallas kernels, last_part(): pl.pallas_call(functools.partial(last_kernel, z_size, taps), in_specs=[vm...  113 us
    pallas_call x1, Pallas kernels, scan_backward(): pl.pallas_call(functools.partial(backward_kernel, chunks, z_size, states,...  94.1 us
    pallas_call x1, Pallas kernels, scan_forward(): pl.pallas_call(functools.partial(forward_kernel, states, rank, skip_row),...  60 us
  transfers between devices with their start and end apart: 1, of which 0 were waited for; matrix products, arithmetic and copies ran while one was open for 3% of the time, Pallas kernels for 46%

profile of v3, /device:TPU:11, one launch (start us, length us, event | category | flops | bytes accessed | tf_op | source)
XLA Modules:
  0.0 451.3 jit_solution(4094344413250663173)
XLA Ops:
  8.6 0.7 dynamic-slice_bitcast_fusion.2
  9.5 0.8 constant_dynamic-slice_fusion
  10.2 1.9 constant_dynamic-slice_fusion.2.out_ref
  12.1 3.2 reshape.156
  15.4 2.4 constant_dynamic-slice_fusion.3
  18.8 1.0 squeeze.23.conv_ref
  19.8 1.0 squeeze.24.gate_ref
  23.5 133.0 %shard_map.220 = (bf16[8,256,2048]{2,1,0:T(8,128)(2,1)}, bf16[8,256,2048]{2,1,0:T(8,128)(2,1)}, bf16[2048,512]{1,0:T(8,128)(2,1)}, bf16[2048,512]{1,0:T(8,128)(2...) custom-call(bf16[256,2048]{1,0:T(8,128)(2,1)} %tokens_ref.3, ...), custom_call_target="tpu_custom_call" | custom-call | flops 120000004096 | bytes 120000000 | tf_op jit(solution)/shard_map/pallas_call | solution.py:574
  156.5 0.8 negate_multiply_fusion
  157.3 0.7 broadcast_in_dim.36.rate_ref
  158.0 60.0 %shard_map.221 = (f32[256,16,8,512]{3,2,1,0:T(8,128)}, f32[16,8,512]{2,1,0:T(8,128)}, f32[256,8,512]{2,1,0:T(8,128)}, bf16[8,256,512]{2,1,0:T(8,128)(2,1)}, bf16...) custom-call(f32[256,8,512]{2,1,0:T(8,128)} %get-tuple-element.48.dt_ref, ...), custom_call_target="tpu_custom_call" | custom-call | flops 60000002048 | bytes 60000000 | tf_op jit(solution)/shard_map/pallas_call | solution.py:764
  218.0 1.6 slice.44.step_w_ref
  219.6 1.4 slice_bitcast_fusion.gain_ref
  221.0 1.2 iota_compare_fusion
  222.2 1.2 add_convert_fusion.1.ones_ref
  223.4 94.1 %shard_map.222 = (f32[256,8,512]{2,1,0:T(8,128)}, f32[2048,256]{1,0:T(8,128)}, f32[16,8,512]{2,1,0:T(8,128)}, f32[512,128]{1,0:T(8,128)}, f32[8,512]{1,0:T(8,128...) custom-call(f32[256,8,512]{2,1,0:T(8,128)} %get-tuple-element.48.dt_ref, ...), custom_call_target="tpu_custom_call" | custom-call | flops 80000000000 | bytes 80000000 | tf_op jit(solution)/shard_map/pallas_call | solution.py:1069
  317.6 113.3 %shard_map.223 = (bf16[256,2048]{1,0:T(8,128)(2,1)}, f32[128,8192]{1,0:T(8,128)}, bf16[2,128,2048]{2,1,0:T(8,128)(2,1)}, bf16[2,128,384]{2,1,0:T(8,128)(2,1)}, b...) custom-call(f32[4,2,256,256]{3,2,1,0:T(8,128)} %bitcast.46, f32[256,8,128]{2,1,0:T(8,128)} %get-tuple-element.51.keep_ref, ...), custom_call_target="tpu_custom_call" | custom-call | flops 120000004096 | bytes 120000000 | tf_op jit(solution)/shard_map/pallas_call | solution.py:1642
  430.9 1.0 bitcast_convert_fusion.1
  434.6 0.8 copy.31
  435.3 1.2 slice_bitcast_fusion.1
  437.1 1.6 bitcast_convert_fusion
  438.8 2.7 add_convert_fusion
  441.5 1.0 copy.39
  442.5 2.0 copy.40
  (43 shorter events, 8.4 us)
Async XLA Ops:
  7.2 2.2 copy-start
  7.2 431.6 %reduce-scatter.2.cloned.1.call-start = ((), (), s32[]{:S(2)}) async-start(), calls=%async_computation.1 | async-start | bytes 9437184 | tf_op jit(solution)/shard_map/reduce_scatter | solution.py:1820
  18.4 2.4 copy-start.7
  18.4 2.4 copy-start.8
  18.4 3.9 copy-start.6
  18.4 4.5 copy-start.9
  430.9 6.2 %copy-start.4 = (bf16[2,128,2048]{2,1,0:T(8,128)(2,1)S(1)}, bf16[2,128,2048]{2,1,0:T(8,128)(2,1)}, u32[]{:S(2)}) copy-start(bf16[2,128,2048]{2,1,0:T(8,128)(2,1)} %get-tuple-element.83) | copy-start | bytes 3145732
  432.0 6.8 %copy-start.3 = (bf16[256,2048]{1,0:T(8,128)(2,1)S(1)}, bf16[256,2048]{1,0:T(8,128)(2,1)}, u32[]{:S(2)}) copy-start(bf16[256,2048]{1,0:T(8,128)(2,1)} %tokens_ref.3) | copy-start | bytes 3145732
  438.7 2.8 copy-start.5
  438.8 3.7 copy-start.2
  442.5 2.0 copy-start.1
Sparse Core Ops, SparseCore 0:
  218.1 76.1 reduce-scatter.1

commit v4 on v3

--- a/solution.py
+++ b/solution.py
@@ -2,6 +2,7 @@
 
 import jax
 import jax.numpy as jnp
+import numpy as np
 from jax import lax
 from jax.experimental import pallas as pl
 from jax.experimental.pallas import tpu as pltpu
@@ -14,7 +15,10 @@
 PLANE = ("x", "y", "c")
 BIG = 1e30
 STEPS = 32
+COLUMNS = 512
 INNER = 4
+BACK_INNER = 8
+TOGETHER = 4
 LOG2E = 1.4426950408889634
 
 
@@ -201,6 +205,10 @@
         self.cross(k).wait()
 
 
+def sigmoid(v):
+    return 0.5 + 0.5 * jnp.tanh(0.5 * v)
+
+
 def softplus(v):
     e = jnp.exp(-jnp.abs(v))
     small = e * (1.0 - e * (0.5 - e * (1.0 / 3.0)))
@@ -216,10 +224,10 @@
     ids_ref,
     rows_ref,
     cot_ref,
-    conv_ref,
-    gate_ref,
+    in_ref,
     out_ref,
-    mats_ref,
+    select_ref,
+    step_ref,
     normed_hbm,
     cot_all,
     conv_hbm,
@@ -231,7 +239,6 @@
     x_hbm,
     dt_hbm,
     pre_hbm,
-    picked_hbm,
     params,
     gain_all,
     selection,
@@ -254,6 +261,7 @@
     stage,
     got,
     local_sem,
+    own_sem,
     gain_send,
     gain_recv,
     ids_send,
@@ -274,6 +282,10 @@
     a_ur,
     a_ds,
     a_dr,
+    m_us,
+    m_ur,
+    m_ds,
+    m_dr,
     b_us,
     b_ur,
     b_ds,
@@ -295,32 +307,41 @@
     seq = x * 4 + y * 2 + c
     sibling = {"c": 1 - c}
     length, width = tokens_ref.shape
-    chans = conv_ref.shape[2]
-    rows_in = conv_ref.shape[1]
-    half = mats_ref.shape[0]
+    chans = conv_w.shape[1]
+    rows_in = width // shares
+    half = chans // z_size
     hops = z_size - 1
+    branch = 8 * chans
     greet(plane_others(me) + z_only(me, shares))
 
     def rows_at(ref, index, count):
         return ref.at[pl.ds(pl.multiple_of(index * count, count), count)]
 
-    def corner_sends(src, dst, send, recv):
+    def pieces(first, dst, to):
+        rows = rows_at(dst, share, rows_in)
+        if len(in_ref.shape) == 4:
+            return [(in_ref.at[1 if first else 0, to], rows)]
+        out = []
+        for zz in range(z_size):
+            col = first + (zz * 4 + to) * 2 * half + x * half
+            src = in_ref.at[:, pl.ds(pl.multiple_of(col, half), half)]
+            out.append((src, rows.at[:, pl.ds(zz * half, half)]))
+        return out
+
+    def corner_sends(first, dst, send, recv):
         out = []
         for k in range(1, 4):
             to = (corner + k) % 4
-            out.append(
-                remote(
-                    src.at[to],
-                    rows_at(dst, share, rows_in),
-                    send.at[k - 1],
-                    recv.at[k - 1],
-                    {"y": to // 2, "c": to % 2},
+            for i, (src, there) in enumerate(pieces(first, dst, to)):
+                out.append(
+                    remote(
+                        src, there, send.at[k - 1, i], recv.at[k - 1, i], {"y": to // 2, "c": to % 2}
+                    )
                 )
-            )
         return out
 
-    swaps = corner_sends(conv_ref, conv_w, conv_send, conv_recv)
-    gates = corner_sends(gate_ref, gate_all, gate_send, gate_recv)
+    swaps = corner_sends(0, conv_w, conv_send, conv_recv)
+    gates = corner_sends(branch, gate_all, gate_send, gate_recv)
     for copy in swaps:
         copy.start()
     gains = [
@@ -330,12 +351,15 @@
     for copy in gains:
         copy.start()
     locals_ = [
-        pltpu.make_async_copy(conv_ref.at[corner], rows_at(conv_w, share, rows_in), local_sem.at[0]),
-        pltpu.make_async_copy(mats_ref, rows_at(mats, z, half), local_sem.at[1]),
-        pltpu.make_async_copy(gate_ref.at[corner], rows_at(gate_all, share, rows_in), local_sem.at[2]),
-        pltpu.make_async_copy(out_ref, rows_at(out_all, z, half), local_sem.at[3]),
+        pltpu.make_async_copy(
+            out_ref.at[pl.ds(pl.multiple_of(x * half, half), half)], rows_at(out_all, z, half), local_sem.at[3]
+        ),
         pltpu.make_async_copy(cot_ref, cot_all.at[seq], local_sem.at[4]),
     ]
+    for i, (src, there) in enumerate(pieces(0, conv_w, corner)):
+        locals_.append(pltpu.make_async_copy(src, there, own_sem.at[0, i]))
+    for i, (src, there) in enumerate(pieces(branch, gate_all, corner)):
+        locals_.append(pltpu.make_async_copy(src, there, own_sem.at[1, i]))
     for copy in locals_:
         copy.start()
     ids_copies = [
@@ -347,6 +371,17 @@
     ids_all[seq] = ids_ref[...]
     gain_got[share] = gain_ref[...]
     rows_all[z] = rows_ref[...]
+    mine_rows = pl.ds(pl.multiple_of(x * half, half), half)
+    at_rows = pl.ds(pl.multiple_of(z * half, half), half)
+    wide = mats.shape[1] - rank
+    mats[at_rows, :wide] = jnp.concatenate(
+        [
+            select_ref[mine_rows, :],
+            jnp.zeros((half, wide - select_ref.shape[1]), BF16),
+        ],
+        axis=1,
+    )
+    mats[at_rows, wide:] = step_ref[mine_rows, :]
 
     values = tokens_ref[...].astype(F32)
     rstd = lax.rsqrt(jnp.mean(values * values, axis=-1, keepdims=True) + epsilon)
@@ -357,7 +392,8 @@
         cols = pl.ds(f * piece, piece)
         normed = tokens_ref[:, cols].astype(F32) * rstd * gain_got[f, 0:1, :]
         normed_all[seq, :, cols] = normed.astype(BF16)
-    gain_all[...] = gain_got[...]
+    for f in range(shares):
+        gain_all[:, f * piece : (f + 1) * piece] = gain_got[f]
 
     ring = Ring(me, normed_all, None, ring_send, ring_recv, sib_send, sib_recv)
     cot_ring = Ring(me, cot_all, cot_ref, cot_ring_send, cot_ring_recv, cot_sib_send, cot_sib_recv)
@@ -371,10 +407,12 @@
         z_size,
         [
             lambda k: rows_at(conv_w, k, 4 * rows_in),
-            lambda k: rows_at(mats, k, half),
             lambda k: rows_all.at[k],
         ],
         (a_us, a_ur, a_ds, a_dr),
+    )
+    m_start, m_arrive, m_sent = z_line(
+        z, z_size, [lambda k: rows_at(mats, k, half)], (m_us, m_ur, m_ds, m_dr)
     )
     b_start, b_arrive, b_sent = z_line(
         z,
@@ -402,11 +440,15 @@
             a_arrive(k)
             if k + 1 < hops:
                 a_start(k + 1)
+            if k + 1 == hops - 1:
+                m_start(0)
         if k < RING - 1:
             ring.arrive(k)
             ring.start(k + 1)
         if k == RING - 2:
             cot_ring.start(0)
+    m_arrive(0)
+    m_start(1)
     for copy in gates:
         copy.wait()
     b_start(0)
@@ -415,7 +457,6 @@
     outs = [
         pltpu.make_async_copy(normed_all, normed_hbm, local_sem.at[6]),
         pltpu.make_async_copy(conv_w, conv_hbm, local_sem.at[7]),
-        pltpu.make_async_copy(mats, mats_hbm, local_sem.at[8]),
     ]
     for copy in outs:
         copy.start()
@@ -427,6 +468,12 @@
         return carry
 
     lax.fori_loop(0, 8, project, 0)
+    for k in range(1, hops):
+        m_arrive(k)
+        if k + 1 < hops:
+            m_start(k + 1)
+    cot_ring.arrive(0)
+    cot_ring.start(1)
 
     cin[0:3] = jnp.zeros((3, 8, chans), F32)
     block = 32
@@ -452,7 +499,7 @@
                 total = (total + tap[2] * cin[t + 1, :, lanes]) * keep[jnp.maximum(t - 1, 0)]
                 total = (total + tap[1] * cin[t + 2, :, lanes]) * keep[t]
                 v = total + tap[0] * cin[t + 3, :, lanes] + offset
-                chosen.append((v / (1.0 + jnp.exp(-v))).astype(BF16))
+                chosen.append((v * sigmoid(v)).astype(BF16))
                 xs[t, :, lanes] = chosen[-1].astype(F32)
             rows = pl.ds(pl.multiple_of(t0 * 8, fine * 8), fine * 8)
             picked[rows, lanes] = jnp.concatenate(chosen, axis=0)
@@ -460,11 +507,11 @@
 
     lax.fori_loop(0, length // fine, convolve, 0)
     outs += [
+        pltpu.make_async_copy(mats, mats_hbm, local_sem.at[8]),
         pltpu.make_async_copy(cin.at[pl.ds(3, length)], cin_hbm, local_sem.at[9]),
         pltpu.make_async_copy(xs, x_hbm, local_sem.at[10]),
-        pltpu.make_async_copy(picked, picked_hbm, local_sem.at[13]),
     ]
-    for copy in outs[3:]:
+    for copy in outs[2:]:
         copy.start()
 
     wide = part.shape[3]
@@ -504,11 +551,10 @@
         spreads.append((k, copy))
     forwards = [remote(here, here, fw_s.at[3], fw_r.at[3], sibling)]
     forwards[0].start()
-    if hops > 1:
-        b_arrive(0)
+    b_arrive(0)
+    if hops > 2:
         b_start(1)
-    cot_ring.arrive(0)
-    cot_ring.start(1)
+    cot_ring.arrive(1)
     for k, copy in reversed(spreads):
         copy.wait_recv()
         ox, oy = chips[k]
@@ -519,6 +565,7 @@
         copy.wait_send()
     for copy in forwards:
         copy.wait()
+    cot_ring.start(2)
 
     bias = params[taps + 1 : taps + 2, :]
 
@@ -538,14 +585,12 @@
         pltpu.make_async_copy(dts, dt_hbm, local_sem.at[11]),
         pltpu.make_async_copy(pres, pre_hbm, local_sem.at[12]),
     ]
-    for copy in outs[6:]:
+    for copy in outs[5:]:
         copy.start()
 
-    cot_ring.arrive(1)
-    cot_ring.start(2)
-    for k in range(1 if hops > 1 else 0, hops):
+    for k in range(1, hops - 1):
         b_arrive(k)
-        if k + 1 < hops:
+        if k + 1 < hops - 1:
             b_start(k + 1)
     cot_ring.arrive(2)
     cot_ring.start(3)
@@ -553,16 +598,20 @@
         cot_ring.sent(k)
     for k in range(hops):
         a_sent(k)
+        m_sent(k)
+    for k in range(hops - 1):
         b_sent(k)
     for copy in outs + [keep_copy]:
         copy.wait()
 
 
-def front(z_size, taps, rank, tokens, gain, ids, rows, cot, conv, gate, out, mats):
+def front(z_size, taps, rank, tokens, gain, ids, rows, cot, weight_in, out, select, step):
     length, width = tokens.shape
     shares = z_size * 4
-    chans = conv.shape[2]
-    wide = mats.shape[1] - rank
+    half = rows.shape[1]
+    chans = half * z_size
+    wide = select.shape[1] + -select.shape[1] % 128
+    cuts = 1 if weight_in.ndim == 4 else z_size
     any_space = pl.BlockSpec(memory_space=pl.ANY)
     vmem = pl.BlockSpec(memory_space=pltpu.VMEM)
     dma = pltpu.SemaphoreType.DMA
@@ -573,29 +622,28 @@
     block = (length, wide)
     return pl.pallas_call(
         functools.partial(front_kernel, z_size, taps, rank),
-        in_specs=[vmem] * 8 + [any_space],
-        out_specs=[any_space] * 12 + [vmem] * 3,
+        in_specs=[vmem] * 5 + [any_space] + [vmem] * 3,
+        out_specs=[any_space] * 11 + [vmem] * 3,
         out_shape=[
             shape(everyone, BF16),
             shape(everyone, BF16),
             shape((width, chans), BF16),
             shape((width, chans), BF16),
             shape((chans, width), BF16),
-            shape((chans, mats.shape[1]), BF16),
+            shape((chans, wide + rank), BF16),
             shape((length, 8, 128), F32),
             shape(per_token, F32),
             shape(per_token, F32),
             shape(per_token, F32),
             shape(per_token, F32),
-            shape((length * 8, chans), BF16),
             shape((rows.shape[0], chans), F32),
-            shape((shares,) + gain.shape, F32),
+            shape((gain.shape[0], width), F32),
             shape((4, 2) + block, BF16),
         ],
         scratch_shapes=[
             pltpu.VMEM(everyone, BF16),
             pltpu.VMEM((width, chans), BF16),
-            pltpu.VMEM((chans, mats.shape[1]), BF16),
+            pltpu.VMEM((chans, wide + rank), BF16),
             pltpu.VMEM((z_size,) + rows.shape, BF16),
             pltpu.VMEM((shares,) + gain.shape, F32),
             pltpu.VMEM((8,) + ids.shape, ids.dtype),
@@ -611,15 +659,17 @@
             pltpu.VMEM((4,) + block, BF16),
             pltpu.VMEM((3,) + block, BF16),
             pltpu.VMEM((3,) + block, BF16),
-            dma((14,)),
+            dma((13,)),
+            dma((2, cuts)),
             dma((shares - 1,)),
             dma((shares - 1,)),
             dma((7,)),
             dma((7,)),
         ]
-        + [dma((3,))] * 4
+        + [dma((3, cuts))] * 4
         + [dma((RING - 1, 2)), dma((RING - 1, 2)), dma((RING,)), dma((RING,))] * 2
-        + [dma((hops, 3))] * 4
+        + [dma((hops, 2))] * 4
+        + [dma((hops, 1))] * 4
         + [dma((hops, 2))] * 4
         + [dma((1,))] * 2
         + [dma((3,))] * 4
@@ -628,7 +678,7 @@
         compiler_params=pltpu.CompilerParams(
             collective_id=0, has_side_effects=True, vmem_limit_bytes=60 << 20
         ),
-    )(tokens, gain, ids, rows, cot, conv, gate, out, mats)
+    )(tokens, gain, ids, rows, cot, weight_in, out, select, step)
 
 
 def add_rows(dst, srcs, rows):
@@ -646,6 +696,8 @@
 
 
 def forward_kernel(
+    z_size,
+    chunks,
     states,
     rank,
     skip_row,
@@ -656,9 +708,11 @@
     rate_ref,
     normed_ref,
     cot_ref,
-    gate_w_ref,
-    out_w_ref,
+    normed_col,
+    cot_col,
     params_ref,
+    gate_given,
+    out_given,
     hist_ref,
     last_ref,
     ds_ref,
@@ -666,6 +720,8 @@
     part_ref,
     gout_ref,
     ggate_ref,
+    gate_all,
+    out_all,
     h_ref,
     bc_ref,
     y_ref,
@@ -673,141 +729,209 @@
     gate_ref,
     bg_ref,
     gated_ref,
-    gout_acc,
-    ggate_acc,
+    gated_all,
+    bgi_all,
+    gate_w_ref,
+    out_w_ref,
+    load_sem,
+    up_s,
+    up_r,
+    down_s,
+    down_r,
 ):
-    chunk = pl.program_id(0)
-
-    @pl.when(chunk == 0)
+    step = pl.program_id(0)
+    me = place()
+    z = me["z"]
+    hops = z_size - 1
+    slab_rows = gate_all.shape[0] // z_size
+    half = out_all.shape[0] // z_size
+    line_start, line_arrive, line_sent = z_line(
+        z,
+        z_size,
+        [
+            lambda k: gate_all.at[pl.ds(pl.multiple_of(k * slab_rows, slab_rows), slab_rows)],
+            lambda k: out_all.at[pl.ds(pl.multiple_of(k * half, half), half)],
+        ],
+        (up_s, up_r, down_s, down_r),
+    )
+
+    @pl.when(step == 0)
     def _():
+        greet([{"z": (z + 1) % z_size}, {"z": (z + z_size - 1) % z_size}])
+        line_start(hops - 1)
         h_ref[...] = jnp.zeros_like(h_ref)
-        gout_acc[...] = jnp.zeros_like(gout_acc)
-        ggate_acc[...] = jnp.zeros_like(ggate_acc)
 
     steps, seqs, width = dt_ref.shape
     groups = width // 128
     rows = steps * seqs
-    bc_ref[...] = sel_ref[:, rank:].astype(F32).reshape(bc_ref.shape)
-
-    def body(tb, carry):
-        t0 = tb * INNER
-        bc = [bc_ref[t0 + i] for i in range(INNER)]
-        off = [(1.0 - keep_ref[t0 + i]) * BIG for i in range(INNER)]
-        for g in range(groups):
-            lanes = pl.ds(g * 128, 128)
-            dt = [dt_ref[t0 + i, :, lanes] for i in range(INNER)]
-            dtm = [dt[i] + off[i] for i in range(INNER)]
-            u = [dt[i] * x_ref[t0 + i, :, lanes] for i in range(INNER)]
-            y = [None] * INNER
-            for n in range(states):
-                h = h_ref[n, :, lanes]
-                rate = rate_ref[n, :, lanes]
+    @pl.when(step < chunks)
+    def _():
+        bc_ref[...] = sel_ref[:, rank:].astype(F32).reshape(bc_ref.shape)
+
+        def body(tb, carry):
+            t0 = tb * INNER
+            bc = [bc_ref[t0 + i] for i in range(INNER)]
+            off = [(1.0 - keep_ref[t0 + i]) * BIG for i in range(INNER)]
+            for g in range(groups):
+                lanes = pl.ds(g * 128, 128)
+                dt = [dt_ref[t0 + i, :, lanes] for i in range(INNER)]
+                dtm = [dt[i] + off[i] for i in range(INNER)]
+                u = [dt[i] * x_ref[t0 + i, :, lanes] for i in range(INNER)]
+                y = [None] * INNER
+                for n in range(states):
+                    h = h_ref[n, :, lanes]
+                    rate = rate_ref[n, :, lanes]
+                    before = []
+                    for i in range(INNER):
+                        before.append(h)
+                        a = jnp.exp2(dtm[i] * rate)
+                        h = a * h + u[i] * bc[i][:, n : n + 1]
+                        term = h * bc[i][:, states + n : states + n + 1]
+                        y[i] = term if y[i] is None else y[i] + term
+                    for i in range(0, INNER, 2):
+                        pair = jnp.concatenate(before[i : i + 2], axis=0).astype(BF16)
+                        hist_ref[t0 // 2 + i // 2, n, :, lanes] = pair
+                    h_ref[n, :, lanes] = h
+                skip = params_ref[skip_row : skip_row + 1, lanes]
                 for i in range(INNER):
-                    hist_ref[t0 + i, n, :, lanes] = h
-                    a = jnp.exp2(dtm[i] * rate)
-                    h = a * h + u[i] * bc[i][:, n : n + 1]
-                    term = h * bc[i][:, states + n : states + n + 1]
-                    y[i] = term if y[i] is None else y[i] + term
-                h_ref[n, :, lanes] = h
-            skip = params_ref[skip_row : skip_row + 1, lanes]
-            for i in range(INNER):
-                y_ref[t0 + i, :, lanes] = y[i] + skip * x_ref[t0 + i, :, lanes]
-        return carry
-
-    lax.fori_loop(0, steps // INNER, body, 0)
-    last_ref[...] = h_ref[...]
-
-    normed = normed_ref[...].reshape(rows, normed_ref.shape[2])
-    cot = cot_ref[...].reshape(rows, cot_ref.shape[2])
-    gate_ref[...] = dot_nn(normed, gate_w_ref[...])
-    bg_ref[...] = dot_nt(cot, out_w_ref[...]).astype(BF16).astype(F32)
-    ys_ref[...] = jnp.swapaxes(y_ref[...], 0, 1).reshape(rows, width)
-    fine = 16
-
-    def gating(i, carry):
-        r = pl.ds(pl.multiple_of(i * fine, fine), fine)
-        v = gate_ref[r, :]
-        bg = bg_ref[r, :]
-        y = ys_ref[r, :]
-        s = 1.0 / (1.0 + jnp.exp(-v))
-        gate = v * s
-        gated_ref[r, :] = (y * gate).astype(BF16)
-        bg_ref[r, :] = bg * gate
-        gate_ref[r, :] = bg * y * (s * (1.0 + v * (1.0 - s)))
-        return carry
-
-    lax.fori_loop(0, rows // fine, gating, 0)
-    ds_ref[...] = jnp.swapaxes(bg_ref[...].reshape(seqs, steps, width), 0, 1)
-    bgi = gate_ref[...].astype(BF16)
-    bgi_ref[...] = bgi.reshape(bgi_ref.shape)
-    gated = gated_ref[...]
-    part_ref[...] = dot_nn(gated, out_w_ref[...]).astype(BF16).reshape(part_ref.shape)
-    gout_acc[...] += dot_tn(gated, cot)
-    ggate_acc[...] += dot_tn(normed, bgi)
-
-    @pl.when(chunk == pl.num_programs(0) - 1)
+                    y_ref[step * steps + t0 + i, :, lanes] = y[i] + skip * x_ref[t0 + i, :, lanes]
+            return carry
+
+        lax.fori_loop(0, steps // INNER, body, 0)
+        last_ref[...] = h_ref[...]
+
+    @pl.when(step == chunks)
     def _():
-        gout_ref[...] = gout_acc[...].astype(BF16)
-        ggate_ref[...] = ggate_acc[...].astype(BF16)
-
-
-def scan_forward(rank, skip_row, dt, x, selection, keep, rate, normed, cot, gate_w, out_w, params):
+        line_arrive(hops - 1)
+        line_sent(hops - 1)
+        loads = [
+            pltpu.make_async_copy(gate_all, gate_w_ref, load_sem.at[0]),
+            pltpu.make_async_copy(out_all, out_w_ref, load_sem.at[1]),
+        ]
+        for copy in loads:
+            copy.start()
+        for copy in loads:
+            copy.wait()
+
+    @pl.when((step >= chunks) & (step < 2 * chunks))
+    def _():
+        normed = normed_ref[...].reshape(rows, normed_ref.shape[2])
+        cot = cot_ref[...].reshape(rows, cot_ref.shape[2])
+        gate_ref[...] = dot_nn(normed, gate_w_ref[...])
+        bg_ref[...] = dot_nt(cot, out_w_ref[...]).astype(BF16).astype(F32)
+        y = y_ref[pl.ds((step - chunks) * steps, steps)]
+        ys_ref[...] = jnp.swapaxes(y, 0, 1).reshape(rows, width)
+        fine = 16
+
+        def gating(i, carry):
+            r = pl.ds(pl.multiple_of(i * fine, fine), fine)
+            v = gate_ref[r, :]
+            bg = bg_ref[r, :]
+            y = ys_ref[r, :]
+            s = sigmoid(v)
+            gate = v * s
+            gated_ref[r, :] = (y * gate).astype(BF16)
+            bg_ref[r, :] = bg * gate
+            gate_ref[r, :] = bg * y * (s + gate * (1.0 - s))
+            return carry
+
+        lax.fori_loop(0, rows // fine, gating, 0)
+        ds_ref[...] = jnp.swapaxes(bg_ref[...].reshape(seqs, steps, width), 0, 1)
+        bgi = gate_ref[...].astype(BF16).reshape(bgi_ref.shape)
+        bgi_ref[...] = bgi
+        gated = gated_ref[...]
+        part_ref[...] = dot_nn(gated, out_w_ref[...]).astype(BF16).reshape(part_ref.shape)
+        at = pl.ds(pl.multiple_of((step - chunks) * steps, steps), steps)
+        gated_all[:, at, :] = gated.reshape(bgi_ref.shape)
+        bgi_all[:, at, :] = bgi
+
+    @pl.when(step >= 2 * chunks)
+    def _():
+        tall = (gated_all.shape[0] * gated_all.shape[1], width)
+        cols = (tall[0], normed_col.shape[2])
+        gout_ref[...] = dot_tn(gated_all[...].reshape(tall), cot_col[...].reshape(cols)).astype(BF16)
+        ggate_ref[...] = dot_tn(normed_col[...].reshape(cols), bgi_all[...].reshape(tall)).astype(BF16)
+
+
+def scan_forward(z_size, rank, skip_row, dt, x, selection, keep, rate, normed, cot, gate_w, out_w, params):
     length, seqs, width = dt.shape
     model = normed.shape[2]
     states = rate.shape[0]
     wide = selection.shape[1]
-    block = lambda *tail: pl.BlockSpec((STEPS,) + tail, lambda i: (i,) + (0,) * len(tail))
-    across = lambda n: pl.BlockSpec((seqs, STEPS, n), lambda i: (0, i, 0))
+    chunks = length // STEPS
+    early = lambda i: jnp.minimum(i, chunks - 1)
+    late = lambda i: jnp.clip(i - chunks, 0, chunks - 1)
+    pieces = model // COLUMNS
+    last_of = lambda i: jnp.maximum(i - 2 * chunks, 0)
+    column = pl.BlockSpec((seqs, length, COLUMNS), lambda i: (0, 0, last_of(i)))
+    block = lambda *tail: pl.BlockSpec((STEPS,) + tail, lambda i: (early(i),) + (0,) * len(tail))
+    across = lambda n: pl.BlockSpec((seqs, STEPS, n), lambda i: (0, late(i), 0))
+    any_space = pl.BlockSpec(memory_space=pl.ANY)
+    dma = pltpu.SemaphoreType.DMA
+    hops = z_size - 1
     whole = lambda *dims: pl.BlockSpec(dims, lambda i: (0,) * len(dims))
     rows = STEPS * seqs
     shape = jax.ShapeDtypeStruct
     return pl.pallas_call(
-        functools.partial(forward_kernel, states, rank, skip_row),
-        grid=(length // STEPS,),
+        functools.partial(forward_kernel, z_size, chunks, states, rank, skip_row),
+        grid=(2 * chunks + pieces,),
         in_specs=[
             block(seqs, width),
             block(seqs, width),
-            pl.BlockSpec((rows, wide), lambda i: (i, 0)),
+            pl.BlockSpec((rows, wide), lambda i: (early(i), 0)),
             block(seqs, 128),
             whole(states, seqs, width),
             across(model),
             across(model),
-            whole(model, width),
-            whole(width, model),
+            column,
+            column,
             whole(*params.shape),
+            any_space,
+            any_space,
         ],
         out_specs=[
-            block(states, seqs, width),
+            pl.BlockSpec((STEPS // 2, states, 2 * seqs, width), lambda i: (early(i), 0, 0, 0)),
             whole(states, seqs, width),
-            block(seqs, width),
+            pl.BlockSpec((STEPS, seqs, width), lambda i: (late(i), 0, 0)),
             across(width),
             across(model),
-            whole(width, model),
-            whole(model, width),
+            pl.BlockSpec((width, COLUMNS), lambda i: (0, last_of(i))),
+            pl.BlockSpec((COLUMNS, width), lambda i: (last_of(i), 0)),
+            any_space,
+            any_space,
         ],
         out_shape=[
-            shape((length, states, seqs, width), F32),
+            shape((length // 2, states, 2 * seqs, width), BF16),
             shape((states, seqs, width), F32),
             shape(dt.shape, F32),
             shape((seqs, length, width), BF16),
             shape((seqs, length, model), BF16),
             shape((width, model), BF16),
             shape((model, width), BF16),
+            shape(gate_w.shape, BF16),
+            shape(out_w.shape, BF16),
         ],
+        input_output_aliases={10: 7, 11: 8},
         scratch_shapes=[
             pltpu.VMEM((states, seqs, width), F32),
             pltpu.VMEM((STEPS, seqs, wide - rank), F32),
-            pltpu.VMEM((STEPS, seqs, width), F32),
+            pltpu.VMEM((length, seqs, width), F32),
             pltpu.VMEM((rows, width), F32),
             pltpu.VMEM((rows, width), F32),
             pltpu.VMEM((rows, width), F32),
             pltpu.VMEM((rows, width), BF16),
-            pltpu.VMEM((width, model), F32),
-            pltpu.VMEM((model, width), F32),
-        ],
+            pltpu.VMEM((seqs, length, width), BF16),
+            pltpu.VMEM((seqs, length, width), BF16),
+            pltpu.VMEM(gate_w.shape, BF16),
+            pltpu.VMEM(out_w.shape, BF16),
+            dma((2,)),
+        ]
+        + [dma((hops, 2))] * 4,
         cost_estimate=busy(60),
-        compiler_params=pltpu.CompilerParams(vmem_limit_bytes=60 << 20),
-    )(dt, x, selection, keep, rate, normed, cot, gate_w, out_w, params)
+        compiler_params=pltpu.CompilerParams(
+            collective_id=5, has_side_effects=True, vmem_limit_bytes=60 << 20
+        ),
+    )(dt, x, selection, keep, rate, normed, cot, normed, cot, params, gate_w, out_w)
 
 
 def z_sums(z, z_size, owns, ups, downs, sems, blocks):
@@ -911,8 +1035,7 @@
     out_fin,
     ag_ref,
     h_ref,
-    pb_ref,
-    pc_ref,
+    p_ref,
     bc_ref,
     bp_ref,
     gate_own,
@@ -945,9 +1068,10 @@
     @pl.when(chunk == 0)
     def _():
         greet([{"z": (z + 1) % z_size}, {"z": (z + z_size - 1) % z_size}])
+        early = pl.ds(0, out_own.shape[2])
         loads = [
             pltpu.make_async_copy(gate_hbm, gate_own, local_sem.at[0]),
-            pltpu.make_async_copy(out_hbm, out_own, local_sem.at[1]),
+            pltpu.make_async_copy(out_hbm.at[:, :, early], out_own, local_sem.at[1]),
         ]
         for copy in loads:
             copy.start()
@@ -962,80 +1086,96 @@
 
     for tau in range(hops):
 
-        @pl.when(chunk == -(-tau * chunks_all // hops))
+        @pl.when(chunk == -(-tau * (chunks_all - 1) // hops))
         def _():
             line(tau, 0)
             line(tau, 1)
 
     steps, seqs, width = dt_ref.shape
     groups = width // 128
-    blocks = steps // INNER
+    blocks = steps // BACK_INNER
     bc_ref[...] = sel_ref[:, rank:].astype(F32).reshape(bc_ref.shape)
 
+    inner = BACK_INNER
+
     def body(back, carry):
-        t0 = (blocks - 1 - back) * INNER
-        rows = pl.ds(pl.multiple_of(t0 * seqs, INNER * seqs), INNER * seqs)
-        bc = [bc_ref[t0 + i] for i in range(INNER)]
-        off = [(1.0 - keep_ref[t0 + i]) * BIG for i in range(INNER)]
-        for g in range(groups):
-            lanes = pl.ds(g * 128, 128)
-            dt = [dt_ref[t0 + i, :, lanes] for i in range(INNER)]
-            dtm = [dt[i] + off[i] for i in range(INNER)]
-            ds = [ds_ref[t0 + i, :, lanes] for i in range(INNER)]
-            u = [dt[i] * x_ref[t0 + i, :, lanes] for i in range(INNER)]
-            s1 = [None] * INNER
-            s2 = [None] * INNER
+        t0 = (blocks - 1 - back) * inner
+        rows = pl.ds(pl.multiple_of(t0 * seqs, inner * seqs), inner * seqs)
+        bc = [bc_ref[t0 + i] for i in range(inner)]
+        off = [(1.0 - keep_ref[t0 + i]) * BIG for i in range(inner)]
+        for g0 in range(0, groups, TOGETHER):
+            lanes = [pl.ds((g0 + q) * 128, 128) for q in range(TOGETHER)]
+            each = [(q, i) for q in range(TOGETHER) for i in range(inner)]
+            dt = {(q, i): dt_ref[t0 + i, :, lanes[q]] for q, i in each}
+            dtm = {(q, i): dt[q, i] + off[i] for q, i in each}
+            ds = {(q, i): ds_ref[t0 + i, :, lanes[q]] for q, i in each}
+            u = {(q, i): dt[q, i] * x_ref[t0 + i, :, lanes[q]] for q, i in each}
+            s1 = {}
+            s2 = {}
             for n in range(states):
-                ag = ag_ref[n, :, lanes]
-                h = h_ref[n, :, lanes]
-                rate = rate_ref[n, :, lanes]
-                da = da_ref[n, :, lanes]
-                pb = [None] * INNER
-                pc = [None] * INNER
-                for i in reversed(range(INNER)):
-                    prev = hist_ref[t0 + i, n, :, lanes]
-                    a = jnp.exp2(dtm[i] * rate)
-                    adj = ds[i] * bc[i][:, states + n : states + n + 1] + ag
-                    pc[i] = ds[i] * h
-                    pb[i] = adj * u[i]
-                    ag = a * adj
-                    w = ag * prev
-                    rw = rate * w
-                    gb = adj * bc[i][:, n : n + 1]
-                    s1[i] = rw if s1[i] is None else s1[i] + rw
-                    s2[i] = gb if s2[i] is None else s2[i] + gb
-                    da = da + dt[i] * w
-                    h = prev
-                ag_ref[n, :, lanes] = ag
-                h_ref[n, :, lanes] = h
-                da_ref[n, :, lanes] = da
-                cols = pl.ds((g * states + n) * 128, 128)
-                pb_ref[rows, cols] = jnp.concatenate(pb, axis=0).astype(BF16)
-                pc_ref[rows, cols] = jnp.concatenate(pc, axis=0).astype(BF16)
-            skip = params_ref[skip_row : skip_row + 1, lanes]
-            bias = bias_ref[:, lanes]
-            direct = skip_ref[:, lanes]
-            low = []
-            for i in range(INNER):
-                x = x_ref[t0 + i, :, lanes]
-                bx_ref[t0 + i, :, lanes] = dt[i] * s2[i] + skip * ds[i]
-                back = (s1[i] * (1.0 / LOG2E) + x * s2[i]) / (1.0 + jnp.exp(-pre_ref[t0 + i, :, lanes]))
-                low.append(back)
-                bias = bias + back
-                direct = direct + ds[i] * x
-            bias_ref[:, lanes] = bias
-            skip_ref[:, lanes] = direct
-            bp_ref[rows, lanes] = jnp.concatenate(low, axis=0).astype(BF16)
+                pb = [None] * inner
+                pc = [None] * inner
+                for q in range(TOGETHER):
+                    ag = ag_ref[n, :, lanes[q]]
+                    h = h_ref[n, :, lanes[q]]
+                    rate = rate_ref[n, :, lanes[q]]
+                    da = da_ref[n, :, lanes[q]]
+                    before = []
+                    for i in range(0, inner, 2):
+                        pair = hist_ref[t0 // 2 + i // 2, n, :, lanes[q]].astype(F32)
+                        before += [pair[:seqs], pair[seqs:]]
+                    for i in reversed(range(inner)):
+                        prev = before[i]
+                        a = jnp.exp2(dtm[q, i] * rate)
+                        adj = ds[q, i] * bc[i][:, states + n : states + n + 1] + ag
+                        c_term = ds[q, i] * h
+                        b_term = adj * u[q, i]
+                        pc[i] = c_term if q == 0 else pc[i] + c_term
+                        pb[i] = b_term if q == 0 else pb[i] + b_term
+                        ag = a * adj
+                        w = ag * prev
+                        rw = rate * w
+                        gb = adj * bc[i][:, n : n + 1]
+                        s1[q, i] = rw if n == 0 else s1[q, i] + rw
+                        s2[q, i] = gb if n == 0 else s2[q, i] + gb
+                        da = da + dt[q, i] * w
+                        h = prev
+                    ag_ref[n, :, lanes[q]] = ag
+                    h_ref[n, :, lanes[q]] = h
+                    da_ref[n, :, lanes[q]] = da
+                cols = pl.ds(n * 128, 128)
+                p_ref[0, g0 // TOGETHER, rows, cols] = jnp.concatenate(pb, axis=0).astype(BF16)
+                p_ref[1, g0 // TOGETHER, rows, cols] = jnp.concatenate(pc, axis=0).astype(BF16)
+            for q in range(TOGETHER):
+                skip = params_ref[skip_row : skip_row + 1, lanes[q]]
+                bias = bias_ref[:, lanes[q]]
+                direct = skip_ref[:, lanes[q]]
+                low = []
+                for i in range(inner):
+                    x = x_ref[t0 + i, :, lanes[q]]
+                    bx_ref[t0 + i, :, lanes[q]] = dt[q, i] * s2[q, i] + skip * ds[q, i]
+                    back_step = s1[q, i] * (1.0 / LOG2E) + x * s2[q, i]
+                    back_pre = back_step / (1.0 + jnp.exp(-pre_ref[t0 + i, :, lanes[q]]))
+                    low.append(back_pre)
+                    bias = bias + back_pre
+                    direct = direct + ds[q, i] * x
+                bias_ref[:, lanes[q]] = bias
+                skip_ref[:, lanes[q]] = direct
+                bp_ref[rows, lanes[q]] = jnp.concatenate(low, axis=0).astype(BF16)
         return carry
 
     lax.fori_loop(0, blocks, body, 0)
     span = states * 128
-    total = jnp.zeros((steps * seqs, 128), F32)
-    for g in range(groups):
-        total = total + dot_nn(pb_ref[:, pl.ds(g * span, span)], ones_ref[0])
-        total = total + dot_nn(pc_ref[:, pl.ds(g * span, span)], ones_ref[1])
-    part_ref[:, rank:] = total
-    part_ref[:, :rank] = dot_nn(bp_ref[...], step_w_ref[...])
+    sets = groups // TOGETHER
+    folded = dot_nn(p_ref[...].reshape(2 * sets * steps * seqs, span), ones_ref[...])
+    folded = folded.reshape(2, sets, steps * seqs, 128)
+    in_sum = folded[0, 0]
+    out_sum = folded[1, 0]
+    for g in range(1, sets):
+        in_sum = in_sum + folded[0, g]
+        out_sum = out_sum + folded[1, g]
+    part_ref[:, rank:] = (in_sum + pltpu.roll(out_sum, states, 1)).astype(BF16)
+    part_ref[:, :rank] = dot_nn(bp_ref[...], step_w_ref[...]).astype(BF16)
     gstep_ref[...] += dot_tn(bp_ref[...], sel_ref[:, :rank])
 
     @pl.when(chunk == chunks - 1)
@@ -1059,11 +1199,10 @@
     whole = lambda *dims: pl.BlockSpec(dims, lambda i: (0,) * len(dims))
     any_space = pl.BlockSpec(memory_space=pl.ANY)
     span = states * 128
-    entry = jnp.arange(span)[:, None] // 128
-    column = jnp.arange(128)[None, :]
-    ones = jnp.stack([entry == column, entry + states == column]).astype(BF16)
+    ones = jnp.asarray((np.arange(span)[:, None] // 128 == np.arange(128)[None, :]).astype(np.float32), BF16)
     hops = z_size - 1
-    gate_shape, out_shape = gate.shape[1:], out.shape[1:]
+    gate_shape = gate.shape[1:]
+    out_shape = (out.shape[1], out.shape[2] // 2)
     shape = jax.ShapeDtypeStruct
     dma = pltpu.SemaphoreType.DMA
     return pl.pallas_call(
@@ -1077,11 +1216,11 @@
             flat(wide),
             block(seqs, 128),
             whole(states, seqs, width),
-            block(states, seqs, width),
+            pl.BlockSpec((STEPS // 2, states, 2 * seqs, width), lambda i: (chunks - 1 - i, 0, 0, 0)),
             whole(states, seqs, width),
-            whole(2, span, 128),
+            whole(span, 128),
             whole(*params.shape),
-            whole(width, rank),
+            pl.BlockSpec((width, rank), lambda i: (0, wide // rank)),
             any_space,
             any_space,
         ],
@@ -1097,7 +1236,7 @@
         ],
         out_shape=[
             shape(dt.shape, F32),
-            shape((length * seqs, wide), F32),
+            shape((length * seqs, wide), BF16),
             shape((states, seqs, width), F32),
             shape((width, rank), F32),
             shape((seqs, width), F32),
@@ -1108,12 +1247,11 @@
         scratch_shapes=[
             pltpu.VMEM((states, seqs, width), F32),
             pltpu.VMEM((states, seqs, width), F32),
-            pltpu.VMEM((rows, width // 128 * span), BF16),
-            pltpu.VMEM((rows, width // 128 * span), BF16),
+            pltpu.VMEM((2, width // 128 // TOGETHER, rows, span), BF16),
             pltpu.VMEM((STEPS, seqs, wide - rank), F32),
             pltpu.VMEM((rows, width), BF16),
             pltpu.VMEM(gate.shape, BF16),
-            pltpu.VMEM(out.shape, BF16),
+            pltpu.VMEM(out.shape[:1] + out_shape, BF16),
             pltpu.VMEM((hops,) + gate_shape, BF16),
             pltpu.VMEM((hops,) + out_shape, BF16),
             pltpu.VMEM((hops,) + gate_shape, BF16),
@@ -1149,11 +1287,11 @@
     gain_ref,
     bx_hbm,
     cin_hbm,
-    picked_hbm,
     normed_hbm,
     conv_hbm,
     gate_hbm,
     bgi_hbm,
+    gout_hbm,
     tgrad_ref,
     in_ref,
     out_ref,
@@ -1161,7 +1299,6 @@
     vec_out,
     gain_out,
     chosen,
-    first,
     from_sib,
     stage,
     got,
@@ -1189,6 +1326,9 @@
     down_small,
     down_vec,
     down_conv,
+    own_out,
+    up_out,
+    down_out,
     fin_conv,
     both_gate,
     both_conv,
@@ -1214,6 +1354,10 @@
     up_recv,
     down_send,
     down_recv,
+    out_us,
+    out_ur,
+    out_ds,
+    out_dr,
     swap_send,
     swap_recv,
     x_send,
@@ -1231,9 +1375,12 @@
     length, width = tokens_ref.shape
     chans = bx.shape[2]
     rows_in = in_ref.shape[0]
-    half = out_fin.shape[0]
+    half = own_out.shape[1]
     hops = z_size - 1
     wide = part_ref.shape[3]
+    out_line, out_settle, out_sent = z_sums(
+        z, z_size, (own_out,), (up_out,), (down_out,), (out_us, out_ur, out_ds, out_dr), (16,)
+    )
     greet(plane_others(me) + z_only(me, shares))
 
     loads = [
@@ -1242,19 +1389,22 @@
             [
                 (cin_hbm, cin.at[pl.ds(3, length)]),
                 (bx_hbm, bx.at[pl.ds(0, length)]),
-                (picked_hbm, picked),
                 (bgi_hbm, bgi),
                 (conv_hbm, conv_w),
                 (gate_hbm, gate_w),
             ]
         )
     ]
+    later = pl.ds(own_out.shape[2], own_out.shape[2])
+    out_load = pltpu.make_async_copy(gout_hbm.at[:, :, later], own_out, local_sem.at[6])
+    out_load.start()
+
+    swap = remote(part_ref.at[:, 1 - c], from_sib, sw_s.at[0], sw_r.at[0], sibling)
+    swap.start()
     for copy in loads:
         copy.start()
-
-    first[...] = part_ref[:, 1 - c].astype(BF16)
-    swap = remote(first, from_sib, sw_s.at[0], sw_r.at[0], sibling)
-    swap.start()
+    out_load.wait()
+    out_line(0, 0)
     cin[0:3] = jnp.zeros((3, 8, chans), F32)
     bx[length : length + 3] = jnp.zeros((3, 8, chans), F32)
     sums[...] = jnp.zeros_like(sums)
@@ -1266,11 +1416,13 @@
     for k in (2, 1, 0):
         ox, oy = chips[k]
         j = ox * 2 + oy
-        stage[k] = (part_ref[j, c] + from_sib[j].astype(F32)).astype(BF16)
+        stage[k] = (part_ref[j, c].astype(F32) + from_sib[j].astype(F32)).astype(BF16)
         copy = remote(stage.at[k], got.at[k], rs_s.at[k], rs_r.at[k], {"x": ox, "y": oy})
         copy.start()
         sends.append(copy)
-    total = part_ref[mine, c] + from_sib[mine].astype(F32)
+    total = part_ref[mine, c].astype(F32) + from_sib[mine].astype(F32)
+    if hops > 1:
+        out_line(1, 0)
     for copy in sends:
         copy.wait()
     for k in range(3):
@@ -1288,25 +1440,23 @@
 
     def corner_sends(src, dst, index):
         out = []
-        for k in range(1, 4):
-            to = (corner + k) % 4
+        for e in range(1, 8):
+            to = (corner + e % 4) % 4
             out.append(
                 remote(
                     src.at[pl.ds(pl.multiple_of(to * rows_in, rows_in), rows_in)],
                     dst.at[x, corner],
-                    swap_send.at[index, k - 1],
-                    swap_recv.at[index, k - 1],
-                    {"y": to // 2, "c": to % 2},
+                    swap_send.at[index, e - 1],
+                    swap_recv.at[index, e - 1],
+                    {"x": (x + e // 4) % 2, "y": to // 2, "c": to % 2},
                 )
             )
         return out
 
     gate_swaps = corner_sends(gate_fin, both_gate, 0)
     conv_swaps = corner_sends(fin_conv, both_conv, 1)
-    for copy in gate_swaps:
-        copy.start()
     both_gate[x, corner] = gate_fin[pl.ds(pl.multiple_of(corner * rows_in, rows_in), rows_in)]
-    out_ref[x] = out_fin[...]
+    out_ref[x, :, : own_out.shape[2]] = out_fin[...]
     out_x = remote(out_ref.at[x], out_ref.at[x], x_send.at[0], x_recv.at[0], over_x)
     for k, copy in reversed(spreads):
         copy.wait_recv()
@@ -1314,13 +1464,16 @@
         there = chosen.at[ox * 2 + oy, c]
         forwards.append(remote(there, there, fw_s.at[k], fw_r.at[k], sibling))
         forwards[-1].start()
-    out_x.start()
     for copy in loads:
         copy.wait()
     for _, copy in spreads:
         copy.wait_send()
     for copy in forwards:
         copy.wait()
+    for copy in gate_swaps:
+        copy.start()
+    for tau in range(2, hops):
+        out_line(tau, 0)
 
     fine = 4
     block = length // 8
@@ -1331,18 +1484,16 @@
         ]
 
     def select(b, carry):
-        rows = pl.ds(pl.multiple_of(b * length, length), length)
         back = chosen[b // 2, b % 2]
         t0 = b * block
         bx[pl.ds(t0, block)] += dot_nt(back, mats_ref[:, :wide]).reshape(block, 8, chans)
-        gsel[...] += dot_tn(picked[rows, :], back)
-
         def convolve(i, carry):
             for g in range(chans // 128):
                 lanes = pl.ds(g * 128, 128)
                 tap = taps_of(lanes)
                 offset = jnp.broadcast_to(params_ref[taps : taps + 1, lanes], (8, 128))
                 acc = [sums[r, :, lanes] for r in range(taps + 1)]
+                taken = []
                 for j in range(fine):
                     t = t0 + i * fine + j
                     k0 = keep_ref[t]
@@ -1353,8 +1504,10 @@
                     v2 = cin[t + 1, :, lanes] * k1
                     v3 = cin[t, :, lanes] * k2
                     v = offset + tap[0] * v0 + tap[1] * v1 + tap[2] * v2 + tap[3] * v3
-                    s = 1.0 / (1.0 + jnp.exp(-v))
-                    back = bx[t, :, lanes] * (s * (1.0 + v * (1.0 - s)))
+                    s = sigmoid(v)
+                    silu = v * s
+                    taken.append(silu)
+                    back = bx[t, :, lanes] * (s + silu * (1.0 - s))
                     bx[t, :, lanes] = back
                     acc[0] = acc[0] + back * v0
                     acc[1] = acc[1] + back * v1
@@ -1363,16 +1516,15 @@
                     acc[4] = acc[4] + back
                 for r in range(taps + 1):
                     sums[r, :, lanes] = acc[r]
+                rows = pl.ds(pl.multiple_of(i * fine * 8, fine * 8), fine * 8)
+                picked[rows, lanes] = jnp.concatenate(taken, axis=0).astype(BF16)
             return carry
 
         lax.fori_loop(0, block // fine, convolve, 0)
+        gsel[...] += dot_tn(picked[...], back)
         return carry
 
     lax.fori_loop(0, 8, select, 0)
-    for copy in gate_swaps:
-        copy.wait()
-    gate_x = remote(both_gate.at[x], both_gate.at[x], x_send.at[1], x_recv.at[1], over_x)
-    gate_x.start()
 
     def unfold(b, carry):
         t0 = b * block
@@ -1403,6 +1555,8 @@
         return zz, pltpu.make_async_copy(normed_hbm.at[:, :, cols], columns.at[slot], column_sem.at[slot])
 
     column(0, 0)[1].start()
+    out_settle(0, out_ref.at[x, :, later])
+    out_x.start()
     lax.fori_loop(0, 8, unfold, 0)
 
     owns = (own_small, own_vec, own_conv)
@@ -1506,7 +1660,7 @@
             )
             values = tokens_ref[r].astype(F32)
             rstd = lax.rsqrt(jnp.mean(values * values, axis=-1, keepdims=True) + epsilon)
-            scaled = back * gain_ref[...]
+            scaled = back * gain_ref[0:1, :]
             inner = jnp.mean(scaled * values, axis=-1, keepdims=True)
             grad = cot_ref[r].astype(F32) + rstd * scaled - values * (rstd * rstd * rstd * inner)
             tgrad_ref[r] = grad.astype(BF16)
@@ -1547,22 +1701,18 @@
     ring_step(2)
     for tau in range(2, hops):
         lines(tau)
+
+    settle(2, fin_conv)
+    for copy in conv_swaps:
+        copy.start()
     ring_end()
     for copy in gains:
-        copy.start()
-
-    settle(2, fin_conv)
-    for copy in conv_swaps:
         copy.start()
     both_conv[x, corner] = fin_conv[pl.ds(pl.multiple_of(corner * rows_in, rows_in), rows_in)]
     settle(0, small_out.at[x])
     settle(1, vec_out.at[x])
     small_x = remote(small_out.at[x], small_out.at[x], x_send.at[2], x_recv.at[2], over_x)
     vec_x = remote(vec_out.at[x], vec_out.at[x], x_send.at[3], x_recv.at[3], over_x)
-    for copy in conv_swaps:
-        copy.wait()
-    conv_x = remote(both_conv.at[x], both_conv.at[x], x_send.at[4], x_recv.at[4], over_x)
-    conv_x.start()
     small_x.start()
     vec_x.start()
 
@@ -1580,16 +1730,19 @@
     gain_half[...] = jnp.sum(gain_got[...], axis=0)
     gain_x = remote(gain_half, gain_pair, x_send.at[5], x_recv.at[5], over_x)
     gain_x.start()
-    gate_x.wait()
+    for copy in gate_swaps:
+        copy.wait()
     lay(branch, both_gate)
     gain_x.wait()
     gain_out[...] = gain_half[...] + gain_pair[...]
-    conv_x.wait()
+    for copy in conv_swaps:
+        copy.wait()
     lay(0, both_conv)
     for copy in (out_x, small_x, vec_x):
         copy.wait()
     for j in range(3):
         sent(j)
+    out_sent(0)
     for k in range(RING - 1):
         for p in range(2):
             ring(k, p).wait_send()
@@ -1606,6 +1759,7 @@
     params,
     gate_fin,
     out_fin,
+    gout,
     da,
     gstep,
     bias,
@@ -1615,7 +1769,6 @@
     gain,
     bx,
     cin,
-    picked,
     normed,
     conv,
     gate,
@@ -1627,7 +1780,7 @@
     shares = z_size * 4
     hops = z_size - 1
     rows_in = gate_fin.shape[0] // 4
-    half = out_fin.shape[0]
+    half = gout.shape[1]
     wide = part.shape[3]
     any_space = pl.BlockSpec(memory_space=pl.ANY)
     vmem = pl.BlockSpec(memory_space=pltpu.VMEM)
@@ -1639,6 +1792,7 @@
     both = pltpu.VMEM((2, 4, rows_in, chans), BF16)
     piece = (8, width // shares)
     few = (length, wide)
+    late_out = (half, width // 2)
     return pl.pallas_call(
         functools.partial(last_kernel, z_size, taps),
         in_specs=[vmem] * 13 + [any_space] * 7,
@@ -1646,7 +1800,7 @@
         out_shape=[
             shape(tokens.shape, BF16),
             shape((rows_in, in_width), F32),
-            shape((2,) + out_fin.shape, BF16),
+            shape((2,) + gout.shape[1:], BF16),
             shape((2,) + slabs[0], BF16),
             shape((2,) + slabs[1], BF16),
             shape(piece, F32),
@@ -1654,12 +1808,11 @@
         scratch_shapes=[
             pltpu.VMEM((4, 2) + few, BF16),
             pltpu.VMEM((4,) + few, BF16),
-            pltpu.VMEM((4,) + few, BF16),
             pltpu.VMEM((3,) + few, BF16),
             pltpu.VMEM((3,) + few, BF16),
             pltpu.VMEM((length + 3, 8, chans), F32),
             pltpu.VMEM((length + 3, 8, chans), F32),
-            pltpu.VMEM(picked.shape, BF16),
+            pltpu.VMEM((length, chans), BF16),
             pltpu.VMEM(conv.shape, BF16),
             pltpu.VMEM(gate.shape, BF16),
             pltpu.VMEM(bgi.shape, BF16),
@@ -1677,6 +1830,9 @@
         + bufs(hops)
         + bufs(hops)
         + [
+            pltpu.VMEM((z_size,) + late_out, BF16),
+            pltpu.VMEM((hops,) + late_out, BF16),
+            pltpu.VMEM((hops,) + late_out, BF16),
             pltpu.VMEM(slabs[2], BF16),
             both,
             both,
@@ -1684,7 +1840,7 @@
             pltpu.VMEM((shares,) + piece, F32),
             pltpu.VMEM(piece, F32),
             pltpu.VMEM(piece, F32),
-            dma((6,)),
+            dma((7,)),
             dma((2,)),
             dma((1,)),
             dma((1,)),
@@ -1694,7 +1850,8 @@
         + [dma((RING,))] * 2
         + [dma((RING - 1, 2))] * 2
         + [dma((hops, 3))] * 4
-        + [dma((2, 3))] * 2
+        + [dma((hops, 1))] * 4
+        + [dma((2, 7))] * 2
         + [dma((6,))] * 2
         + [dma((shares - 1,))] * 2,
         cost_estimate=busy(120),
@@ -1717,11 +1874,11 @@
         gain,
         bx,
         cin,
-        picked,
         normed,
         conv,
         gate,
         bgi,
+        gout,
     )
 
 
@@ -1770,13 +1927,12 @@
         axis=1,
     ).T
     vectors = jnp.pad(vectors, ((0, -vectors.shape[0] % 32), (0, 0)))
-    mats = jnp.concatenate(
-        [jnp.pad(own_half(select_weight), ((0, 0), (0, spare))), own_half(step_weight)], axis=1
-    )
-    columns = lax.dynamic_index_in_dim(
-        in_weight.reshape(in_rows, 2, z_size, 4, 2, half), x_at, 4, keepdims=False
-    )
-    packed = columns.transpose(1, 3, 0, 2, 4).reshape(2, 4, in_rows, chans)
+    weight_in = in_weight
+    if half % 128:
+        columns = lax.dynamic_index_in_dim(
+            in_weight.reshape(in_rows, 2, z_size, 4, 2, half), x_at, 4, keepdims=False
+        )
+        weight_in = columns.transpose(1, 3, 0, 2, 4).reshape(2, 4, in_rows, chans)
     gain_tile = jnp.broadcast_to(norm_gain.astype(F32)[None, :], (8, norm_gain.shape[0]))
     ids_tile = jnp.broadcast_to(doc_ids, (8, length))
     (
@@ -1791,7 +1947,6 @@
         x,
         dt,
         pre,
-        picked,
         vectors,
         gains,
         selection,
@@ -1804,18 +1959,17 @@
         ids_tile,
         vectors,
         cotangent,
-        packed[0],
-        packed[1],
-        own_half(out_weight),
-        mats,
+        weight_in,
+        out_weight,
+        select_weight,
+        step_weight,
     )
-    gain = gains[:, 0, :].reshape(1, width)
     selection = selection.reshape(length * seqs, wide)
     rates = -jnp.exp(vectors[taps + 3 : taps + 3 + states])
     rate2 = jnp.broadcast_to((rates * LOG2E)[:, None, :], (states, seqs, chans))
 
-    hist, last, back_scan, back_gate_in, out_part, grad_out, grad_gate = scan_forward(
-        rank, taps + 2, dt, x, selection, keep, rate2, all_normed, all_cot, w_gate, w_out, vectors
+    hist, last, back_scan, back_gate_in, out_part, grad_out, grad_gate, w_gate, _ = scan_forward(
+        z_size, rank, taps + 2, dt, x, selection, keep, rate2, all_normed, all_cot, w_gate, w_out, vectors
     )
     layer_sum = lax.psum_scatter(
         out_part.reshape(-1, width), PLANE, scatter_dimension=0, tiled=True
@@ -1835,7 +1989,7 @@
         hist,
         last,
         vectors,
-        w_mats[:, wide:],
+        w_mats,
         grad_gate.reshape(z_size, -1, chans),
         grad_out.reshape(z_size, half, width),
     )
@@ -1848,16 +2002,16 @@
         vectors,
         gate_fin,
         out_fin,
+        grad_out.reshape(z_size, half, width),
         da,
         g_step,
         g_bias,
         g_skip,
         tokens,
         cotangent,
-        gain,
+        gains,
         back_x,
         conv_in,
-        picked,
         all_normed,
         w_conv,
         w_gate,

time: 454 us -> 418 us (0.921)
  Pallas kernels: 400 us -> 379 us
  local copies, waits for them, and re-layouts: 26.7 us -> 15.3 us
    pallas_call x1, Pallas kernels: 94.1 us -> 69.8 us  [scan_backward(): pl.pallas_call(functools.partial(backward_kernel, chunks, z_size, states,...]
    pallas_call x1, Pallas kernels: 60 us -> 79.3 us  [scan_forward(): pl.pallas_call(functools.partial(forward_kernel, z_size, chunks, states,...]
    pallas_call x1, Pallas kernels: 133 us -> 120 us  [front(): pl.pallas_call(functools.partial(front_kernel, z_size, taps, rank), in_sp...]
  transfers between devices with their start and end apart: 1 -> 1, of which waited for: 0 -> 0; matrix products, arithmetic and copies ran while one was open for 3% -> 2% of each run, Pallas kernels for 46% -> 43%
where the time goes in v4:
time: 418 us; the launch traced here: 415 us
  Pallas kernels  379 us (91%)
  local copies, waits for them, and re-layouts  15.3 us (4%)
  between operations  14.1 us (3%)
  other arithmetic  6.94 us (2%)
    pallas_call x1, Pallas kernels, front(): pl.pallas_call(functools.partial(front_kernel, z_size, taps, rank), in_sp...  120 us
    pallas_call x1, Pallas kernels, last_part(): pl.pallas_call(functools.partial(last_kernel, z_size, taps), in_specs=[vm...  110 us
    pallas_call x1, Pallas kernels, scan_forward(): pl.pallas_call(functools.partial(forward_kernel, z_size, chunks, states,...  79.3 us
    pallas_call x1, Pallas kernels, scan_backward(): pl.pallas_call(functools.partial(backward_kernel, chunks, z_size, states,...  69.8 us
  transfers between devices with their start and end apart: 1, of which 0 were waited for; matrix products, arithmetic and copies ran while one was open for 2% of the time, Pallas kernels for 43%

profile of v4, /device:TPU:11, one launch (start us, length us, event | category | flops | bytes accessed | tf_op | source)
XLA Modules:
  0.0 415.5 jit_solution(16145869730576344024)
XLA Ops:
  7.2 0.7 dynamic-slice_bitcast_fusion.2
  8.0 0.7 constant_dynamic-slice_fusion.1
  8.7 1.6 copy.30.select_ref
  10.3 0.7 dynamic-slice_bitcast_fusion
  11.2 0.6 pad.4.rows_ref
  11.8 1.2 broadcast_in_dim.28.gain_ref
  13.1 1.3 broadcast_in_dim.30.ids_ref
  14.4 120.0 %shard_map.229 = (bf16[8,256,2048]{2,1,0:T(8,128)(2,1)}, bf16[8,256,2048]{2,1,0:T(8,128)(2,1)}, bf16[2048,512]{1,0:T(8,128)(2,1)}, bf16[2048,512]{1,0:T(8,128)(2...) custom-call(bf16[256,2048]{1,0:T(8,128)(2,1)} %tokens_ref.3, ...), custom_call_target="tpu_custom_call" | custom-call | flops 120000004096 | bytes 120000000 | tf_op jit(solution)/shard_map/pallas_call | solution.py:623
  134.4 0.8 negate_multiply_fusion
  135.2 0.7 broadcast_in_dim.34.rate_ref
  135.9 79.3 %shard_map.230 = (bf16[128,16,16,512]{3,2,1,0:T(8,128)(2,1)}, f32[16,8,512]{2,1,0:T(8,128)}, f32[256,8,512]{2,1,0:T(8,128)}, bf16[8,256,512]{2,1,0:T(8,128)(2,1)...) custom-call(f32[256,8,512]{2,1,0:T(8,128)} %get-tuple-element.48.dt_, ...), custom_call_target="tpu_custom_call", output_to_operand_aliasing={{7}: (10, {}), {8}: (11, {})} | custom-call | flops 60000002048 | bytes 60000000 | tf_op jit(solution)/shard_map/pallas_call | solution.py:875
  215.3 69.8 %shard_map.231 = (f32[256,8,512]{2,1,0:T(8,128)}, bf16[2048,256]{1,0:T(8,128)(2,1)}, f32[16,8,512]{2,1,0:T(8,128)}, f32[512,128]{1,0:T(8,128)}, f32[8,512]{1,0:T...) custom-call(f32[256,8,512]{2,1,0:T(8,128)} %get-tuple-element.48.dt_ref, ...), custom_call_target="tpu_custom_call" | custom-call | flops 80000000000 | bytes 80000000 | tf_op jit(solution)/shard_map/pallas_call | solution.py:1208
  285.0 110.0 %shard_map.232 = (bf16[256,2048]{1,0:T(8,128)(2,1)}, f32[128,8192]{1,0:T(8,128)}, bf16[2,128,2048]{2,1,0:T(8,128)(2,1)}, bf16[2,128,384]{2,1,0:T(8,128)(2,1)}, b...) custom-call(bf16[4,2,256,256]{3,2,1,0:T(8,128)(2,1)} %bitcast.41, f32[256,8,128]{2,1,0:T(8,128)} %get-tuple-element.51.keep_ref, ...), custom_call_target="tpu_custom_call" | custom-call | flops 120000004096 | bytes 120000000 | tf_op jit(solution)/shard_map/pallas_call | solution.py:1796
  395.0 0.8 copy_bitcast_fusion
  395.9 0.6 slice.36
  396.5 0.6 slice.41
  397.1 1.0 bitcast_convert_fusion.1
  398.0 0.7 slice.39
  398.7 0.8 copy.32
  399.5 1.2 slice_bitcast_fusion
  401.2 1.6 bitcast_convert_fusion
  402.9 2.7 add_convert_fusion
  405.6 1.0 copy.39
  406.6 2.0 copy.40
  (19 shorter events, 0.8 us)
Async XLA Ops:
  7.2 1.5 copy-start
  7.2 395.7 %reduce-scatter.2.cloned.1.call-start = ((), (), s32[]{:S(2)}) async-start(), calls=%async_computation.1 | async-start | bytes 9437184 | tf_op jit(solution)/shard_map/reduce_scatter | solution.py:1974
  395.0 6.2 %copy-start.4 = (bf16[2,128,2048]{2,1,0:T(8,128)(2,1)S(1)}, bf16[2,128,2048]{2,1,0:T(8,128)(2,1)}, u32[]{:S(2)}) copy-start(bf16[2,128,2048]{2,1,0:T(8,128)(2,1)} %get-tuple-element.83) | copy-start | bytes 3145732
  398.7 4.2 %copy-start.3 = (bf16[256,2048]{1,0:T(8,128)(2,1)S(1)}, bf16[256,2048]{1,0:T(8,128)(2,1)}, u32[]{:S(2)}) copy-start(bf16[256,2048]{1,0:T(8,128)(2,1)} %tokens_ref.3) | copy-start | bytes 3145732
  402.9 2.8 copy-start.5
  402.9 3.7 copy-start.2
  406.6 2.0 copy-start.1
Sparse Core Ops, SparseCore 0:
  215.4 70.9 reduce-scatter.1

commit v5 on v4

--- a/solution.py
+++ b/solution.py
@@ -340,12 +340,14 @@
                 )
         return out
 
+    gain_got[share] = jnp.broadcast_to(gain_ref[...].astype(F32), gain_got.shape[1:])
+    ids_all[seq] = jnp.broadcast_to(ids_ref[...], ids_all.shape[1:])
     swaps = corner_sends(0, conv_w, conv_send, conv_recv)
     gates = corner_sends(branch, gate_all, gate_send, gate_recv)
     for copy in swaps:
         copy.start()
     gains = [
-        remote(gain_ref, gain_got.at[share], gain_send.at[k], gain_recv.at[k], device)
+        remote(gain_got.at[share], gain_got.at[share], gain_send.at[k], gain_recv.at[k], device)
         for k, device in enumerate(share_others(me, shares))
     ]
     for copy in gains:
@@ -363,13 +365,11 @@
     for copy in locals_:
         copy.start()
     ids_copies = [
-        remote(ids_ref, ids_all.at[seq], ids_send.at[k], ids_recv.at[k], device)
+        remote(ids_all.at[seq], ids_all.at[seq], ids_send.at[k], ids_recv.at[k], device)
         for k, device in enumerate(plane_others(me))
     ]
     for copy in ids_copies:
         copy.start()
-    ids_all[seq] = ids_ref[...]
-    gain_got[share] = gain_ref[...]
     rows_all[z] = rows_ref[...]
     mine_rows = pl.ds(pl.multiple_of(x * half, half), half)
     at_rows = pl.ds(pl.multiple_of(z * half, half), half)
@@ -637,7 +637,7 @@
             shape(per_token, F32),
             shape(per_token, F32),
             shape((rows.shape[0], chans), F32),
-            shape((gain.shape[0], width), F32),
+            shape((8, width), F32),
             shape((4, 2) + block, BF16),
         ],
         scratch_shapes=[
@@ -645,8 +645,8 @@
             pltpu.VMEM((width, chans), BF16),
             pltpu.VMEM((chans, wide + rank), BF16),
             pltpu.VMEM((z_size,) + rows.shape, BF16),
-            pltpu.VMEM((shares,) + gain.shape, F32),
-            pltpu.VMEM((8,) + ids.shape, ids.dtype),
+            pltpu.VMEM((shares, 8, gain.shape[1]), F32),
+            pltpu.VMEM((8, 8, length), ids.dtype),
             pltpu.VMEM((8, length, chans), F32),
             pltpu.VMEM((length + 3, 8, chans), F32),
             pltpu.VMEM(per_token, F32),
@@ -695,6 +695,13 @@
     lax.fori_loop(0, count, body, 0)
 
 
+def fill_rates(rate_ref, params_ref, first):
+    states = rate_ref.shape[0]
+    rows = -LOG2E * jnp.exp(params_ref[first : first + states, :])
+    for n in range(states):
+        rate_ref[n] = jnp.broadcast_to(rows[n : n + 1, :], rate_ref.shape[1:])
+
+
 def forward_kernel(
     z_size,
     chunks,
@@ -705,7 +712,6 @@
     x_ref,
     sel_ref,
     keep_ref,
-    rate_ref,
     normed_ref,
     cot_ref,
     normed_col,
@@ -722,6 +728,7 @@
     ggate_ref,
     gate_all,
     out_all,
+    rate_ref,
     h_ref,
     bc_ref,
     y_ref,
@@ -759,6 +766,7 @@
     def _():
         greet([{"z": (z + 1) % z_size}, {"z": (z + z_size - 1) % z_size}])
         line_start(hops - 1)
+        fill_rates(rate_ref, params_ref, skip_row + 1)
         h_ref[...] = jnp.zeros_like(h_ref)
 
     steps, seqs, width = dt_ref.shape
@@ -853,10 +861,11 @@
         ggate_ref[...] = dot_tn(normed_col[...].reshape(cols), bgi_all[...].reshape(tall)).astype(BF16)
 
 
-def scan_forward(z_size, rank, skip_row, dt, x, selection, keep, rate, normed, cot, gate_w, out_w, params):
+def scan_forward(
+    z_size, rank, states, skip_row, dt, x, selection, keep, normed, cot, gate_w, out_w, params
+):
     length, seqs, width = dt.shape
     model = normed.shape[2]
-    states = rate.shape[0]
     wide = selection.shape[1]
     chunks = length // STEPS
     early = lambda i: jnp.minimum(i, chunks - 1)
@@ -880,7 +889,6 @@
             block(seqs, width),
             pl.BlockSpec((rows, wide), lambda i: (early(i), 0)),
             block(seqs, 128),
-            whole(states, seqs, width),
             across(model),
             across(model),
             column,
@@ -911,8 +919,9 @@
             shape(gate_w.shape, BF16),
             shape(out_w.shape, BF16),
         ],
-        input_output_aliases={10: 7, 11: 8},
+        input_output_aliases={9: 7, 10: 8},
         scratch_shapes=[
+            pltpu.VMEM((states, seqs, width), F32),
             pltpu.VMEM((states, seqs, width), F32),
             pltpu.VMEM((STEPS, seqs, wide - rank), F32),
             pltpu.VMEM((length, seqs, width), F32),
@@ -931,7 +940,7 @@
         compiler_params=pltpu.CompilerParams(
             collective_id=5, has_side_effects=True, vmem_limit_bytes=60 << 20
         ),
-    )(dt, x, selection, keep, rate, normed, cot, normed, cot, params, gate_w, out_w)
+    )(dt, x, selection, keep, normed, cot, normed, cot, params, gate_w, out_w)
 
 
 def z_sums(z, z_size, owns, ups, downs, sems, blocks):
@@ -1017,7 +1026,6 @@
     pre_ref,
     sel_ref,
     keep_ref,
-    rate_ref,
     hist_ref,
     last_ref,
     ones_ref,
@@ -1033,6 +1041,7 @@
     skip_ref,
     gate_fin,
     out_fin,
+    rate_ref,
     ag_ref,
     h_ref,
     p_ref,
@@ -1075,6 +1084,7 @@
         ]
         for copy in loads:
             copy.start()
+        fill_rates(rate_ref, params_ref, skip_row + 1)
         ag_ref[...] = jnp.zeros_like(ag_ref)
         da_ref[...] = jnp.zeros_like(da_ref)
         gstep_ref[...] = jnp.zeros_like(gstep_ref)
@@ -1187,10 +1197,10 @@
 
 
 def scan_backward(
-    z_size, rank, skip_row, dt, x, ds, pre, selection, keep, rate, hist, last, params, step_w, gate, out
+    z_size, rank, skip_row, dt, x, ds, pre, selection, keep, hist, last, params, step_w, gate, out
 ):
     length, seqs, width = dt.shape
-    states = rate.shape[0]
+    states = last.shape[0]
     chunks = length // STEPS
     wide = selection.shape[1]
     rows = STEPS * seqs
@@ -1215,7 +1225,6 @@
             block(seqs, width),
             flat(wide),
             block(seqs, 128),
-            whole(states, seqs, width),
             pl.BlockSpec((STEPS // 2, states, 2 * seqs, width), lambda i: (chunks - 1 - i, 0, 0, 0)),
             whole(states, seqs, width),
             whole(span, 128),
@@ -1247,6 +1256,7 @@
         scratch_shapes=[
             pltpu.VMEM((states, seqs, width), F32),
             pltpu.VMEM((states, seqs, width), F32),
+            pltpu.VMEM((states, seqs, width), F32),
             pltpu.VMEM((2, width // 128 // TOGETHER, rows, span), BF16),
             pltpu.VMEM((STEPS, seqs, wide - rank), F32),
             pltpu.VMEM((rows, width), BF16),
@@ -1266,7 +1276,7 @@
         compiler_params=pltpu.CompilerParams(
             collective_id=4, has_side_effects=True, vmem_limit_bytes=62 << 20
         ),
-    )(dt, x, ds, pre, selection, keep, rate, hist, last, ones, params, step_w, gate, out)
+    )(dt, x, ds, pre, selection, keep, hist, last, ones, params, step_w, gate, out)
 
 
 def last_kernel(
@@ -1293,7 +1303,8 @@
     bgi_hbm,
     gout_hbm,
     tgrad_ref,
-    in_ref,
+    both_gate,
+    both_conv,
     out_ref,
     small_out,
     vec_out,
@@ -1330,8 +1341,6 @@
     up_out,
     down_out,
     fin_conv,
-    both_gate,
-    both_conv,
     gain_parts,
     gain_got,
     gain_half,
@@ -1374,7 +1383,7 @@
     over_x = {"x": 1 - x}
     length, width = tokens_ref.shape
     chans = bx.shape[2]
-    rows_in = in_ref.shape[0]
+    rows_in = both_gate.shape[2]
     half = own_out.shape[1]
     hops = z_size - 1
     wide = part_ref.shape[3]
@@ -1398,6 +1407,42 @@
     later = pl.ds(own_out.shape[2], own_out.shape[2])
     out_load = pltpu.make_async_copy(gout_hbm.at[:, :, later], own_out, local_sem.at[6])
     out_load.start()
+
+    fine = 4
+    block = length // 8
+
+    def taps_of(lanes):
+        return [
+            jnp.broadcast_to(params_ref[taps - 1 - j : taps - j, lanes], (8, 128)) for j in range(taps)
+        ]
+
+    def activate(b, carry):
+        t0 = b * block
+
+        def convolve(i, carry):
+            for g in range(chans // 128):
+                lanes = pl.ds(g * 128, 128)
+                tap = taps_of(lanes)
+                offset = jnp.broadcast_to(params_ref[taps : taps + 1, lanes], (8, 128))
+                taken = []
+                slopes = []
+                for j in range(fine):
+                    t = t0 + i * fine + j
+                    total = tap[3] * cin[t, :, lanes] * keep_ref[jnp.maximum(t - 2, 0)]
+                    total = (total + tap[2] * cin[t + 1, :, lanes]) * keep_ref[jnp.maximum(t - 1, 0)]
+                    total = (total + tap[1] * cin[t + 2, :, lanes]) * keep_ref[t]
+                    v = total + tap[0] * cin[t + 3, :, lanes] + offset
+                    s = sigmoid(v)
+                    silu = v * s
+                    taken.append(silu)
+                    slopes.append(s + silu * (1.0 - s))
+                rows = pl.ds(pl.multiple_of(i * fine * 8, fine * 8), fine * 8)
+                picked[b, rows, lanes] = jnp.concatenate(taken, axis=0).astype(BF16)
+                bci[b, rows, lanes] = jnp.concatenate(slopes, axis=0).astype(BF16)
+            return carry
+
+        lax.fori_loop(0, block // fine, convolve, 0)
+        return carry
 
     swap = remote(part_ref.at[:, 1 - c], from_sib, sw_s.at[0], sw_r.at[0], sibling)
     swap.start()
@@ -1420,6 +1465,8 @@
         copy = remote(stage.at[k], got.at[k], rs_s.at[k], rs_r.at[k], {"x": ox, "y": oy})
         copy.start()
         sends.append(copy)
+    loads[0].wait()
+    lax.fori_loop(0, 8, activate, 0)
     total = part_ref[mine, c].astype(F32) + from_sib[mine].astype(F32)
     if hops > 1:
         out_line(1, 0)
@@ -1464,7 +1511,7 @@
         there = chosen.at[ox * 2 + oy, c]
         forwards.append(remote(there, there, fw_s.at[k], fw_r.at[k], sibling))
         forwards[-1].start()
-    for copy in loads:
+    for copy in loads[1:]:
         copy.wait()
     for _, copy in spreads:
         copy.wait_send()
@@ -1475,53 +1522,34 @@
     for tau in range(2, hops):
         out_line(tau, 0)
 
-    fine = 4
-    block = length // 8
-
-    def taps_of(lanes):
-        return [
-            jnp.broadcast_to(params_ref[taps - 1 - j : taps - j, lanes], (8, 128)) for j in range(taps)
-        ]
-
     def select(b, carry):
         back = chosen[b // 2, b % 2]
         t0 = b * block
         bx[pl.ds(t0, block)] += dot_nt(back, mats_ref[:, :wide]).reshape(block, 8, chans)
+
         def convolve(i, carry):
             for g in range(chans // 128):
                 lanes = pl.ds(g * 128, 128)
-                tap = taps_of(lanes)
-                offset = jnp.broadcast_to(params_ref[taps : taps + 1, lanes], (8, 128))
                 acc = [sums[r, :, lanes] for r in range(taps + 1)]
-                taken = []
+                slopes = bci[b, pl.ds(pl.multiple_of(i * fine * 8, fine * 8), fine * 8), lanes].astype(F32)
                 for j in range(fine):
                     t = t0 + i * fine + j
                     k0 = keep_ref[t]
                     k1 = k0 * keep_ref[jnp.maximum(t - 1, 0)]
                     k2 = k1 * keep_ref[jnp.maximum(t - 2, 0)]
-                    v0 = cin[t + 3, :, lanes]
-                    v1 = cin[t + 2, :, lanes] * k0
-                    v2 = cin[t + 1, :, lanes] * k1
-                    v3 = cin[t, :, lanes] * k2
-                    v = offset + tap[0] * v0 + tap[1] * v1 + tap[2] * v2 + tap[3] * v3
-                    s = sigmoid(v)
-                    silu = v * s
-                    taken.append(silu)
-                    back = bx[t, :, lanes] * (s + silu * (1.0 - s))
+                    back = bx[t, :, lanes] * slopes[j * 8 : (j + 1) * 8]
                     bx[t, :, lanes] = back
-                    acc[0] = acc[0] + back * v0
-                    acc[1] = acc[1] + back * v1
-                    acc[2] = acc[2] + back * v2
-                    acc[3] = acc[3] + back * v3
+                    acc[0] = acc[0] + back * cin[t + 3, :, lanes]
+                    acc[1] = acc[1] + back * (cin[t + 2, :, lanes] * k0)
+                    acc[2] = acc[2] + back * (cin[t + 1, :, lanes] * k1)
+                    acc[3] = acc[3] + back * (cin[t, :, lanes] * k2)
                     acc[4] = acc[4] + back
                 for r in range(taps + 1):
                     sums[r, :, lanes] = acc[r]
-                rows = pl.ds(pl.multiple_of(i * fine * 8, fine * 8), fine * 8)
-                picked[rows, lanes] = jnp.concatenate(taken, axis=0).astype(BF16)
             return carry
 
         lax.fori_loop(0, block // fine, convolve, 0)
-        gsel[...] += dot_tn(picked[...], back)
+        gsel[...] += dot_tn(picked[b], back)
         return carry
 
     lax.fori_loop(0, 8, select, 0)
@@ -1716,15 +1744,6 @@
     small_x.start()
     vec_x.start()
 
-    branch = 8 * half * z_size
-
-    def lay(first, both):
-        for zz in range(z_size):
-            for j in range(4):
-                for xx in range(2):
-                    col = first + (zz * 4 + j) * 2 * half + xx * half
-                    in_ref[:, col : col + half] = both[xx, j, :, zz * half : (zz + 1) * half].astype(F32)
-
     for copy in gains:
         copy.wait()
     gain_half[...] = jnp.sum(gain_got[...], axis=0)
@@ -1732,12 +1751,10 @@
     gain_x.start()
     for copy in gate_swaps:
         copy.wait()
-    lay(branch, both_gate)
     gain_x.wait()
     gain_out[...] = gain_half[...] + gain_pair[...]
     for copy in conv_swaps:
         copy.wait()
-    lay(0, both_conv)
     for copy in (out_x, small_x, vec_x):
         copy.wait()
     for j in range(3):
@@ -1773,7 +1790,6 @@
     conv,
     gate,
     bgi,
-    in_width,
 ):
     length, width = tokens.shape
     chans = bx.shape[2]
@@ -1789,17 +1805,18 @@
     block = (length, width)
     slabs = [(half, mats.shape[1]), (params.shape[0], half), (4 * rows_in, chans)]
     bufs = lambda n: [pltpu.VMEM((n,) + s, BF16) for s in slabs]
-    both = pltpu.VMEM((2, 4, rows_in, chans), BF16)
+    both = shape((2, 4, rows_in, chans), BF16)
     piece = (8, width // shares)
     few = (length, wide)
     late_out = (half, width // 2)
     return pl.pallas_call(
         functools.partial(last_kernel, z_size, taps),
         in_specs=[vmem] * 13 + [any_space] * 7,
-        out_specs=[vmem] * 6,
+        out_specs=[vmem] * 7,
         out_shape=[
             shape(tokens.shape, BF16),
-            shape((rows_in, in_width), F32),
+            both,
+            both,
             shape((2,) + gout.shape[1:], BF16),
             shape((2,) + slabs[0], BF16),
             shape((2,) + slabs[1], BF16),
@@ -1812,7 +1829,7 @@
             pltpu.VMEM((3,) + few, BF16),
             pltpu.VMEM((length + 3, 8, chans), F32),
             pltpu.VMEM((length + 3, 8, chans), F32),
-            pltpu.VMEM((length, chans), BF16),
+            pltpu.VMEM((8, length, chans), BF16),
             pltpu.VMEM(conv.shape, BF16),
             pltpu.VMEM(gate.shape, BF16),
             pltpu.VMEM(bgi.shape, BF16),
@@ -1834,8 +1851,6 @@
             pltpu.VMEM((hops,) + late_out, BF16),
             pltpu.VMEM((hops,) + late_out, BF16),
             pltpu.VMEM(slabs[2], BF16),
-            both,
-            both,
             pltpu.VMEM((shares,) + piece, F32),
             pltpu.VMEM((shares,) + piece, F32),
             pltpu.VMEM(piece, F32),
@@ -1882,6 +1897,76 @@
     )
 
 
+def close_kernel(
+    taps,
+    wide,
+    tokens_ref,
+    sum_ref,
+    mats_ref,
+    vec_ref,
+    weight_ref,
+    gate_ref,
+    conv_ref,
+    layer_ref,
+    in_ref,
+    taps_ref,
+    offset_ref,
+    select_ref,
+    step_ref,
+    bias_ref,
+    decay_ref,
+    skip_ref,
+    out_ref,
+):
+    layer_ref[...] = (tokens_ref[...].astype(F32) + sum_ref[...].astype(F32)).astype(BF16)
+    half = mats_ref.shape[1]
+    for xx in range(2):
+        rows = pl.ds(xx * half, half)
+        select_ref[rows, :] = mats_ref[xx, :, : select_ref.shape[1]].astype(F32)
+        step_ref[rows, :] = mats_ref[xx, :, wide:].astype(F32)
+        out_ref[rows, :] = weight_ref[xx].astype(F32)
+    z_size = conv_ref.shape[3] // half
+    for first, both in ((0, conv_ref), (in_ref.shape[1] // 2, gate_ref)):
+        for zz in range(z_size):
+            for j in range(4):
+                for xx in range(2):
+                    col = first + (zz * 4 + j) * 2 * half + xx * half
+                    in_ref[:, col : col + half] = both[xx, j, :, zz * half : (zz + 1) * half].astype(F32)
+    vectors = jnp.concatenate([vec_ref[0].astype(F32), vec_ref[1].astype(F32)], axis=1)
+    offset_ref[...] = vectors[taps : taps + 1, :]
+    bias_ref[...] = vectors[taps + 1 : taps + 2, :]
+    skip_ref[...] = vectors[taps + 2 : taps + 3, :]
+    tall = vectors.T
+    taps_ref[...] = tall[:, :taps]
+    decay_ref[...] = tall[:, taps + 3 : taps + 3 + decay_ref.shape[1]]
+
+
+def close(taps, states, select_width, tokens, layer_sum, mats, vectors, weight, gate, conv):
+    rows = 2 * mats.shape[1]
+    wide = select_width + -select_width % 128
+    rank = mats.shape[2] - wide
+    vmem = pl.BlockSpec(memory_space=pltpu.VMEM)
+    shape = jax.ShapeDtypeStruct
+    return pl.pallas_call(
+        functools.partial(close_kernel, taps, wide),
+        in_specs=[vmem] * 7,
+        out_specs=[vmem] * 10,
+        out_shape=[
+            shape(tokens.shape, BF16),
+            shape((gate.shape[2], 16 * gate.shape[3]), F32),
+            shape((rows, taps), F32),
+            shape((1, rows), F32),
+            shape((rows, select_width), F32),
+            shape((rows, rank), F32),
+            shape((1, rows), F32),
+            shape((rows, states), F32),
+            shape((1, rows), F32),
+            shape((rows, weight.shape[2]), F32),
+        ],
+        compiler_params=pltpu.CompilerParams(vmem_limit_bytes=60 << 20),
+    )(tokens, layer_sum, mats, vectors, weight, gate, conv)
+
+
 def shards(
     tokens,
     doc_ids,
@@ -1933,8 +2018,6 @@
             in_weight.reshape(in_rows, 2, z_size, 4, 2, half), x_at, 4, keepdims=False
         )
         weight_in = columns.transpose(1, 3, 0, 2, 4).reshape(2, 4, in_rows, chans)
-    gain_tile = jnp.broadcast_to(norm_gain.astype(F32)[None, :], (8, norm_gain.shape[0]))
-    ids_tile = jnp.broadcast_to(doc_ids, (8, length))
     (
         all_normed,
         all_cot,
@@ -1955,8 +2038,8 @@
         taps,
         rank,
         tokens,
-        gain_tile,
-        ids_tile,
+        norm_gain.reshape(1, -1),
+        doc_ids,
         vectors,
         cotangent,
         weight_in,
@@ -1965,16 +2048,13 @@
         step_weight,
     )
     selection = selection.reshape(length * seqs, wide)
-    rates = -jnp.exp(vectors[taps + 3 : taps + 3 + states])
-    rate2 = jnp.broadcast_to((rates * LOG2E)[:, None, :], (states, seqs, chans))
 
     hist, last, back_scan, back_gate_in, out_part, grad_out, grad_gate, w_gate, _ = scan_forward(
-        z_size, rank, taps + 2, dt, x, selection, keep, rate2, all_normed, all_cot, w_gate, w_out, vectors
+        z_size, rank, states, taps + 2, dt, x, selection, keep, all_normed, all_cot, w_gate, w_out, vectors
     )
     layer_sum = lax.psum_scatter(
         out_part.reshape(-1, width), PLANE, scatter_dimension=0, tiled=True
     )
-    layer_out = (tokens.astype(F32) + layer_sum.astype(F32)).astype(BF16)
     back_x, part, da, g_step, g_bias, g_skip, gate_fin, out_fin = scan_backward(
         z_size,
         rank,
@@ -1985,7 +2065,6 @@
         pre,
         selection,
         keep,
-        rate2,
         hist,
         last,
         vectors,
@@ -1993,7 +2072,7 @@
         grad_gate.reshape(z_size, -1, chans),
         grad_out.reshape(z_size, half, width),
     )
-    tokens_grad, g_in, g_out, g_mats, g_vectors, g_gain = last_part(
+    tokens_grad, g_in_gate, g_in_conv, g_out, g_mats, g_vectors, g_gain = last_part(
         z_size,
         taps,
         part.reshape(4, 2, length, wide),
@@ -2016,28 +2095,29 @@
         w_conv,
         w_gate,
         back_gate_in,
-        in_weight.shape[1],
     )
-    g_gain = g_gain[0]
-    g_out = g_out.reshape(rows, width).astype(F32)
-    g_mats = g_mats.reshape(rows, -1).astype(F32)
-    g_vectors = g_vectors.transpose(0, 2, 1).reshape(rows, -1).astype(F32)
     if rh_size > 1:
-        g_mats, g_vectors, g_in, g_out, g_gain = lax.psum(
-            (g_mats, g_vectors, g_in, g_out, g_gain), "rh"
+        g_mats, g_vectors, g_in_gate, g_in_conv, g_out, g_gain = lax.psum(
+            tuple(
+                v.astype(F32) for v in (g_mats, g_vectors, g_in_gate, g_in_conv, g_out, g_gain)
+            ),
+            "rh",
         )
+    layer_out, g_in, g_taps, g_offset, g_select, g_step, g_bias, g_decay, g_skip, g_out = close(
+        taps, states, rank + 2 * states, tokens, layer_sum, g_mats, g_vectors, g_out, g_in_gate, g_in_conv
+    )
     return (
         layer_out,
         tokens_grad,
-        g_gain,
+        g_gain[0],
         g_in,
-        g_vectors[:, :taps],
-        g_vectors[:, taps],
-        g_mats[:, : rank + 2 * states],
-        g_mats[:, wide:],
-        g_vectors[:, taps + 1],
-        g_vectors[:, taps + 3 : taps + 3 + states],
-        g_vectors[:, taps + 2],
+        g_taps,
+        g_offset[0],
+        g_select,
+        g_step,
+        g_bias[0],
+        g_decay,
+        g_skip[0],
         g_out,
     )
 

time: 418 us -> 406 us (0.971)
  other arithmetic: 6.94 us -> 0 us
    pallas_call x0 -> x1, Pallas kernels: none -> 6.29 us  [close(): pl.pallas_call(functools.partial(close_kernel, taps, wide), in_specs=[vme...]
    convert_element_type x4 -> x0, other arithmetic: 6.13 us -> none  [the longest x1 2.74 us: shards(): layer_out = (tokens.astype(F32) + layer_sum.astype(F32)).astype(BF16)]
  transfers between devices with their start and end apart: 1 -> 1, of which waited for: 0 -> 0; matrix products, arithmetic and copies ran while one was open for 2% -> 0% of each run, Pallas kernels for 43% -> 43%
where the time goes in v5:
time: 406 us; the launch traced here: 405 us
  Pallas kernels  379 us (93%)
  between operations  14.1 us (3%)
  local copies, waits for them, and re-layouts  11.7 us (3%)
    pallas_call x1, Pallas kernels, front(): pl.pallas_call(functools.partial(front_kernel, z_size, taps, rank), in_sp...  120 us
    pallas_call x1, Pallas kernels, last_part(): pl.pallas_call(functools.partial(last_kernel, z_size, taps), in_specs=[vm...  108 us
    pallas_call x1, Pallas kernels, scan_forward(): pl.pallas_call(functools.partial(forward_kernel, z_size, chunks, states,...  79 us
    pallas_call x1, Pallas kernels, scan_backward(): pl.pallas_call(functools.partial(backward_kernel, chunks, z_size, states,...  66.2 us
  transfers between devices with their start and end apart: 1, of which 0 were waited for; matrix products, arithmetic and copies ran while one was open for 0% of the time, Pallas kernels for 43%

profile of v5, /device:TPU:11, one launch (start us, length us, event | category | flops | bytes accessed | tf_op | source)
XLA Modules:
  0.0 405.0 jit_solution(15333365442336230178)
XLA Ops:
  7.2 0.0 copy-start
  7.2 0.0 reduce-scatter.2.cloned.1.call-start
  7.2 0.7 dynamic-slice_bitcast_fusion.2
  8.0 0.7 constant_dynamic-slice_fusion.1
  8.7 0.0 copy-done
  8.7 1.6 copy.28.select_ref
  10.3 0.7 dynamic-slice_bitcast_fusion
  11.1 0.2 concatenate.3
  11.2 0.6 pad.4.rows_ref
  11.8 119.9 %shard_map.229 = (bf16[8,256,2048]{2,1,0:T(8,128)(2,1)}, bf16[8,256,2048]{2,1,0:T(8,128)(2,1)}, bf16[2048,512]{1,0:T(8,128)(2,1)}, bf16[2048,512]{1,0:T(8,128)(2...) custom-call(bf16[256,2048]{1,0:T(8,128)(2,1)} %tokens_ref.5, ...), custom_call_target="tpu_custom_call" | custom-call | flops 120000004096 | bytes 120000000 | tf_op jit(solution)/shard_map/pallas_call | solution.py:623
  131.7 79.0 %shard_map.230 = (bf16[128,16,16,512]{3,2,1,0:T(8,128)(2,1)}, f32[16,8,512]{2,1,0:T(8,128)}, f32[256,8,512]{2,1,0:T(8,128)}, bf16[8,256,512]{2,1,0:T(8,128)(2,1)...) custom-call(f32[256,8,512]{2,1,0:T(8,128)} %get-tuple-element.59.dt_, ...), custom_call_target="tpu_custom_call", output_to_operand_aliasing={{7}: (9, {}), {8}: (10, {})} | custom-call | flops 60000002048 | bytes 60000000 | tf_op jit(solution)/shard_map/pallas_call | solution.py:884
  210.7 0.0 reduce-scatter.2.cloned.1.call-update
  210.8 66.2 %shard_map.231 = (f32[256,8,512]{2,1,0:T(8,128)}, bf16[2048,256]{1,0:T(8,128)(2,1)}, f32[16,8,512]{2,1,0:T(8,128)}, f32[512,128]{1,0:T(8,128)}, f32[8,512]{1,0:T...) custom-call(f32[256,8,512]{2,1,0:T(8,128)} %get-tuple-element.59.dt_ref, ...), custom_call_target="tpu_custom_call" | custom-call | flops 80000000000 | bytes 80000000 | tf_op jit(solution)/shard_map/pallas_call | solution.py:1218
  276.9 0.0 copy-start.1
  276.9 107.8 %shard_map.232 = (bf16[256,2048]{1,0:T(8,128)(2,1)}, bf16[2,4,128,512]{3,2,1,0:T(8,128)(2,1)}, bf16[2,4,128,512]{3,2,1,0:T(8,128)(2,1)}, bf16[2,128,2048]{2,1,0:...) custom-call(bf16[4,2,256,256]{3,2,1,0:T(8,128)(2,1)} %bitcast.29, ...), custom_call_target="tpu_custom_call" | custom-call | flops 120000004096 | bytes 120000000 | tf_op jit(solution)/shard_map/pallas_call | solution.py:1812
  384.7 0.0 copy-start.2
  384.7 1.3 slice_bitcast_fusion
  386.0 6.3 %shard_map.233 = (bf16[256,2048]{1,0:T(8,128)(2,1)}, f32[128,8192]{1,0:T(8,128)}, f32[256,4]{1,0:T(8,128)}, f32[1,256]{1,0:T(1,128)}, f32[256,160]{1,0:T(8,128)}...) custom-call(bf16[256,2048]{1,0:T(8,128)(2,1)} %tokens_ref.5, ...), custom_call_target="tpu_custom_call" | custom-call | tf_op jit(solution)/shard_map/pallas_call | solution.py:1950
  392.3 1.6 copy.29
  393.9 1.6 copy.31
  395.4 1.7 copy.30
  397.2 0.0 copy-done.2
  397.2 1.0 copy.35
  398.1 0.0 copy-done.1
  (2 shorter events, 0.0 us)
Async XLA Ops:
  7.2 1.5 copy-start
  7.2 378.8 %reduce-scatter.2.cloned.1.call-start = ((), (), s32[]{:S(2)}) async-start(), calls=%async_computation.1 | async-start | bytes 9437184 | tf_op jit(solution)/shard_map/reduce_scatter | solution.py:2055
  276.9 121.2 %copy-start.1 = (bf16[256,16]{0,1:T(8,128)(2,1)S(1)}, bf16[256,16]{0,1:T(8,128)(2,1)}, u32[]{:S(2)}) copy-start(bf16[256,16]{0,1:T(8,128)(2,1)} %param.23) | copy-start | bytes 24580
  384.7 12.5 %copy-start.2 = (bf16[256,2048]{1,0:T(8,128)(2,1)S(1)}, bf16[256,2048]{1,0:T(8,128)(2,1)}, u32[]{:S(2)}) copy-start(bf16[256,2048]{1,0:T(8,128)(2,1)} %get-tuple-element.133) | copy-start | bytes 3145732
Sparse Core Ops, SparseCore 0:
  210.9 70.9 reduce-scatter.1

commit v6 on v5

--- a/solution.py
+++ b/solution.py
@@ -358,11 +358,13 @@
         ),
         pltpu.make_async_copy(cot_ref, cot_all.at[seq], local_sem.at[4]),
     ]
-    for i, (src, there) in enumerate(pieces(0, conv_w, corner)):
-        locals_.append(pltpu.make_async_copy(src, there, own_sem.at[0, i]))
+    conv_own = [
+        pltpu.make_async_copy(src, there, own_sem.at[0, i])
+        for i, (src, there) in enumerate(pieces(0, conv_w, corner))
+    ]
     for i, (src, there) in enumerate(pieces(branch, gate_all, corner)):
         locals_.append(pltpu.make_async_copy(src, there, own_sem.at[1, i]))
-    for copy in locals_:
+    for copy in conv_own + locals_:
         copy.start()
     ids_copies = [
         remote(ids_all.at[seq], ids_all.at[seq], ids_send.at[k], ids_recv.at[k], device)
@@ -400,7 +402,7 @@
     ring.start(0)
     for copy in swaps:
         copy.wait()
-    for copy in locals_:
+    for copy in conv_own:
         copy.wait()
     a_start, a_arrive, a_sent = z_line(
         z,
@@ -440,16 +442,15 @@
             a_arrive(k)
             if k + 1 < hops:
                 a_start(k + 1)
-            if k + 1 == hops - 1:
-                m_start(0)
+            if k:
+                m_arrive(k - 1)
+            m_start(k)
         if k < RING - 1:
             ring.arrive(k)
             ring.start(k + 1)
         if k == RING - 2:
             cot_ring.start(0)
-    m_arrive(0)
-    m_start(1)
-    for copy in gates:
+    for copy in gates + locals_:
         copy.wait()
     b_start(0)
     for k in range(RING):
@@ -468,10 +469,7 @@
         return carry
 
     lax.fori_loop(0, 8, project, 0)
-    for k in range(1, hops):
-        m_arrive(k)
-        if k + 1 < hops:
-            m_start(k + 1)
+    m_arrive(hops - 1)
     cot_ring.arrive(0)
     cot_ring.start(1)
 

time: 406 us -> 394 us (0.970)
  Pallas kernels: 379 us -> 365 us
    pallas_call x1, Pallas kernels: 79 us -> 65.3 us  [scan_forward(): pl.pallas_call(functools.partial(forward_kernel, z_size, chunks, states,...]
  transfers between devices with their start and end apart: 1 -> 1, of which waited for: 0 -> 0; matrix products, arithmetic and copies ran while one was open for 0% -> 0% of each run, Pallas kernels for 43% -> 44%
where the time goes in v6:
time: 394 us; the launch traced here: 391 us
  Pallas kernels  365 us (93%)
  between operations  14.1 us (4%)
  local copies, waits for them, and re-layouts  11.7 us (3%)
    pallas_call x1, Pallas kernels, front(): pl.pallas_call(functools.partial(front_kernel, z_size, taps, rank), in_sp...  120 us
    pallas_call x1, Pallas kernels, last_part(): pl.pallas_call(functools.partial(last_kernel, z_size, taps), in_specs=[vm...  106 us
    pallas_call x1, Pallas kernels, scan_backward(): pl.pallas_call(functools.partial(backward_kernel, chunks, z_size, states,...  67.7 us
    pallas_call x1, Pallas kernels, scan_forward(): pl.pallas_call(functools.partial(forward_kernel, z_size, chunks, states,...  65.3 us
  transfers between devices with their start and end apart: 1, of which 0 were waited for; matrix products, arithmetic and copies ran while one was open for 0% of the time, Pallas kernels for 44%

profile of v6, /device:TPU:11, one launch (start us, length us, event | category | flops | bytes accessed | tf_op | source)
XLA Modules:
  0.0 391.3 jit_solution(18007829222334060809)
XLA Ops:
  7.2 0.0 copy-start
  7.2 0.0 reduce-scatter.2.cloned.1.call-start
  7.2 0.7 dynamic-slice_bitcast_fusion.2
  8.0 0.7 constant_dynamic-slice_fusion.1
  8.7 0.0 copy-done
  8.7 1.6 copy.28.select_ref
  10.3 0.7 dynamic-slice_bitcast_fusion
  11.1 0.2 concatenate.3
  11.2 0.6 pad.4.rows_ref
  11.8 120.2 %shard_map.229 = (bf16[8,256,2048]{2,1,0:T(8,128)(2,1)}, bf16[8,256,2048]{2,1,0:T(8,128)(2,1)}, bf16[2048,512]{1,0:T(8,128)(2,1)}, bf16[2048,512]{1,0:T(8,128)(2...) custom-call(bf16[256,2048]{1,0:T(8,128)(2,1)} %tokens_ref.5, ...), custom_call_target="tpu_custom_call" | custom-call | flops 120000004096 | bytes 120000000 | tf_op jit(solution)/shard_map/pallas_call | solution.py:621
  132.0 65.3 %shard_map.230 = (bf16[128,16,16,512]{3,2,1,0:T(8,128)(2,1)}, f32[16,8,512]{2,1,0:T(8,128)}, f32[256,8,512]{2,1,0:T(8,128)}, bf16[8,256,512]{2,1,0:T(8,128)(2,1)...) custom-call(f32[256,8,512]{2,1,0:T(8,128)} %get-tuple-element.59.dt_, ...), custom_call_target="tpu_custom_call", output_to_operand_aliasing={{7}: (9, {}), {8}: (10, {})} | custom-call | flops 60000002048 | bytes 60000000 | tf_op jit(solution)/shard_map/pallas_call | solution.py:882
  197.3 0.0 reduce-scatter.2.cloned.1.call-update
  197.3 67.7 %shard_map.231 = (f32[256,8,512]{2,1,0:T(8,128)}, bf16[2048,256]{1,0:T(8,128)(2,1)}, f32[16,8,512]{2,1,0:T(8,128)}, f32[512,128]{1,0:T(8,128)}, f32[8,512]{1,0:T...) custom-call(f32[256,8,512]{2,1,0:T(8,128)} %get-tuple-element.59.dt_ref, ...), custom_call_target="tpu_custom_call" | custom-call | flops 80000000000 | bytes 80000000 | tf_op jit(solution)/shard_map/pallas_call | solution.py:1216
  265.0 0.0 copy-start.1
  265.0 106.1 %shard_map.232 = (bf16[256,2048]{1,0:T(8,128)(2,1)}, bf16[2,4,128,512]{3,2,1,0:T(8,128)(2,1)}, bf16[2,4,128,512]{3,2,1,0:T(8,128)(2,1)}, bf16[2,128,2048]{2,1,0:...) custom-call(bf16[4,2,256,256]{3,2,1,0:T(8,128)(2,1)} %bitcast.29, ...), custom_call_target="tpu_custom_call" | custom-call | flops 120000004096 | bytes 120000000 | tf_op jit(solution)/shard_map/pallas_call | solution.py:1810
  371.1 0.0 copy-start.2
  371.1 1.3 slice_bitcast_fusion
  372.4 6.3 %shard_map.233 = (bf16[256,2048]{1,0:T(8,128)(2,1)}, f32[128,8192]{1,0:T(8,128)}, f32[256,4]{1,0:T(8,128)}, f32[1,256]{1,0:T(1,128)}, f32[256,160]{1,0:T(8,128)}...) custom-call(bf16[256,2048]{1,0:T(8,128)(2,1)} %tokens_ref.5, ...), custom_call_target="tpu_custom_call" | custom-call | tf_op jit(solution)/shard_map/pallas_call | solution.py:1948
  378.6 1.6 copy.29
  380.2 1.6 copy.31
  381.8 1.7 copy.30
  383.5 0.0 copy-done.2
  383.5 1.0 copy.35
  384.5 0.0 copy-done.1
  (2 shorter events, 0.0 us)
Async XLA Ops:
  7.2 1.5 copy-start
  7.2 365.2 %reduce-scatter.2.cloned.1.call-start = ((), (), s32[]{:S(2)}) async-start(), calls=%async_computation.1 | async-start | bytes 9437184 | tf_op jit(solution)/shard_map/reduce_scatter | solution.py:2053
  265.0 119.5 %copy-start.1 = (bf16[256,16]{0,1:T(8,128)(2,1)S(1)}, bf16[256,16]{0,1:T(8,128)(2,1)}, u32[]{:S(2)}) copy-start(bf16[256,16]{0,1:T(8,128)(2,1)} %param.23) | copy-start | bytes 24580
  371.1 12.5 %copy-start.2 = (bf16[256,2048]{1,0:T(8,128)(2,1)S(1)}, bf16[256,2048]{1,0:T(8,128)(2,1)}, u32[]{:S(2)}) copy-start(bf16[256,2048]{1,0:T(8,128)(2,1)} %get-tuple-element.133) | copy-start | bytes 3145732
Sparse Core Ops, SparseCore 0:
  197.4 72.2 reduce-scatter.1

commit v7 on v6

--- a/solution.py
+++ b/solution.py
@@ -470,8 +470,6 @@
 
     lax.fori_loop(0, 8, project, 0)
     m_arrive(hops - 1)
-    cot_ring.arrive(0)
-    cot_ring.start(1)
 
     cin[0:3] = jnp.zeros((3, 8, chans), F32)
     block = 32
@@ -483,6 +481,8 @@
         return carry
 
     lax.fori_loop(0, length // block, turn, 0)
+    cot_ring.arrive(0)
+    cot_ring.start(1)
 
     def convolve(i, carry):
         t0 = i * fine

time: 394 us -> 394 us (level)
  no operation moved by 1% of the time
where the time goes in v7:
time: 394 us; the launch traced here: 391 us
  Pallas kernels  365 us (93%)
  between operations  14.1 us (4%)
  local copies, waits for them, and re-layouts  11.7 us (3%)
    pallas_call x1, Pallas kernels, front(): pl.pallas_call(functools.partial(front_kernel, z_size, taps, rank), in_sp...  120 us
    pallas_call x1, Pallas kernels, last_part(): pl.pallas_call(functools.partial(last_kernel, z_size, taps), in_specs=[vm...  106 us
    pallas_call x1, Pallas kernels, scan_backward(): pl.pallas_call(functools.partial(backward_kernel, chunks, z_size, states,...  67.7 us
    pallas_call x1, Pallas kernels, scan_forward(): pl.pallas_call(functools.partial(forward_kernel, z_size, chunks, states,...  65.3 us
  transfers between devices with their start and end apart: 1, of which 0 were waited for; matrix products, arithmetic and copies ran while one was open for 0% of the time, Pallas kernels for 44%

profile of v7, /device:TPU:11, one launch (start us, length us, event | category | flops | bytes accessed | tf_op | source)
XLA Modules:
  0.0 391.4 jit_solution(13190847902912647392)
XLA Ops:
  7.2 0.0 copy-start
  7.2 0.0 reduce-scatter.2.cloned.1.call-start
  7.2 0.7 dynamic-slice_bitcast_fusion.2
  8.0 0.7 constant_dynamic-slice_fusion.1
  8.7 0.0 copy-done
  8.7 1.6 copy.28.select_ref
  10.3 0.7 dynamic-slice_bitcast_fusion
  11.1 0.2 concatenate.3
  11.2 0.6 pad.4.rows_ref
  11.8 120.2 %shard_map.229 = (bf16[8,256,2048]{2,1,0:T(8,128)(2,1)}, bf16[8,256,2048]{2,1,0:T(8,128)(2,1)}, bf16[2048,512]{1,0:T(8,128)(2,1)}, bf16[2048,512]{1,0:T(8,128)(2...) custom-call(bf16[256,2048]{1,0:T(8,128)(2,1)} %tokens_ref.5, ...), custom_call_target="tpu_custom_call" | custom-call | flops 120000004096 | bytes 120000000 | tf_op jit(solution)/shard_map/pallas_call | solution.py:621
  132.0 65.3 %shard_map.230 = (bf16[128,16,16,512]{3,2,1,0:T(8,128)(2,1)}, f32[16,8,512]{2,1,0:T(8,128)}, f32[256,8,512]{2,1,0:T(8,128)}, bf16[8,256,512]{2,1,0:T(8,128)(2,1)...) custom-call(f32[256,8,512]{2,1,0:T(8,128)} %get-tuple-element.59.dt_, ...), custom_call_target="tpu_custom_call", output_to_operand_aliasing={{7}: (9, {}), {8}: (10, {})} | custom-call | flops 60000002048 | bytes 60000000 | tf_op jit(solution)/shard_map/pallas_call | solution.py:882
  197.3 0.0 reduce-scatter.2.cloned.1.call-update
  197.3 67.7 %shard_map.231 = (f32[256,8,512]{2,1,0:T(8,128)}, bf16[2048,256]{1,0:T(8,128)(2,1)}, f32[16,8,512]{2,1,0:T(8,128)}, f32[512,128]{1,0:T(8,128)}, f32[8,512]{1,0:T...) custom-call(f32[256,8,512]{2,1,0:T(8,128)} %get-tuple-element.59.dt_ref, ...), custom_call_target="tpu_custom_call" | custom-call | flops 80000000000 | bytes 80000000 | tf_op jit(solution)/shard_map/pallas_call | solution.py:1216
  265.0 0.0 copy-start.1
  265.0 106.1 %shard_map.232 = (bf16[256,2048]{1,0:T(8,128)(2,1)}, bf16[2,4,128,512]{3,2,1,0:T(8,128)(2,1)}, bf16[2,4,128,512]{3,2,1,0:T(8,128)(2,1)}, bf16[2,128,2048]{2,1,0:...) custom-call(bf16[4,2,256,256]{3,2,1,0:T(8,128)(2,1)} %bitcast.29, ...), custom_call_target="tpu_custom_call" | custom-call | flops 120000004096 | bytes 120000000 | tf_op jit(solution)/shard_map/pallas_call | solution.py:1810
  371.1 0.0 copy-start.2
  371.1 1.3 slice_bitcast_fusion
  372.4 6.3 %shard_map.233 = (bf16[256,2048]{1,0:T(8,128)(2,1)}, f32[128,8192]{1,0:T(8,128)}, f32[256,4]{1,0:T(8,128)}, f32[1,256]{1,0:T(1,128)}, f32[256,160]{1,0:T(8,128)}...) custom-call(bf16[256,2048]{1,0:T(8,128)(2,1)} %tokens_ref.5, ...), custom_call_target="tpu_custom_call" | custom-call | tf_op jit(solution)/shard_map/pallas_call | solution.py:1948
  378.7 1.6 copy.29
  380.3 1.6 copy.31
  381.8 1.7 copy.30
  383.6 0.0 copy-done.2
  383.6 1.0 copy.35
  384.5 0.0 copy-done.1
  (2 shorter events, 0.0 us)
Async XLA Ops:
  7.2 1.5 copy-start
  7.2 365.2 %reduce-scatter.2.cloned.1.call-start = ((), (), s32[]{:S(2)}) async-start(), calls=%async_computation.1 | async-start | bytes 9437184 | tf_op jit(solution)/shard_map/reduce_scatter | solution.py:2053
  265.0 119.6 %copy-start.1 = (bf16[256,16]{0,1:T(8,128)(2,1)S(1)}, bf16[256,16]{0,1:T(8,128)(2,1)}, u32[]{:S(2)}) copy-start(bf16[256,16]{0,1:T(8,128)(2,1)} %param.23) | copy-start | bytes 24580
  371.1 12.5 %copy-start.2 = (bf16[256,2048]{1,0:T(8,128)(2,1)S(1)}, bf16[256,2048]{1,0:T(8,128)(2,1)}, u32[]{:S(2)}) copy-start(bf16[256,2048]{1,0:T(8,128)(2,1)} %get-tuple-element.133) | copy-start | bytes 3145732
Sparse Core Ops, SparseCore 0:
  197.4 72.2 reduce-scatter.1
